TPU v7x, 32 devices: a whole 2x2x4 slice. The times are simulated.
32 devices in a mesh: section: 2 (over core), tensor: 4 (over y, x), dp: 4 (over z).
Axes of the slice: x: 2, y: 2, z: 4, core: 2. Of those that a mesh axis runs over, the one named last changes fastest.
Arguments:
- x_in: bfloat16 [3, 4096, 1152], P(None, ('dp', 'tensor')), may hold values from -6 to 6
- cotangent: bfloat16 [3, 4096, 1152], P(None, ('dp', 'tensor')), may hold values from -6 to 6
- cond: bfloat16 [3, 32, 1152], P(None, 'dp'), may hold values from -6 to 6
- crop_len: int32 [3, 32], P(None, 'dp'), may hold values from 0 to 512, as said below
- head_mask: int32 [3, 32, 16], P(None, 'dp', 'tensor'), may hold values 0 or 1
- skip_mask: int32 [3, 4096], P(None, 'dp'), may hold values 0 or 1
- ada_w: bfloat16 [2, 1152, 6912], P('section', None, 'tensor'), may hold values from -0.1875 to 0.1875
- qkv_w: bfloat16 [2, 3, 1152, 1152], P('section', None, None, 'tensor'), may hold values from -0.1875 to 0.1875
- proj_w: bfloat16 [2, 1152, 1152], P('section', 'tensor'), may hold values from -1.5 to 1.5
- fc1_w: bfloat16 [2, 1152, 4608], P('section', None, 'tensor'), may hold values from -0.1875 to 0.1875
- fc2_w: bfloat16 [2, 4608, 1152], P('section', 'tensor'), may hold values from -0.09375 to 0.09375
Outputs:
- residual: float32 [2, 3, 4096, 1152], P('section', None, ('dp', 'tensor'))
- input_grad: bfloat16 [2, 3, 4096, 1152], P('section', None, ('dp', 'tensor'))
- sublayer_rms: float32 [2, 2, 3, 4096], P('section', None, None, ('dp', 'tensor'))
- ada_grad: float32 [2, 1152, 6912], P('section', 'dp', 'tensor')
- qkv_grad: float32 [2, 3, 1152, 1152], P('section', None, 'dp', 'tensor')
- proj_grad: float32 [2, 1152, 1152], P('section', 'tensor', 'dp')
- fc1_grad: float32 [2, 1152, 4608], P('section', 'dp', 'tensor')
- fc2_grad: float32 [2, 4608, 1152], P('section', 'tensor', 'dp')
Inputs may be any that keep to these rules, and one draw needn't show every extreme that they name: `crop_len`: A row's crops fill its first slots in order from the row's start, later slots hold 0; a crop has 128 to 512 tokens, a row's lengths sum to at most 1024, and every micro-batch has a crop of exactly 512 tokens.
All inputs are finite; a program needn't handle non-finite values. No bound on the sum of `head_mask` or of `skip_mask` on one device may be relied on, other than what follows from the above.
Results may differ from a plain program's by a relative error of at most 0.033.
The roundings to bfloat16 on the way count: a program that leaves them out, or rounds other values in their place, can miss the bound.
Values may be sent and summed in bfloat16 or wider, within the bound.
No kernel may reach another device: no remote copies, remote signals or barrier semaphores. Data moves between devices by JAX's collectives and lax.ppermute only.
A program may use at most 320 MiB of HBM per device.

v0:
```python
import jax
import jax.numpy as jnp
from jax import lax
from jax.sharding import PartitionSpec as P

highest = lax.Precision.HIGHEST
epsilon = 1e-06
block_rows = 512


def passed_along(block, axis, distance):
    devices = range(lax.axis_size(axis))
    route = [(i - distance, i) for i in devices if i - distance in devices]
    return lax.ppermute(block, axis, route)


def normalize_keep(value):
    centered = value - jnp.mean(value, axis=-1, keepdims=True)
    factor = lax.rsqrt(jnp.mean(centered * centered, axis=-1, keepdims=True) + epsilon)
    return (centered * factor, factor)


def normalize_back(normed, factor, upstream):
    return factor * (
        upstream
        - jnp.mean(upstream, axis=-1, keepdims=True)
        - normed * jnp.mean(upstream * normed, axis=-1, keepdims=True)
    )


def pick(array, index):
    return lax.dynamic_index_in_dim(array, index, 0, keepdims=False)


def masked_scores(query_block, keys, labels, begin, scale):
    scores = (
        jnp.einsum("qhe,khe->hqk", query_block, keys, preferred_element_type=jnp.float32) * scale
    )
    same = labels[begin : begin + query_block.shape[0], None] == labels[None, :]
    return jnp.where(same[None], scores, -1e30)


def attend_forward(query, keys, values, labels):
    rows = query.shape[0]
    scale = query.shape[2] ** (-0.5)
    block = min(block_rows, rows)
    outputs = []
    totals = []
    for begin in range(0, rows, block):
        scores = masked_scores(query[begin : begin + block], keys, labels, begin, scale)
        peak = jnp.max(scores, axis=-1, keepdims=True)
        expos = jnp.exp(scores - peak)
        total = jnp.sum(expos, axis=-1, keepdims=True)
        weights = (expos / total).astype(jnp.bfloat16)
        outputs.append(
            jnp.einsum("hqk,khe->qhe", weights, values, preferred_element_type=jnp.float32)
        )
        totals.append((peak + jnp.log(total))[..., 0])
    return (jnp.concatenate(outputs, axis=0), jnp.concatenate(totals, axis=1))


def attend_back(query, keys, values, labels, logsum, upstream):
    rows = query.shape[0]
    scale = query.shape[2] ** (-0.5)
    block = min(block_rows, rows)
    query_parts = []
    key_grad = jnp.zeros(keys.shape, jnp.float32)
    value_grad = jnp.zeros(values.shape, jnp.float32)
    for begin in range(0, rows, block):
        query_block = query[begin : begin + block]
        upstream_block = upstream[begin : begin + block]
        scores = masked_scores(query_block, keys, labels, begin, scale)
        weights = jnp.exp(scores - logsum[:, begin : begin + block, None])
        weight_grad = jnp.einsum(
            "qhe,khe->hqk", upstream_block, values, preferred_element_type=jnp.float32
        )
        delta = jnp.sum(weight_grad * weights, axis=-1, keepdims=True)
        score_grad = (weights * (weight_grad - delta)).astype(jnp.bfloat16)
        query_parts.append(
            jnp.einsum("hqk,khe->qhe", score_grad, keys, preferred_element_type=jnp.float32) * scale
        )
        key_grad = (
            key_grad
            + jnp.einsum(
                "hqk,qhe->khe", score_grad, query_block, preferred_element_type=jnp.float32
            )
            * scale
        )
        value_grad = value_grad + jnp.einsum(
            "hqk,qhe->khe",
            weights.astype(jnp.bfloat16),
            upstream_block,
            preferred_element_type=jnp.float32,
        )
    return (jnp.concatenate(query_parts, axis=0), key_grad, value_grad)


def on_device(
    x_in, cotangent, cond, crop_len, head_mask, skip_mask, ada_w, qkv_w, proj_w, fc1_w, fc2_w
):
    micro, local, width = x_in.shape
    row = skip_mask.shape[1]
    slots = crop_len.shape[1]
    heads_here = head_mask.shape[2]
    ada = ada_w[0]
    wqkv = qkv_w[0]
    wproj = proj_w[0]
    wup = fc1_w[0]
    wdown = fc2_w[0]
    head_cols = wqkv.shape[2]
    head_dim = head_cols // heads_here
    hidden_cols = wup.shape[1]
    section = lax.axis_index("section")
    tensor_index = lax.axis_index("tensor")
    condition = jax.nn.silu(cond.astype(jnp.float32)).astype(jnp.bfloat16)
    mod_local = jnp.einsum("msd,de->mse", condition, ada, preferred_element_type=jnp.float32)
    modulation = lax.all_gather(mod_local, "tensor", axis=2, tiled=True)
    places = jnp.arange(row, dtype=jnp.int32)
    finish = jnp.cumsum(crop_len, axis=1)
    begin = finish - crop_len
    inside = (places[None, :, None] >= begin[:, None, :]) & (
        places[None, :, None] < finish[:, None, :]
    )
    flags = inside.astype(jnp.int32)
    labels = jnp.sum(flags * jnp.arange(slots, dtype=jnp.int32)[None, None, :], axis=2)
    labels = labels + (1 - jnp.sum(flags, axis=2)) * slots
    member = inside.astype(jnp.float32)
    token_heads = jnp.einsum("mns,msh->mnh", member, head_mask.astype(jnp.float32))
    member_mine = lax.dynamic_slice_in_dim(member, tensor_index * local, local, 1)
    skip_rows = skip_mask.astype(jnp.float32)

    def token_mod(index):
        return jnp.split(
            jnp.dot(pick(member_mine, index), pick(modulation, index), precision=highest), 6, axis=1
        )

    def forward(index, inputs):
        shift_one, scale_one, gate_one, shift_two, scale_two, gate_two = token_mod(index)
        normed_one, factor_one = normalize_keep(inputs)
        first_local = (normed_one * (1.0 + scale_one) + shift_one).astype(jnp.bfloat16)
        first_rows = lax.all_gather(first_local, "tensor", axis=0, tiled=True)
        project = jnp.einsum(
            "nd,cde->cne", first_rows, wqkv, preferred_element_type=jnp.float32
        ).astype(jnp.bfloat16)
        query = project[0].reshape(row, heads_here, head_dim)
        keys = project[1].reshape(row, heads_here, head_dim)
        values = project[2].reshape(row, heads_here, head_dim)
        mixed, logsum = attend_forward(query, keys, values, pick(labels, index))
        mixed = (
            (mixed * pick(token_heads, index)[:, :, None])
            .reshape(row, head_cols)
            .astype(jnp.bfloat16)
        )
        attended = lax.psum_scatter(
            jnp.dot(mixed, wproj, preferred_element_type=jnp.float32),
            "tensor",
            scatter_dimension=0,
            tiled=True,
        )
        middle = inputs + gate_one * attended
        normed_two, factor_two = normalize_keep(middle)
        second_local = (normed_two * (1.0 + scale_two) + shift_two).astype(jnp.bfloat16)
        second_rows = lax.all_gather(second_local, "tensor", axis=0, tiled=True)
        hidden_pre = jnp.dot(second_rows, wup, preferred_element_type=jnp.float32)
        skip_now = pick(skip_rows, index)
        hidden = (jax.nn.gelu(hidden_pre, approximate=True) * skip_now[:, None]).astype(
            jnp.bfloat16
        )
        feed = lax.psum_scatter(
            jnp.dot(hidden, wdown, preferred_element_type=jnp.float32),
            "tensor",
            scatter_dimension=0,
            tiled=True,
        )
        output = middle + gate_two * feed
        squares = jnp.stack(
            [
                jnp.sqrt(jnp.mean(attended * attended, axis=1)),
                jnp.sqrt(jnp.mean(feed * feed, axis=1)),
            ]
        )
        kept = (
            inputs,
            first_rows,
            project,
            logsum,
            mixed,
            attended,
            middle,
            second_rows,
            hidden_pre,
            feed,
        )
        return (output, squares, kept)

    def backward(index, upstream, kept):
        (
            inputs,
            first_rows,
            project,
            logsum,
            mixed_keep,
            attended,
            middle,
            second_rows,
            hidden_pre,
            feed,
        ) = kept
        shift_one, scale_one, gate_one, shift_two, scale_two, gate_two = token_mod(index)
        normed_one, factor_one = normalize_keep(inputs)
        normed_two, factor_two = normalize_keep(middle)
        skip_now = pick(skip_rows, index)
        feed_grad = (upstream * gate_two).astype(jnp.bfloat16)
        gate_two_grad = upstream * feed
        feed_rows = lax.all_gather(feed_grad, "tensor", axis=0, tiled=True)

        def activation(value):
            return jax.nn.gelu(value, approximate=True) * skip_now[:, None]

        hidden_value, activation_back = jax.vjp(activation, hidden_pre)
        hidden = hidden_value.astype(jnp.bfloat16)
        down_grad = jnp.einsum("nf,nd->fd", hidden, feed_rows, preferred_element_type=jnp.float32)
        hidden_grad = jnp.einsum("nd,fd->nf", feed_rows, wdown, preferred_element_type=jnp.float32)
        pre_grad = activation_back(hidden_grad)[0].astype(jnp.bfloat16)
        up_grad = jnp.einsum("nd,nf->df", second_rows, pre_grad, preferred_element_type=jnp.float32)
        second_grad = lax.psum_scatter(
            jnp.einsum(
                "nf,df->nd",
                lax.slice_in_dim(pre_grad, 0, lax.axis_size("tensor") * local, axis=0),
                wup,
                preferred_element_type=jnp.float32,
            ),
            "tensor",
            scatter_dimension=0,
            tiled=True,
        )
        scale_two_grad = second_grad * normed_two
        middle_grad = upstream + normalize_back(
            normed_two, factor_two, second_grad * (1.0 + scale_two)
        )
        gate_one_grad = middle_grad * attended
        attn_grad = (middle_grad * gate_one).astype(jnp.bfloat16)
        attn_rows = lax.all_gather(attn_grad, "tensor", axis=0, tiled=True)
        mixed_grad = jnp.einsum(
            "nd,ed->ne", attn_rows, wproj, preferred_element_type=jnp.float32
        ).astype(jnp.bfloat16)
        proj_grad = jnp.einsum(
            "ne,nd->ed", mixed_keep, attn_rows, preferred_element_type=jnp.float32
        )
        head_gate = pick(token_heads, index).astype(jnp.bfloat16)
        mixed_grad = mixed_grad.reshape(row, heads_here, head_dim) * head_gate[:, :, None]
        query = project[0].reshape(row, heads_here, head_dim)
        keys = project[1].reshape(row, heads_here, head_dim)
        values = project[2].reshape(row, heads_here, head_dim)
        query_grad, key_grad, value_grad = attend_back(
            query, keys, values, pick(labels, index), logsum, mixed_grad
        )
        project_grad = (
            jnp.stack([query_grad, key_grad, value_grad])
            .reshape(3, row, head_cols)
            .astype(jnp.bfloat16)
        )
        qkv_grad = jnp.einsum(
            "nd,cne->cde", first_rows, project_grad, preferred_element_type=jnp.float32
        )
        first_grad = lax.psum_scatter(
            jnp.einsum("cne,cde->nd", project_grad, wqkv, preferred_element_type=jnp.float32),
            "tensor",
            scatter_dimension=0,
            tiled=True,
        )
        input_grad = middle_grad + normalize_back(
            normed_one, factor_one, first_grad * (1.0 + scale_one)
        )
        token_grad = jnp.concatenate(
            [
                first_grad,
                first_grad * normed_one,
                gate_one_grad,
                second_grad,
                scale_two_grad,
                gate_two_grad,
            ],
            axis=1,
        )
        mod_grad = jnp.einsum("ns,ne->se", pick(member_mine, index), token_grad, precision=highest)
        return (input_grad, (qkv_grad, proj_grad, up_grad, down_grad), mod_grad)

    def forward_tick(received, tick):
        index = jnp.clip(tick - section, 0, micro - 1)
        first_in = pick(x_in, jnp.clip(tick, 0, micro - 1)).astype(jnp.float32)
        inputs = jnp.where(section == 0, first_in, received)
        output, squares, kept = forward(index, inputs)
        sent = passed_along(output, "section", 1)
        return (sent, (output, squares, kept))

    start_recv = jnp.zeros((local, width), jnp.float32)
    ticks = jnp.arange(micro + 1, dtype=jnp.int32)
    unused, (outputs, squares_all, kept_all) = lax.scan(forward_tick, start_recv, ticks)
    residual = lax.dynamic_slice_in_dim(outputs, section, micro, 0)
    sublayer = lax.dynamic_slice_in_dim(squares_all, section, micro, 0)
    part = 1
    start_sums = (
        jnp.zeros((3, width // part, head_cols), jnp.float32),
        jnp.zeros((head_cols, width // part), jnp.float32),
        jnp.zeros((width // part, hidden_cols), jnp.float32),
        jnp.zeros((hidden_cols, width // part), jnp.float32),
    )

    def backward_tick(carry, tick):
        received, sums = carry
        raw_index = micro - tick - section
        valid = (raw_index >= 0) & (raw_index < micro)
        index = jnp.clip(raw_index, 0, micro - 1)
        first_in = pick(cotangent, index).astype(jnp.float32)
        upstream = jnp.where(section == 1, first_in, received)
        kept = jax.tree.map(lambda stacked: pick(stacked, index + section), kept_all)
        input_grad, grads, mod_grad = backward(index, upstream, kept)
        qkv_part, proj_part, up_part, down_part = grads
        fresh = (qkv_part, proj_part, up_part, down_part)
        sums = jax.tree.map(
            lambda total, extra: jnp.where(valid, total + extra, total), sums, fresh
        )
        low_grad = input_grad.astype(jnp.bfloat16)
        sent = passed_along(input_grad, "section", -1)
        return ((sent, sums), (low_grad, mod_grad))

    (unused_recv, sums), (grad_stack, mod_stack) = lax.scan(
        backward_tick, (start_recv, start_sums), ticks
    )
    input_grads = jnp.flip(lax.dynamic_slice_in_dim(grad_stack, 1 - section, micro, 0), 0)
    mod_grads = jnp.flip(lax.dynamic_slice_in_dim(mod_stack, 1 - section, micro, 0), 0)
    mod_mine = lax.psum_scatter(mod_grads, "tensor", scatter_dimension=2, tiled=True)
    ada_grad = jnp.einsum("msd,mse->de", condition.astype(jnp.float32), mod_mine, precision=highest)
    qkv_sum, proj_sum, up_sum, down_sum = sums
    ada_grad, qkv_sum, proj_sum, up_sum, down_sum = (
        lax.psum_scatter(ada_grad, "dp", scatter_dimension=0, tiled=True),
        lax.psum_scatter(qkv_sum, "dp", scatter_dimension=1, tiled=True),
        lax.psum_scatter(proj_sum, "dp", scatter_dimension=1, tiled=True),
        lax.psum_scatter(up_sum, "dp", scatter_dimension=0, tiled=True),
        lax.psum_scatter(down_sum, "dp", scatter_dimension=1, tiled=True),
    )
    sublayer_rms = jnp.transpose(sublayer, (1, 0, 2))
    return (
        residual[None],
        input_grads[None],
        sublayer_rms[None],
        ada_grad[None],
        qkv_sum[None],
        proj_sum[None],
        up_sum[None],
        down_sum[None],
    )


def solution(mesh):
    in_specs = (
        P(None, ("dp", "tensor"), None),
        P(None, ("dp", "tensor"), None),
        P(None, "dp", None),
        P(None, "dp"),
        P(None, "dp", "tensor"),
        P(None, "dp"),
        P("section", None, "tensor"),
        P("section", None, None, "tensor"),
        P("section", "tensor", None),
        P("section", None, "tensor"),
        P("section", "tensor", None),
    )
    out_specs = (
        P("section", None, ("dp", "tensor"), None),
        P("section", None, ("dp", "tensor"), None),
        P("section", None, None, ("dp", "tensor")),
        P("section", "dp", "tensor"),
        P("section", None, "dp", "tensor"),
        P("section", "tensor", "dp"),
        P("section", "dp", "tensor"),
        P("section", "tensor", "dp"),
    )
    return jax.shard_map(
        on_device, mesh=mesh, in_specs=in_specs, out_specs=out_specs, check_vma=False
    )
```

profile of v0, /device:TPU:0, one launch (start us, length us, event | category | flops | bytes accessed | tf_op | source)
XLA Modules:
  0.0 2917.1 jit_solution(14826599475353044328)
XLA Ops:
  18.1 122.7 %all_gather.23 = f32[3,8,6912]{1,0,2:T(4,128)} all-gather(f32[3,8,1728]{1,0,2:T(4,128)S(1)} %copy.22), channel_id=1, replica_groups=mesh['section'=2,'tensor'=4,'dp'=4] {'tensor'}, dimensions={2}, use_global_device_ids=true | all-gather | bytes 829440 | tf_op jit(solution)/shard_map/all_gather | solution.py:117
  140.9 10.8 copy.23
  154.5 1039.2 %while.60 = (s32[]{:T(128)}, f32[256,1152]{1,0:T(8,128)S(1)}, f32[4,256,1152]{2,1,0:T(8,128)}, f32[4,2,256]{2,1,0:T(2,128)}, f32[4,256,1152]{2,1,0:T(8,128)}, /*...) while((s32[]{:T(128)}, f32[256,1152]{1,0:T(8,128)S(1)}, ...), condition=%wide.region_16.17_spmd, body=%wide.region_3.16_spmd.sunk | while | flops 9606234112 | bytes 266242736 | solution.py:299
  170.8 37.1 %all-gather.5.cloned.1.call-done = bf16[1024,1152]{1,0:T(8,128)(2,1)} async-done(((bf16[256,1152]{1,0:T(8,128)(2,1)}), bf16[1024,1152]{1,0:T(8,128)(2,1)}) %all-gather.5.cloned.1.call-update) | async-done | bytes 2359312 | tf_op jit(solution)/shard_map/while/body/eval_jaxpr/all_gather | solution.py:141
  232.1 57.2 %reduce-scatter.27.cloned.1.call-done = f32[256,1152]{1,0:T(8,128)} async-done(((f32[1024,1152]{1,0:T(8,128)}), f32[256,1152]{1,0:T(8,128)}) %reduce-scatter.27.cloned.1.call-update) | async-done | bytes 1179664 | tf_op jit(solution)/shard_map/while/body/eval_jaxpr/reduce_scatter | solution.py:154
  296.6 36.8 %all-gather.7.cloned.1.call-done = bf16[1024,1152]{1,0:T(8,128)(2,1)} async-done(((bf16[256,1152]{1,0:T(8,128)(2,1)}), bf16[1024,1152]{1,0:T(8,128)(2,1)}) %all-gather.7.cloned.1.call-update) | async-done | bytes 2359312 | tf_op jit(solution)/shard_map/while/body/eval_jaxpr/all_gather | solution.py:163
  333.4 8.3 bitcast_dynamic-update-slice_fusion.21
  354.3 50.8 %reduce-scatter.29.cloned.1.call-done = f32[256,1152]{1,0:T(8,128)} async-done(((f32[1024,1152]{1,0:T(8,128)}), f32[256,1152]{1,0:T(8,128)}) %reduce-scatter.29.cloned.1.call-update) | async-done | bytes 1179664 | tf_op jit(solution)/shard_map/while/body/eval_jaxpr/reduce_scatter | solution.py:169
  430.8 36.8 %all-gather.5.cloned.1.call-done = bf16[1024,1152]{1,0:T(8,128)(2,1)} async-done(((bf16[256,1152]{1,0:T(8,128)(2,1)}), bf16[1024,1152]{1,0:T(8,128)(2,1)}) %all-gather.5.cloned.1.call-update) | async-done | bytes 2359312 | tf_op jit(solution)/shard_map/while/body/eval_jaxpr/all_gather | solution.py:141
  491.9 57.2 %reduce-scatter.27.cloned.1.call-done = f32[256,1152]{1,0:T(8,128)} async-done(((f32[1024,1152]{1,0:T(8,128)}), f32[256,1152]{1,0:T(8,128)}) %reduce-scatter.27.cloned.1.call-update) | async-done | bytes 1179664 | tf_op jit(solution)/shard_map/while/body/eval_jaxpr/reduce_scatter | solution.py:154
  556.3 36.9 %all-gather.7.cloned.1.call-done = bf16[1024,1152]{1,0:T(8,128)(2,1)} async-done(((bf16[256,1152]{1,0:T(8,128)(2,1)}), bf16[1024,1152]{1,0:T(8,128)(2,1)}) %all-gather.7.cloned.1.call-update) | async-done | bytes 2359312 | tf_op jit(solution)/shard_map/while/body/eval_jaxpr/all_gather | solution.py:163
  593.1 8.3 bitcast_dynamic-update-slice_fusion.21
  614.0 50.9 %reduce-scatter.29.cloned.1.call-done = f32[256,1152]{1,0:T(8,128)} async-done(((f32[1024,1152]{1,0:T(8,128)}), f32[256,1152]{1,0:T(8,128)}) %reduce-scatter.29.cloned.1.call-update) | async-done | bytes 1179664 | tf_op jit(solution)/shard_map/while/body/eval_jaxpr/reduce_scatter | solution.py:169
  690.6 36.8 %all-gather.5.cloned.1.call-done = bf16[1024,1152]{1,0:T(8,128)(2,1)} async-done(((bf16[256,1152]{1,0:T(8,128)(2,1)}), bf16[1024,1152]{1,0:T(8,128)(2,1)}) %all-gather.5.cloned.1.call-update) | async-done | bytes 2359312 | tf_op jit(solution)/shard_map/while/body/eval_jaxpr/all_gather | solution.py:141
  751.6 57.2 %reduce-scatter.27.cloned.1.call-done = f32[256,1152]{1,0:T(8,128)} async-done(((f32[1024,1152]{1,0:T(8,128)}), f32[256,1152]{1,0:T(8,128)}) %reduce-scatter.27.cloned.1.call-update) | async-done | bytes 1179664 | tf_op jit(solution)/shard_map/while/body/eval_jaxpr/reduce_scatter | solution.py:154
  816.2 36.8 %all-gather.7.cloned.1.call-done = bf16[1024,1152]{1,0:T(8,128)(2,1)} async-done(((bf16[256,1152]{1,0:T(8,128)(2,1)}), bf16[1024,1152]{1,0:T(8,128)(2,1)}) %all-gather.7.cloned.1.call-update) | async-done | bytes 2359312 | tf_op jit(solution)/shard_map/while/body/eval_jaxpr/all_gather | solution.py:163
  853.0 8.2 bitcast_dynamic-update-slice_fusion.21
  873.8 50.8 %reduce-scatter.29.cloned.1.call-done = f32[256,1152]{1,0:T(8,128)} async-done(((f32[1024,1152]{1,0:T(8,128)}), f32[256,1152]{1,0:T(8,128)}) %reduce-scatter.29.cloned.1.call-update) | async-done | bytes 1179664 | tf_op jit(solution)/shard_map/while/body/eval_jaxpr/reduce_scatter | solution.py:169
  950.3 36.8 %all-gather.5.cloned.1.call-done = bf16[1024,1152]{1,0:T(8,128)(2,1)} async-done(((bf16[256,1152]{1,0:T(8,128)(2,1)}), bf16[1024,1152]{1,0:T(8,128)(2,1)}) %all-gather.5.cloned.1.call-update) | async-done | bytes 2359312 | tf_op jit(solution)/shard_map/while/body/eval_jaxpr/all_gather | solution.py:141
  1011.4 57.2 %reduce-scatter.27.cloned.1.call-done = f32[256,1152]{1,0:T(8,128)} async-done(((f32[1024,1152]{1,0:T(8,128)}), f32[256,1152]{1,0:T(8,128)}) %reduce-scatter.27.cloned.1.call-update) | async-done | bytes 1179664 | tf_op jit(solution)/shard_map/while/body/eval_jaxpr/reduce_scatter | solution.py:154
  1075.8 36.8 %all-gather.7.cloned.1.call-done = bf16[1024,1152]{1,0:T(8,128)(2,1)} async-done(((bf16[256,1152]{1,0:T(8,128)(2,1)}), bf16[1024,1152]{1,0:T(8,128)(2,1)}) %all-gather.7.cloned.1.call-update) | async-done | bytes 2359312 | tf_op jit(solution)/shard_map/while/body/eval_jaxpr/all_gather | solution.py:163
  1112.7 8.2 bitcast_dynamic-update-slice_fusion.21
  1133.5 50.8 %reduce-scatter.29.cloned.1.call-done = f32[256,1152]{1,0:T(8,128)} async-done(((f32[1024,1152]{1,0:T(8,128)}), f32[256,1152]{1,0:T(8,128)}) %reduce-scatter.29.cloned.1.call-update) | async-done | bytes 1179664 | tf_op jit(solution)/shard_map/while/body/eval_jaxpr/reduce_scatter | solution.py:169
  1194.4 1163.0 %while.61 = (s32[]{:T(128)}, f32[256,1152]{1,0:T(8,128)S(1)}, f32[3,1152,288]{1,2,0:T(8,128)}, f32[288,1152]{1,0:T(8,128)}, f32[1152,1152]{1,0:T(8,128)}, /*inde...) while((s32[]{:T(128)}, f32[256,1152]{1,0:T(8,128)S(1)}, ...), condition=%wide.region_30.31_spmd.clone, body=%wide.region_17.30_spmd.clone.sunk | while | flops 19803746304 | bytes 553315328 | solution.py:328
  1216.9 36.8 %all-gather.9.cloned.1.call-done = bf16[1024,1152]{1,0:T(8,128)(2,1)} async-done(((bf16[256,1152]{1,0:T(8,128)(2,1)}), bf16[1024,1152]{1,0:T(8,128)(2,1)}) %all-gather.9.cloned.1.call-update) | async-done | bytes 2359312 | tf_op jit(solution)/shard_map/while/body/eval_jaxpr/all_gather | solution.py:215
  1253.8 9.3 fusion.353
  1273.1 53.8 %reduce-scatter.31.cloned.1.call-done = f32[256,1152]{1,0:T(8,128)} async-done(((f32[1024,1152]{1,0:T(8,128)}), f32[256,1152]{1,0:T(8,128)}) %reduce-scatter.31.cloned.1.call-update) | async-done | bytes 1179664 | tf_op jit(solution)/shard_map/while/body/eval_jaxpr/reduce_scatter | solution.py:226
  1349.2 21.9 all-gather.11.cloned.1.call-done
  1416.4 8.2 fusion.369
  1424.6 8.8 fusion.370
  1442.7 28.0 reduce-scatter.33.cloned.1.call-done
  1502.9 37.7 %all-gather.9.cloned.1.call-done = bf16[1024,1152]{1,0:T(8,128)(2,1)} async-done(((bf16[256,1152]{1,0:T(8,128)(2,1)}), bf16[1024,1152]{1,0:T(8,128)(2,1)}) %all-gather.9.cloned.1.call-update) | async-done | bytes 2359312 | tf_op jit(solution)/shard_map/while/body/eval_jaxpr/all_gather | solution.py:215
  1540.6 9.2 fusion.353
  1556.6 13.0 all-gather.11.cloned.1.call-start
  1572.7 41.1 %reduce-scatter.31.cloned.1.call-done = f32[256,1152]{1,0:T(8,128)} async-done(((f32[1024,1152]{1,0:T(8,128)}), f32[256,1152]{1,0:T(8,128)}) %reduce-scatter.31.cloned.1.call-update) | async-done | bytes 1179664 | tf_op jit(solution)/shard_map/while/body/eval_jaxpr/reduce_scatter | solution.py:226
  1636.0 21.9 all-gather.11.cloned.1.call-done
  1703.1 10.1 fusion.369
  1713.3 10.7 fusion.370
  1734.8 22.6 reduce-scatter.33.cloned.1.call-done
  1789.7 37.7 %all-gather.9.cloned.1.call-done = bf16[1024,1152]{1,0:T(8,128)(2,1)} async-done(((bf16[256,1152]{1,0:T(8,128)(2,1)}), bf16[1024,1152]{1,0:T(8,128)(2,1)}) %all-gather.9.cloned.1.call-update) | async-done | bytes 2359312 | tf_op jit(solution)/shard_map/while/body/eval_jaxpr/all_gather | solution.py:215
  1827.4 9.2 fusion.353
  1846.8 53.8 %reduce-scatter.31.cloned.1.call-done = f32[256,1152]{1,0:T(8,128)} async-done(((f32[1024,1152]{1,0:T(8,128)}), f32[256,1152]{1,0:T(8,128)}) %reduce-scatter.31.cloned.1.call-update) | async-done | bytes 1179664 | tf_op jit(solution)/shard_map/while/body/eval_jaxpr/reduce_scatter | solution.py:226
  1922.8 21.9 all-gather.11.cloned.1.call-done
  1990.1 10.1 fusion.369
  2000.2 10.7 fusion.370
  2014.5 7.4 add_select_fusion.2
  2021.8 22.5 reduce-scatter.33.cloned.1.call-done
  2076.6 37.7 %all-gather.9.cloned.1.call-done = bf16[1024,1152]{1,0:T(8,128)(2,1)} async-done(((bf16[256,1152]{1,0:T(8,128)(2,1)}), bf16[1024,1152]{1,0:T(8,128)(2,1)}) %all-gather.9.cloned.1.call-update) | async-done | bytes 2359312 | tf_op jit(solution)/shard_map/while/body/eval_jaxpr/all_gather | solution.py:215
  2114.3 9.2 fusion.353
  2130.2 13.0 all-gather.11.cloned.1.call-start
  2146.4 41.1 %reduce-scatter.31.cloned.1.call-done = f32[256,1152]{1,0:T(8,128)} async-done(((f32[1024,1152]{1,0:T(8,128)}), f32[256,1152]{1,0:T(8,128)}) %reduce-scatter.31.cloned.1.call-update) | async-done | bytes 1179664 | tf_op jit(solution)/shard_map/while/body/eval_jaxpr/reduce_scatter | solution.py:226
  2209.7 21.9 all-gather.11.cloned.1.call-done
  2276.9 10.1 fusion.369
  2287.0 10.7 fusion.370
  2308.6 22.5 reduce-scatter.33.cloned.1.call-done
  2358.6 9.0 copy.28
  2367.7 14.3 reshape.406
  2398.9 31.1 %reduce-scatter.23.cloned.1.call-done = f32[1728,24]{1,0:T(8,128)} async-done(((f32[6912,24]{1,0:T(8,128)}), f32[1728,24]{1,0:T(8,128)}) %reduce-scatter.23.cloned.1.call-update) | async-done | bytes 165904
  2433.0 10.9 convolution_bitcast_fusion.2
  2451.1 19.4 reduce-scatter.25.cloned.1.call-done
  2472.5 94.6 %reduce-scatter.17.cloned.1.call-done = f32[3,288,288]{2,1,0:T(8,128)} async-done(((f32[3,1152,288]{2,1,0:T(8,128)}), f32[3,288,288]{2,1,0:T(8,128)}) %reduce-scatter.17.cloned.1.call-update) | async-done | bytes 995344 | tf_op jit(solution)/shard_map/reduce_scatter | solution.py:338
  2567.1 98.2 %reduce-scatter.19.cloned.1.call-done = f32[288,1152]{1,0:T(8,128)} async-done(((f32[1152,1152]{1,0:T(8,128)}), f32[288,1152]{1,0:T(8,128)}) %reduce-scatter.19.cloned.1.call-update) | async-done | bytes 1327120 | tf_op jit(solution)/shard_map/reduce_scatter | solution.py:340
  2665.3 98.3 %reduce-scatter.21.cloned.1.call-done = f32[1152,288]{0,1:T(8,128)} async-done(((f32[1152,1152]{0,1:T(8,128)}), f32[1152,288]{0,1:T(8,128)}) %reduce-scatter.21.cloned.1.call-update) | async-done | bytes 1327120 | tf_op jit(solution)/shard_map/reduce_scatter | solution.py:341
  2763.6 145.9 %reduce-scatter.15.cloned.1.call-done = f32[288,1728]{1,0:T(8,128)} async-done(((f32[1152,1728]{1,0:T(8,128)}), f32[288,1728]{1,0:T(8,128)}) %reduce-scatter.15.cloned.1.call-update) | async-done | bytes 1990672 | tf_op jit(solution)/shard_map/reduce_scatter | solution.py:337
  (984 shorter events, 784.3 us)
Async XLA Ops:
  154.5 15.6 copy-start.34
  154.6 53.3 %all-gather.5.cloned.1.call-start = ((), (), s32[]{:S(2)}) async-start(), calls=%async_computation.16 | async-start | bytes 2949120 | tf_op jit(solution)/shard_map/while/body/eval_jaxpr/all_gather | solution.py:141
  170.0 119.4 %reduce-scatter.27.cloned.1.call-start = ((), (), s32[]{:S(2)}) async-start(), calls=%async_computation.17 | async-start | bytes 5898240 | tf_op jit(solution)/shard_map/while/body/eval_jaxpr/reduce_scatter | solution.py:154
  232.1 101.4 %all-gather.7.cloned.1.call-start = ((), (), s32[]{:S(2)}) async-start(), calls=%async_computation.18 | async-start | bytes 2949120 | tf_op jit(solution)/shard_map/while/body/eval_jaxpr/all_gather | solution.py:163
  295.8 109.3 %reduce-scatter.29.cloned.1.call-start = ((), (), s32[]{:S(2)}) async-start(), calls=%async_computation.19 | async-start | bytes 5898240 | tf_op jit(solution)/shard_map/while/body/eval_jaxpr/reduce_scatter | solution.py:169
  408.5 6.0 collective-permute-start
  414.5 15.5 copy-start.28
  414.5 15.6 copy-start.34
  414.5 53.1 %all-gather.5.cloned.1.call-start = ((), (), s32[]{:S(2)}) async-start(), calls=%async_computation.16 | async-start | bytes 2949120 | tf_op jit(solution)/shard_map/while/body/eval_jaxpr/all_gather | solution.py:141
  430.0 119.1 %reduce-scatter.27.cloned.1.call-start = ((), (), s32[]{:S(2)}) async-start(), calls=%async_computation.17 | async-start | bytes 5898240 | tf_op jit(solution)/shard_map/while/body/eval_jaxpr/reduce_scatter | solution.py:154
  491.8 101.3 %all-gather.7.cloned.1.call-start = ((), (), s32[]{:S(2)}) async-start(), calls=%async_computation.18 | async-start | bytes 2949120 | tf_op jit(solution)/shard_map/while/body/eval_jaxpr/all_gather | solution.py:163
  555.5 109.3 %reduce-scatter.29.cloned.1.call-start = ((), (), s32[]{:S(2)}) async-start(), calls=%async_computation.19 | async-start | bytes 5898240 | tf_op jit(solution)/shard_map/while/body/eval_jaxpr/reduce_scatter | solution.py:169
  668.2 6.1 collective-permute-start
  674.3 15.6 copy-start.34
  674.3 53.0 %all-gather.5.cloned.1.call-start = ((), (), s32[]{:S(2)}) async-start(), calls=%async_computation.16 | async-start | bytes 2949120 | tf_op jit(solution)/shard_map/while/body/eval_jaxpr/all_gather | solution.py:141
  689.7 119.1 %reduce-scatter.27.cloned.1.call-start = ((), (), s32[]{:S(2)}) async-start(), calls=%async_computation.17 | async-start | bytes 5898240 | tf_op jit(solution)/shard_map/while/body/eval_jaxpr/reduce_scatter | solution.py:154
  751.6 101.4 %all-gather.7.cloned.1.call-start = ((), (), s32[]{:S(2)}) async-start(), calls=%async_computation.18 | async-start | bytes 2949120 | tf_op jit(solution)/shard_map/while/body/eval_jaxpr/all_gather | solution.py:163
  815.4 109.2 %reduce-scatter.29.cloned.1.call-start = ((), (), s32[]{:S(2)}) async-start(), calls=%async_computation.19 | async-start | bytes 5898240 | tf_op jit(solution)/shard_map/while/body/eval_jaxpr/reduce_scatter | solution.py:169
  928.1 6.0 collective-permute-start
  934.1 15.5 copy-start.28
  934.1 15.6 copy-start.34
  934.1 53.0 %all-gather.5.cloned.1.call-start = ((), (), s32[]{:S(2)}) async-start(), calls=%async_computation.16 | async-start | bytes 2949120 | tf_op jit(solution)/shard_map/while/body/eval_jaxpr/all_gather | solution.py:141
  949.5 119.1 %reduce-scatter.27.cloned.1.call-start = ((), (), s32[]{:S(2)}) async-start(), calls=%async_computation.17 | async-start | bytes 5898240 | tf_op jit(solution)/shard_map/while/body/eval_jaxpr/reduce_scatter | solution.py:154
  1011.4 101.3 %all-gather.7.cloned.1.call-start = ((), (), s32[]{:S(2)}) async-start(), calls=%async_computation.18 | async-start | bytes 2949120 | tf_op jit(solution)/shard_map/while/body/eval_jaxpr/all_gather | solution.py:163
  1075.0 109.2 %reduce-scatter.29.cloned.1.call-start = ((), (), s32[]{:S(2)}) async-start(), calls=%async_computation.19 | async-start | bytes 5898240 | tf_op jit(solution)/shard_map/while/body/eval_jaxpr/reduce_scatter | solution.py:169
  1187.7 6.0 collective-permute-start
  1203.1 50.6 %all-gather.9.cloned.1.call-start = ((), (), s32[]{:S(2)}) async-start(), calls=%async_computation.20 | async-start | bytes 2949120 | tf_op jit(solution)/shard_map/while/body/eval_jaxpr/all_gather | solution.py:215
  1216.1 110.8 %reduce-scatter.31.cloned.1.call-start = ((), (), s32[]{:S(2)}) async-start(), calls=%async_computation.21 | async-start | bytes 5898240 | tf_op jit(solution)/shard_map/while/body/eval_jaxpr/reduce_scatter | solution.py:226
  1216.9 46.1 %copy-start.36 = (f32[1,1024]{1,0:T(1,128)}, f32[1,1024]{1,0:T(1,128)S(1)}, u32[]{:S(2)}) copy-start(f32[1,1024]{1,0:T(1,128)S(1)} %constant_dynamic-slice_fusion.23) | copy-start | bytes 12292 | tf_op jit(solution)/shard_map/while
  1269.7 101.3 %all-gather.11.cloned.1.call-start = ((), (), s32[]{:S(2)}) async-start(), calls=%async_computation.22 | async-start | bytes 2949120 | tf_op jit(solution)/shard_map/while/body/eval_jaxpr/all_gather | solution.py:243
  1271.6 61.8 %copy-start.26 = (f32[256]{0:T(256)}, f32[256]{0:T(256)S(1)}, u32[]{:S(2)}) copy-start(f32[256]{0:T(256)S(1)} %broadcast_multiply_fusion.19) | copy-start | bytes 3076 | tf_op jit(solution)/shard_map/while
  1273.1 60.2 %copy-start.32 = (f32[256]{0:T(256)}, f32[256]{0:T(256)S(1)}, u32[]{:S(2)}) copy-start(f32[256]{0:T(256)S(1)} %add_rsqrt_fusion.10) | copy-start | bytes 3076 | tf_op jit(solution)/shard_map/while
  1333.4 137.3 %reduce-scatter.33.cloned.1.call-start = ((), (), s32[]{:S(2)}) async-start(), calls=%async_computation.23 | async-start | bytes 5898240 | tf_op jit(solution)/shard_map/while/body/eval_jaxpr/reduce_scatter | solution.py:266
  1477.6 11.1 collective-permute-start.1
  1489.1 51.5 %all-gather.9.cloned.1.call-start = ((), (), s32[]{:S(2)}) async-start(), calls=%async_computation.20 | async-start | bytes 2949120 | tf_op jit(solution)/shard_map/while/body/eval_jaxpr/all_gather | solution.py:215
  1502.1 111.7 %reduce-scatter.31.cloned.1.call-start = ((), (), s32[]{:S(2)}) async-start(), calls=%async_computation.21 | async-start | bytes 5898240 | tf_op jit(solution)/shard_map/while/body/eval_jaxpr/reduce_scatter | solution.py:226
  1502.9 46.9 %copy-start.36 = (f32[1,1024]{1,0:T(1,128)}, f32[1,1024]{1,0:T(1,128)S(1)}, u32[]{:S(2)}) copy-start(f32[1,1024]{1,0:T(1,128)S(1)} %constant_dynamic-slice_fusion.23) | copy-start | bytes 12292 | tf_op jit(solution)/shard_map/while
  1556.6 101.3 %all-gather.11.cloned.1.call-start = ((), (), s32[]{:S(2)}) async-start(), calls=%async_computation.22 | async-start | bytes 2949120 | tf_op jit(solution)/shard_map/while/body/eval_jaxpr/all_gather | solution.py:243
  1571.2 49.1 %copy-start.26 = (f32[256]{0:T(256)}, f32[256]{0:T(256)S(1)}, u32[]{:S(2)}) copy-start(f32[256]{0:T(256)S(1)} %broadcast_multiply_fusion.19) | copy-start | bytes 3076 | tf_op jit(solution)/shard_map/while
  1572.7 47.5 %copy-start.32 = (f32[256]{0:T(256)}, f32[256]{0:T(256)S(1)}, u32[]{:S(2)}) copy-start(f32[256]{0:T(256)S(1)} %add_rsqrt_fusion.10) | copy-start | bytes 3076 | tf_op jit(solution)/shard_map/while
  1620.3 137.1 %reduce-scatter.33.cloned.1.call-start = ((), (), s32[]{:S(2)}) async-start(), calls=%async_computation.23 | async-start | bytes 5898240 | tf_op jit(solution)/shard_map/while/body/eval_jaxpr/reduce_scatter | solution.py:266
  1764.3 11.3 collective-permute-start.1
  1775.9 51.5 %all-gather.9.cloned.1.call-start = ((), (), s32[]{:S(2)}) async-start(), calls=%async_computation.20 | async-start | bytes 2949120 | tf_op jit(solution)/shard_map/while/body/eval_jaxpr/all_gather | solution.py:215
  1788.9 111.7 %reduce-scatter.31.cloned.1.call-start = ((), (), s32[]{:S(2)}) async-start(), calls=%async_computation.21 | async-start | bytes 5898240 | tf_op jit(solution)/shard_map/while/body/eval_jaxpr/reduce_scatter | solution.py:226
  1789.7 46.9 %copy-start.36 = (f32[1,1024]{1,0:T(1,128)}, f32[1,1024]{1,0:T(1,128)S(1)}, u32[]{:S(2)}) copy-start(f32[1,1024]{1,0:T(1,128)S(1)} %constant_dynamic-slice_fusion.23) | copy-start | bytes 12292 | tf_op jit(solution)/shard_map/while
  1843.3 101.4 %all-gather.11.cloned.1.call-start = ((), (), s32[]{:S(2)}) async-start(), calls=%async_computation.22 | async-start | bytes 2949120 | tf_op jit(solution)/shard_map/while/body/eval_jaxpr/all_gather | solution.py:243
  1845.2 61.8 %copy-start.26 = (f32[256]{0:T(256)}, f32[256]{0:T(256)S(1)}, u32[]{:S(2)}) copy-start(f32[256]{0:T(256)S(1)} %broadcast_multiply_fusion.19) | copy-start | bytes 3076 | tf_op jit(solution)/shard_map/while
  1846.8 60.3 %copy-start.32 = (f32[256]{0:T(256)}, f32[256]{0:T(256)S(1)}, u32[]{:S(2)}) copy-start(f32[256]{0:T(256)S(1)} %add_rsqrt_fusion.10) | copy-start | bytes 3076 | tf_op jit(solution)/shard_map/while
  1907.1 137.3 %reduce-scatter.33.cloned.1.call-start = ((), (), s32[]{:S(2)}) async-start(), calls=%async_computation.23 | async-start | bytes 5898240 | tf_op jit(solution)/shard_map/while/body/eval_jaxpr/reduce_scatter | solution.py:266
  2051.3 11.1 collective-permute-start.1
  2062.8 51.5 %all-gather.9.cloned.1.call-start = ((), (), s32[]{:S(2)}) async-start(), calls=%async_computation.20 | async-start | bytes 2949120 | tf_op jit(solution)/shard_map/while/body/eval_jaxpr/all_gather | solution.py:215
  2075.8 111.7 %reduce-scatter.31.cloned.1.call-start = ((), (), s32[]{:S(2)}) async-start(), calls=%async_computation.21 | async-start | bytes 5898240 | tf_op jit(solution)/shard_map/while/body/eval_jaxpr/reduce_scatter | solution.py:226
  2076.6 46.9 %copy-start.36 = (f32[1,1024]{1,0:T(1,128)}, f32[1,1024]{1,0:T(1,128)S(1)}, u32[]{:S(2)}) copy-start(f32[1,1024]{1,0:T(1,128)S(1)} %constant_dynamic-slice_fusion.23) | copy-start | bytes 12292 | tf_op jit(solution)/shard_map/while
  2130.2 101.4 %all-gather.11.cloned.1.call-start = ((), (), s32[]{:S(2)}) async-start(), calls=%async_computation.22 | async-start | bytes 2949120 | tf_op jit(solution)/shard_map/while/body/eval_jaxpr/all_gather | solution.py:243
  2144.8 49.1 %copy-start.26 = (f32[256]{0:T(256)}, f32[256]{0:T(256)S(1)}, u32[]{:S(2)}) copy-start(f32[256]{0:T(256)S(1)} %broadcast_multiply_fusion.19) | copy-start | bytes 3076 | tf_op jit(solution)/shard_map/while
  2146.4 47.5 %copy-start.32 = (f32[256]{0:T(256)}, f32[256]{0:T(256)S(1)}, u32[]{:S(2)}) copy-start(f32[256]{0:T(256)S(1)} %add_rsqrt_fusion.10) | copy-start | bytes 3076 | tf_op jit(solution)/shard_map/while
  2194.0 137.1 %reduce-scatter.33.cloned.1.call-start = ((), (), s32[]{:S(2)}) async-start(), calls=%async_computation.23 | async-start | bytes 5898240 | tf_op jit(solution)/shard_map/while/body/eval_jaxpr/reduce_scatter | solution.py:266
  2338.1 11.3 collective-permute-start.1
  2357.4 72.6 %reduce-scatter.23.cloned.1.call-start = ((), (), s32[]{:S(2)}) async-start(), calls=%async_computation.14 | async-start | bytes 4423680
  2382.0 88.5 %reduce-scatter.25.cloned.1.call-start = ((), (), s32[]{:S(2)}) async-start(), calls=%async_computation.15 | async-start | bytes 2211840
  2385.1 182.0 %reduce-scatter.17.cloned.1.call-start = ((), (), s32[]{:S(2)}) async-start(), calls=%async_computation.11 | async-start | bytes 6635520 | tf_op jit(solution)/shard_map/reduce_scatter | solution.py:338
  2391.1 274.2 %reduce-scatter.19.cloned.1.call-start = ((), (), s32[]{:S(2)}) async-start(), calls=%async_computation.12 | async-start | bytes 6635520 | tf_op jit(solution)/shard_map/reduce_scatter | solution.py:340
  2391.8 371.7 %reduce-scatter.21.cloned.1.call-start = ((), (), s32[]{:S(2)}) async-start(), calls=%async_computation.13 | async-start | bytes 6635520 | tf_op jit(solution)/shard_map/reduce_scatter | solution.py:341
  2398.8 510.7 %reduce-scatter.15.cloned.1.call-start = ((), (), s32[]{:S(2)}) async-start(), calls=%async_computation.10 | async-start | bytes 10321920 | tf_op jit(solution)/shard_map/reduce_scatter | solution.py:337
  (212 other events, 1139.6 us)
Sparse Core Ops, SparseCore 0:
  170.1 37.7 all-gather.4
  232.2 57.0 reduce-scatter.26
  295.9 37.4 all-gather.6
  348.0 57.0 reduce-scatter.28
  430.1 37.4 all-gather.4
  491.9 57.0 reduce-scatter.26
  555.6 37.4 all-gather.6
  607.7 57.0 reduce-scatter.28
  689.9 37.4 all-gather.4
  751.7 57.0 reduce-scatter.26
  815.5 37.4 all-gather.6
  867.5 57.0 reduce-scatter.28
  949.6 37.4 all-gather.4
  1011.5 57.0 reduce-scatter.26
  1075.2 37.4 all-gather.6
  1127.2 57.0 reduce-scatter.28
  1216.2 37.4 all-gather.8
  1269.8 57.0 reduce-scatter.30
  1333.5 37.4 all-gather.10
  1413.6 57.0 reduce-scatter.32
  1502.3 38.3 all-gather.8
  1556.7 57.0 reduce-scatter.30
  1620.4 37.4 all-gather.10
  1700.3 57.0 reduce-scatter.32
  1789.0 38.3 all-gather.8
  1843.5 57.1 reduce-scatter.30
  1907.2 37.4 all-gather.10
  1987.2 57.0 reduce-scatter.32
  2075.9 38.3 all-gather.8
  2130.4 57.1 reduce-scatter.30
  2194.1 37.4 all-gather.10
  2274.0 57.0 reduce-scatter.32
Sparse Core Ops, SparseCore 1:
  2382.1 47.9 reduce-scatter.22
  2432.2 38.3 reduce-scatter.24
  2473.4 93.7 reduce-scatter.16
  2570.0 95.2 reduce-scatter.18
  2668.3 95.2 reduce-scatter.20
  2766.5 142.9 reduce-scatter.14
where the time goes:
time: 2940 us; the launch traced here: 2920 us
  waiting for transfers between devices  1740 us (59%)
  matrix products  575 us (20%)
  other arithmetic  230 us (8%)
  local copies, waits for them, and re-layouts  163 us (6%)
  blocking collectives  123 us (4%)
  starting transfers between devices  43 us (1%)
    reduce_scatter x4, waiting for transfers between devices, forward(): lax.psum_scatter(jnp.dot(mixed, wproj, preferred_element_type=jnp.float32...  229 us
    reduce_scatter x4, waiting for transfers between devices, forward(): lax.psum_scatter(jnp.dot(hidden, wdown, preferred_element_type=jnp.float3...  203 us
    reduce_scatter x4, waiting for transfers between devices, backward(): lax.psum_scatter(jnp.einsum('nf,df->nd', lax.slice_in_dim(pre_grad, 0, la...  190 us
    all_gather x4, waiting for transfers between devices, backward(): feed_rows = lax.all_gather(feed_grad, 'tensor', axis=0, tiled=True)  150 us
    all_gather x4, waiting for transfers between devices, forward(): first_rows = lax.all_gather(first_local, 'tensor', axis=0, tiled=True)  147 us
    all_gather x4, waiting for transfers between devices, forward(): second_rows = lax.all_gather(second_local, 'tensor', axis=0, tiled=True)  147 us
    reduce_scatter x1, waiting for transfers between devices, on_device(): lax.psum_scatter(ada_grad, 'dp', scatter_dimension=0, tiled=True)  146 us
    all_gather x1, blocking collectives, on_device(): modulation = lax.all_gather(mod_local, 'tensor', axis=2, tiled=True)  123 us
  transfers between devices with their start and end apart: 46, of which 38 were waited for; matrix products, arithmetic and copies ran while one was open for 11% of the time, Pallas kernels for 0%

commit v1 on v0

v1 whole, which is shorter than its diff:
```python
import functools
import math

import jax
import jax.numpy as jnp
from jax import lax
from jax.experimental import pallas as pl
from jax.experimental.pallas import tpu as pltpu
from jax.sharding import PartitionSpec as P

highest = lax.Precision.HIGHEST
epsilon = 1e-06
f32 = jnp.float32
bf16 = jnp.bfloat16
log2e = math.log2(math.e)
kernel_vmem = 48 * 1024 * 1024


def normalize_keep(value):
    centered = value - jnp.mean(value, axis=-1, keepdims=True)
    factor = lax.rsqrt(jnp.mean(centered * centered, axis=-1, keepdims=True) + epsilon)
    return (centered * factor, factor)


def normalize_back(normed, factor, upstream):
    return factor * (
        upstream
        - jnp.mean(upstream, axis=-1, keepdims=True)
        - normed * jnp.mean(upstream * normed, axis=-1, keepdims=True)
    )


def swap_cores(block):
    return lax.ppermute(block, "section", [(0, 1), (1, 0)])


def along_x(block):
    return lax.ppermute(block, "tensor", [(0, 1), (1, 0), (2, 3), (3, 2)])


def along_y(block):
    return lax.ppermute(block, "tensor", [(0, 2), (2, 0), (1, 3), (3, 1)])


def square():
    return lax.axis_size("tensor") == 4


def half_order():
    if square():
        return [(0, 0), (2, 0), (0, 1), (1, 1), (1, 0), (3, 0), (2, 1), (3, 1)]
    return [(chunk, half) for chunk in range(lax.axis_size("tensor")) for half in (0, 1)]


def gather_rows(block):
    if not square():
        return lax.all_gather(block, "tensor", axis=0, tiled=True)
    half = block.shape[0] // 2
    from_x = along_x(block)
    from_y = along_y(block)
    far_first = along_y(from_x[:half])
    far_second = along_x(from_y[half:])
    return jnp.concatenate(
        [
            block[:half],
            from_y[:half],
            block[half:],
            from_x[half:],
            from_x[:half],
            far_first,
            from_y[half:],
            far_second,
        ],
        axis=0,
    )


def scatter_rows(partial):
    if not square():
        return lax.psum_scatter(partial, "tensor", scatter_dimension=0, tiled=True).astype(f32)
    half = partial.shape[0] // 8
    sum_x = partial[: 2 * half].astype(f32) + along_x(partial[4 * half : 6 * half]).astype(f32)
    sum_y = partial[2 * half : 4 * half].astype(f32) + along_y(partial[6 * half :]).astype(f32)
    first = sum_x[:half] + along_y(sum_x[half:].astype(bf16)).astype(f32)
    second = sum_y[:half] + along_x(sum_y[half:].astype(bf16)).astype(f32)
    return jnp.concatenate([first, second], axis=0)


def gather_columns(block):
    if not square():
        return lax.all_gather(block, "tensor", axis=1, tiled=True)
    from_x = along_x(block)
    from_y = along_y(block)
    pieces = jnp.stack([block, from_x, from_y, along_x(from_y)])
    here = lax.axis_index("tensor")
    return jnp.concatenate(
        [lax.dynamic_index_in_dim(pieces, here ^ j, 0, keepdims=False) for j in range(4)], axis=1
    )


def scatter_columns(partial):
    if not square():
        return lax.psum_scatter(partial, "tensor", scatter_dimension=1, tiled=True)
    here = lax.axis_index("tensor")
    columns = partial.shape[1] // 4

    def piece(distance):
        return lax.dynamic_slice_in_dim(partial, (here ^ distance) * columns, columns, 1)

    arrived = along_x(jnp.stack([piece(1), piece(3)]))
    return piece(0) + arrived[0] + along_y(piece(2) + arrived[1])


def gather_dp(block):
    size = lax.axis_size("dp")
    others = [
        lax.ppermute(block, "dp", [(i, (i + step) % size) for i in range(size)])
        for step in range(1, size)
    ]
    return jnp.stack([block] + others)


def dot_last(left, right):
    return lax.dot_general(left, right, (((1,), (1,)), ((), ())), preferred_element_type=f32)


def dot_plain(left, right):
    return lax.dot_general(left, right, (((1,), (0,)), ((), ())), preferred_element_type=f32)


def dot_first(left, right):
    return lax.dot_general(left, right, (((0,), (0,)), ((), ())), preferred_element_type=f32)


def attention_forward_kernel(
    heads, dim, own_ref, other_ref, label_ref, key_label_ref, mask_ref, mixed_ref, lse_ref
):
    rows = own_ref.shape[0]
    cols = heads * dim
    scale = dim ** (-0.5)
    labels = label_ref[...]
    same = [labels == key_label_ref[:, :rows], labels == key_label_ref[:, rows:]]
    mixed = []
    totals = []
    for head in range(heads):
        lo = head * dim
        query = own_ref[:, lo : lo + dim]
        keys = [own_ref[:, cols + lo : cols + lo + dim], other_ref[:, lo : lo + dim]]
        values = [
            own_ref[:, 2 * cols + lo : 2 * cols + lo + dim],
            other_ref[:, cols + lo : cols + lo + dim],
        ]
        scores = [jnp.where(same[j], dot_last(query, keys[j]), -1e30) for j in range(2)]
        peak = jnp.maximum(
            jnp.max(scores[0], axis=1, keepdims=True), jnp.max(scores[1], axis=1, keepdims=True)
        )
        expos = [jnp.exp2((scores[j] - peak) * (scale * log2e)) for j in range(2)]
        total = jnp.sum(expos[0], axis=1, keepdims=True) + jnp.sum(expos[1], axis=1, keepdims=True)
        inverse = 1.0 / total
        out = dot_plain((expos[0] * inverse).astype(bf16), values[0])
        out = out + dot_plain((expos[1] * inverse).astype(bf16), values[1])
        mixed.append((out * mask_ref[:, head : head + 1]).astype(bf16))
        totals.append(peak * scale + jnp.log(total))
    mixed_ref[...] = jnp.concatenate(mixed, axis=1)
    lse_ref[...] = jnp.concatenate(totals, axis=1)


def attention_forward(own, other, label_column, key_label_row, head_gate, heads):
    rows = own.shape[0]
    cols = own.shape[1] // 3
    return pl.pallas_call(
        functools.partial(attention_forward_kernel, heads, cols // heads),
        out_shape=(
            jax.ShapeDtypeStruct((rows, cols), bf16),
            jax.ShapeDtypeStruct((rows, heads), f32),
        ),
        compiler_params=pltpu.CompilerParams(vmem_limit_bytes=kernel_vmem),
        cost_estimate=pl.CostEstimate(
            flops=8 * rows * rows * cols,
            bytes_accessed=2 * rows * cols * 6,
            transcendentals=2 * rows * rows * heads,
        ),
        name="attend",
    )(own, other, label_column, key_label_row, head_gate)


def attention_back_kernel(
    heads,
    dim,
    own_ref,
    other_ref,
    label_ref,
    key_label_ref,
    mask_ref,
    lse_ref,
    upstream_ref,
    query_grad_ref,
    own_grad_ref,
    other_grad_ref,
):
    rows = own_ref.shape[0]
    cols = heads * dim
    scale = dim ** (-0.5)
    labels = label_ref[...]
    same = [key_label_ref[:rows, :] == labels, key_label_ref[rows:, :] == labels]
    query_grads = []
    key_grads = [[], []]
    value_grads = [[], []]
    for head in range(heads):
        lo = head * dim
        query = own_ref[:, lo : lo + dim]
        keys = [own_ref[:, cols + lo : cols + lo + dim], other_ref[:, lo : lo + dim]]
        values = [
            own_ref[:, 2 * cols + lo : 2 * cols + lo + dim],
            other_ref[:, cols + lo : cols + lo + dim],
        ]
        upstream = (upstream_ref[:, lo : lo + dim].astype(f32) * mask_ref[:, head : head + 1]).astype(bf16)
        lse = lse_ref[head : head + 1, :] * log2e
        weights = []
        weight_grads = []
        for j in range(2):
            scores = jnp.where(same[j], dot_last(keys[j], query) * (scale * log2e), -1e30)
            weights.append(jnp.exp2(scores - lse))
            weight_grads.append(dot_last(values[j], upstream))
            value_grads[j].append(dot_plain(weights[j].astype(bf16), upstream))
        delta = jnp.sum(weights[0] * weight_grads[0], axis=0, keepdims=True)
        delta = delta + jnp.sum(weights[1] * weight_grads[1], axis=0, keepdims=True)
        query_grad = None
        for j in range(2):
            score_grad = (weights[j] * (weight_grads[j] - delta)).astype(bf16)
            key_grads[j].append(dot_plain(score_grad, query) * scale)
            term = dot_first(score_grad, keys[j])
            query_grad = term if query_grad is None else query_grad + term
        query_grads.append((query_grad * scale).astype(bf16))
    query_grad_ref[...] = jnp.concatenate(query_grads, axis=1)
    own_grad_ref[...] = jnp.concatenate(key_grads[0] + value_grads[0], axis=1)
    other_grad_ref[...] = jnp.concatenate(key_grads[1] + value_grads[1], axis=1).astype(bf16)


def attention_back(own, other, label_row, key_label_column, head_gate, lse, upstream, heads):
    rows = own.shape[0]
    cols = own.shape[1] // 3
    return pl.pallas_call(
        functools.partial(attention_back_kernel, heads, cols // heads),
        out_shape=(
            jax.ShapeDtypeStruct((rows, cols), bf16),
            jax.ShapeDtypeStruct((rows, 2 * cols), f32),
            jax.ShapeDtypeStruct((rows, 2 * cols), bf16),
        ),
        compiler_params=pltpu.CompilerParams(vmem_limit_bytes=kernel_vmem),
        cost_estimate=pl.CostEstimate(
            flops=20 * rows * rows * cols,
            bytes_accessed=2 * rows * cols * 12,
            transcendentals=2 * rows * rows * heads,
        ),
        name="attend_back",
    )(own, other, label_row, key_label_column, head_gate, lse, upstream)


def dot(left, right):
    return jnp.dot(left, right, preferred_element_type=f32)


def dot_t(left, right):
    return jnp.einsum("nf,df->nd", left, right, preferred_element_type=f32)


def outer(lefts, rights):
    left = jnp.concatenate(lefts, axis=0)
    right = jnp.concatenate(rights, axis=0)
    return jnp.einsum("nd,nf->df", left, right, preferred_element_type=f32).astype(bf16)


def on_device(
    x_in, cotangent, cond, crop_len, head_mask, skip_mask, ada_w, qkv_w, proj_w, fc1_w, fc2_w
):
    micro, local, width = x_in.shape
    row = skip_mask.shape[1]
    slots = crop_len.shape[1]
    heads = head_mask.shape[2]
    mine = local // 2
    half = mine // 2
    section = lax.axis_index("section")
    tensor_index = lax.axis_index("tensor")
    dp_index = lax.axis_index("dp")
    first_core = section == 0

    def choose(zero, one):
        return jax.tree.map(lambda a, b: jnp.where(first_core, a, b), zero, one)

    def both_blocks(own):
        other = swap_cores(own)
        return (choose(own, other), choose(other, own))

    def to_owner(zero, one):
        own = choose(zero, one)
        other = swap_cores(choose(one, zero))
        return (choose(own, other), choose(other, own))

    hc = qkv_w.shape[3]
    wqkv = both_blocks(jnp.concatenate([qkv_w[0, c] for c in range(3)], axis=1))
    wproj = both_blocks(proj_w[0])
    wup = both_blocks(fc1_w[0])
    wdown = both_blocks(fc2_w[0])

    condition = jax.nn.silu(cond.astype(f32)).astype(bf16)
    flat_condition = condition.reshape(micro * slots, width)
    mod_local = jnp.dot(flat_condition, ada_w[0], preferred_element_type=f32)
    modulation = [
        part.reshape(micro, slots, 6 * width) for part in both_blocks(gather_columns(mod_local))
    ]

    finish = jnp.cumsum(crop_len, axis=1)
    begin = finish - crop_len

    def layout(places):
        inside = (places[None, :, None] >= begin[:, None, :]) & (
            places[None, :, None] < finish[:, None, :]
        )
        flags = inside.astype(jnp.int32)
        labels = jnp.sum(flags * jnp.arange(slots, dtype=jnp.int32)[None, None, :], axis=2)
        labels = labels + (1 - jnp.sum(flags, axis=2)) * slots
        return (inside.astype(f32), labels)

    def starts(core):
        out = []
        for chunk, part in half_order():
            index = tensor_index ^ chunk if square() else chunk
            out.append(index * local + core * mine + part * half)
        return out

    def row_places(core):
        steps = jnp.arange(half, dtype=jnp.int32)
        return jnp.concatenate([start + steps for start in starts(core)])

    my_places = tensor_index * local + section * mine + jnp.arange(mine, dtype=jnp.int32)
    member, unused = layout(my_places)
    row_member, row_labels = layout(row_places(section))
    unused, other_labels = layout(row_places(1 - section))
    key_labels = jnp.concatenate([row_labels, other_labels], axis=1)
    head_gate = jnp.einsum(
        "mns,msh->mnh", row_member, head_mask.astype(f32), precision=highest
    )
    skip = jnp.concatenate(
        [lax.dynamic_slice_in_dim(skip_mask, start, half, 1) for start in starts(section)], axis=1
    ).astype(f32)

    token_mod = [
        [
            jnp.split(jnp.dot(member[i], modulation[b][i], precision=highest), 6, axis=1)
            for i in range(micro)
        ]
        for b in range(2)
    ]

    def forward(b, xs):
        outs, rms, kept = [], [], []
        for i in range(micro):
            shift_one, scale_one, gate_one, shift_two, scale_two, gate_two = token_mod[b][i]
            x = xs[i]
            normed_one, factor_one = normalize_keep(x)
            first = gather_rows((normed_one * (1.0 + scale_one) + shift_one).astype(bf16))
            qkv = dot(first, wqkv[b]).astype(bf16)
            other_kv = swap_cores(qkv[:, hc:])
            mixed, lse = attention_forward(
                qkv, other_kv, row_labels[i][:, None], key_labels[i][None, :], head_gate[i], heads
            )
            attended = scatter_rows(dot(mixed, wproj[b]).astype(bf16))
            middle = x + gate_one * attended
            normed_two, factor_two = normalize_keep(middle)
            second = gather_rows((normed_two * (1.0 + scale_two) + shift_two).astype(bf16))
            pre = dot(second, wup[b])
            hidden = (jax.nn.gelu(pre, approximate=True) * skip[i][:, None]).astype(bf16)
            feed = scatter_rows(dot(hidden, wdown[b]).astype(bf16))
            outs.append(middle + gate_two * feed)
            rms.append(
                jnp.stack(
                    [
                        jnp.sqrt(jnp.mean(attended * attended, axis=1)),
                        jnp.sqrt(jnp.mean(feed * feed, axis=1)),
                    ]
                )
            )
            kept.append((x, first, qkv, other_kv, lse.T, mixed, attended, middle, second, pre, hidden, feed))
        return (outs, jnp.stack(rms, axis=1), kept)

    def backward(b, gs, kept_all):
        grads, mods, pairs = [], [], []
        for i in range(micro):
            x, first, qkv, other_kv, lse, mixed, attended, middle, second, pre, hidden, feed = (
                kept_all[i]
            )
            shift_one, scale_one, gate_one, shift_two, scale_two, gate_two = token_mod[b][i]
            g = gs[i]
            normed_one, factor_one = normalize_keep(x)
            normed_two, factor_two = normalize_keep(middle)
            feed_rows = gather_rows((g * gate_two).astype(bf16))
            unused, activation_back = jax.vjp(
                lambda value: jax.nn.gelu(value, approximate=True) * skip[i][:, None], pre
            )
            pre_grad = activation_back(dot_t(feed_rows, wdown[b]))[0].astype(bf16)
            second_grad = scatter_rows(dot_t(pre_grad, wup[b]).astype(bf16))
            middle_grad = g + normalize_back(
                normed_two, factor_two, second_grad * (1.0 + scale_two)
            )
            attn_rows = gather_rows((middle_grad * gate_one).astype(bf16))
            mixed_grad = dot_t(attn_rows, wproj[b]).astype(bf16)
            query_grad, own_grad, other_grad = attention_back(
                qkv,
                other_kv,
                row_labels[i][None, :],
                key_labels[i][:, None],
                head_gate[i],
                lse,
                mixed_grad,
                heads,
            )
            kv_grad = (own_grad + swap_cores(other_grad).astype(f32)).astype(bf16)
            qkv_grad = jnp.concatenate([query_grad, kv_grad], axis=1)
            first_grad = scatter_rows(dot_t(qkv_grad, wqkv[b]).astype(bf16))
            grads.append(
                middle_grad
                + normalize_back(normed_one, factor_one, first_grad * (1.0 + scale_one))
            )
            token_grad = jnp.concatenate(
                [
                    first_grad,
                    first_grad * normed_one,
                    middle_grad * attended,
                    second_grad,
                    second_grad * normed_two,
                    g * feed,
                ],
                axis=1,
            )
            mods.append(jnp.einsum("ns,ne->se", member[i], token_grad, precision=highest))
            pairs.append((second, pre_grad, feed_rows, hidden, first, qkv_grad, attn_rows, mixed))
        second, pre_grad, feed_rows, hidden, first, qkv_grad, attn_rows, mixed = zip(*pairs)
        up = outer(second, pre_grad)
        down = outer(feed_rows, hidden)
        proj = outer(attn_rows, mixed)
        qkv = outer(first, qkv_grad)

        def reduced(zero, one):
            total = choose(zero, one).astype(f32) + swap_cores(choose(one, zero)).astype(f32)
            return lax.psum_scatter(total.astype(bf16), "dp", scatter_dimension=0, tiled=True)

        wide = reduced(up, down)
        narrow = reduced(qkv[:, : 2 * hc], jnp.concatenate([qkv[:, 2 * hc :], proj], axis=1))
        return (grads, jnp.concatenate(mods, axis=0), (wide, narrow))

    def my_rows(array):
        block = lax.dynamic_slice_in_dim(array, section * mine, mine, 1)
        return [block[i].astype(f32) for i in range(micro)]

    out_zero, rms_zero, kept_zero = forward(0, my_rows(x_in))
    out_one, rms_one, kept_one = forward(1, out_zero)
    back_one, mods_one, weights_one = backward(1, my_rows(cotangent), kept_one)
    back_zero, mods_zero, weights_zero = backward(0, back_one, kept_zero)

    residual = jnp.concatenate(to_owner(jnp.stack(out_zero), jnp.stack(out_one)), axis=1)
    input_grad = jnp.concatenate(
        to_owner(jnp.stack(back_zero).astype(bf16), jnp.stack(back_one).astype(bf16)), axis=1
    )
    sublayer_rms = jnp.concatenate(to_owner(rms_zero, rms_one), axis=2)

    mod_sum = choose(mods_zero, mods_one) + swap_cores(choose(mods_one, mods_zero))
    mod_all = gather_dp(scatter_columns(mod_sum))
    condition_all = gather_dp(flat_condition)
    rows_here = width // lax.axis_size("dp")
    condition_here = lax.dynamic_slice_in_dim(condition_all, dp_index * rows_here, rows_here, 2)
    ada_grad = jnp.einsum(
        "psd,pse->de", condition_here.astype(f32), mod_all, precision=highest
    )

    wide, narrow = (
        to_owner(zero, one) for zero, one in zip(weights_zero, weights_one)
    )
    up_grad = wide[0].astype(f32)
    down_grad = wide[1].astype(f32).T
    qkv_grad = jnp.stack([narrow[0][:, :hc], narrow[0][:, hc:], narrow[1][:, :hc]]).astype(f32)
    proj_grad = narrow[1][:, hc:].astype(f32).T
    return (
        residual[None],
        input_grad[None],
        sublayer_rms[None],
        ada_grad[None],
        qkv_grad[None],
        proj_grad[None],
        up_grad[None],
        down_grad[None],
    )


def solution(mesh):
    in_specs = (
        P(None, ("dp", "tensor"), None),
        P(None, ("dp", "tensor"), None),
        P(None, "dp", None),
        P(None, "dp"),
        P(None, "dp", "tensor"),
        P(None, "dp"),
        P("section", None, "tensor"),
        P("section", None, None, "tensor"),
        P("section", "tensor", None),
        P("section", None, "tensor"),
        P("section", "tensor", None),
    )
    out_specs = (
        P("section", None, ("dp", "tensor"), None),
        P("section", None, ("dp", "tensor"), None),
        P("section", None, None, ("dp", "tensor")),
        P("section", "dp", "tensor"),
        P("section", None, "dp", "tensor"),
        P("section", "tensor", "dp"),
        P("section", "dp", "tensor"),
        P("section", "tensor", "dp"),
    )
    return jax.shard_map(
        on_device, mesh=mesh, in_specs=in_specs, out_specs=out_specs, check_vma=False
    )
```

time: 2940 us -> 1470 us (0.50)
  waiting for transfers between devices: 1740 us -> 609 us
  matrix products: 575 us -> 179 us
  starting transfers between devices: 43 us -> 214 us
  blocking collectives: 123 us -> 0 us
  other arithmetic: 230 us -> 130 us
  Pallas kernels: 0 us -> 78.3 us
  local copies, waits for them, and re-layouts: 163 us -> 229 us
    reduce_scatter x20 -> x2, waiting for transfers between devices: 1150 us -> 44.3 us  [reduced(): lax.psum_scatter(total.astype(bf16), 'dp', scatter_dimension=0, tiled=True)]
    ppermute x8 -> x230, waiting for transfers between devices: 0.02 us -> 565 us  [the longest x98 273 us: along_y(): return lax.ppermute(block, 'tensor', [(0, 2), (2, 0), (1, 3), (3, 1)])]
    all_gather x16 -> x0, waiting for transfers between devices: 532 us -> none  [the longest x4 150 us: backward(): feed_rows = lax.all_gather(feed_grad, 'tensor', axis=0, tiled=True)]
    dot_general x119 -> x71, matrix products: 575 us -> 179 us  [the longest x24 48.1 us: dot_t(): return jnp.einsum('nf,df->nd', left, right, preferred_element_type=f32)]
    ppermute x8 -> x230, starting transfers between devices: 14.7 us -> 214 us  [the longest x99 104 us: along_x(): return lax.ppermute(block, 'tensor', [(0, 1), (1, 0), (2, 3), (3, 2)])]
    unnamed x25 -> x1159, local copies, waits for them, and re-layouts: 33.1 us -> 179 us
    all_gather x1 -> x0, blocking collectives: 123 us -> none  [on_device(): modulation = lax.all_gather(mod_local, 'tensor', axis=2, tiled=True)]
    pallas_call x0 -> x12, Pallas kernels: none -> 78.3 us  [the longest x6 42.9 us: attention_back(): pl.pallas_call(functools.partial(attention_back_kernel, heads, cols // he...]
  transfers between devices with their start and end apart: 46 -> 234, of which waited for: 38 -> 165; matrix products, arithmetic and copies ran while one was open for 11% -> 26% of each run, Pallas kernels for 0% -> 3%
where the time goes in v1:
time: 1470 us; the launch traced here: 1460 us
  waiting for transfers between devices  609 us (41%)
  local copies, waits for them, and re-layouts  229 us (16%)
  starting transfers between devices  214 us (15%)
  matrix products  179 us (12%)
  other arithmetic  130 us (9%)
  Pallas kernels  78.3 us (5%)
  between operations  20.9 us (1%)
    ppermute x98, waiting for transfers between devices, along_y(): return lax.ppermute(block, 'tensor', [(0, 2), (2, 0), (1, 3), (3, 1)])  273 us
    ppermute x99, waiting for transfers between devices, along_x(): return lax.ppermute(block, 'tensor', [(0, 1), (1, 0), (2, 3), (3, 2)])  261 us
    unnamed x1159, local copies, waits for them, and re-layouts  179 us
    ppermute x99, starting transfers between devices, along_x(): return lax.ppermute(block, 'tensor', [(0, 1), (1, 0), (2, 3), (3, 2)])  104 us
    ppermute x98, starting transfers between devices, along_y(): return lax.ppermute(block, 'tensor', [(0, 2), (2, 0), (1, 3), (3, 1)])  98.5 us
    dot_general x24, matrix products, dot_t(): return jnp.einsum('nf,df->nd', left, right, preferred_element_type=f32)  48.1 us
    dot_general x24, matrix products, dot(): return jnp.dot(left, right, preferred_element_type=f32)  46.4 us
    dot_general x8, matrix products, outer(): jnp.einsum('nd,nf->df', left, right, preferred_element_type=f32)  44.6 us
  transfers between devices with their start and end apart: 234, of which 165 were waited for; matrix products, arithmetic and copies ran while one was open for 26% of the time, Pallas kernels for 3%

profile of v1, /device:TPU:0, one launch (start us, length us, event | category | flops | bytes accessed | tf_op | source)
XLA Modules:
  0.0 1461.0 jit_solution(5802468500962871532)
XLA Ops:
  20.6 5.5 collective-permute-done.2
  36.1 8.5 collective-permute-done.42
  45.1 4.8 collective-permute-done.44
  66.8 5.9 attend.8
  77.9 6.9 collective-permute-done.47
  97.5 6.5 collective-permute-done.51
  125.0 4.9 collective-permute-done.55
  136.0 5.0 collective-permute-done.56
  144.1 5.2 collective-permute-done.93
  167.6 5.7 attend.11
  177.3 6.0 collective-permute-done.98
  196.4 10.6 collective-permute-done.102
  253.4 6.2 collective-permute-done.187
  280.4 7.4 attend_back.10
  298.6 7.3 collective-permute-done.192
  320.6 6.0 collective-permute-done.196
  345.3 6.4 collective-permute-done.200
  354.8 4.8 collective-permute-done.203
  364.3 5.6 collective-permute-done.204
  387.9 7.0 attend_back.11
  403.9 7.1 collective-permute-done.209
  426.6 5.5 collective-permute-done.4
  453.8 5.7 attend.6
  462.8 7.2 collective-permute-done.11
  483.0 4.9 collective-permute-done.15
  510.1 6.4 collective-permute-done.21
  529.5 6.0 collective-permute-done.59
  557.2 5.9 attend.9
  566.0 7.2 collective-permute-done.64
  587.6 8.1 collective-permute-done.68
  648.5 5.9 collective-permute-done.119
  680.7 7.0 attend_back.6
  705.2 5.7 collective-permute-done.124
  726.2 4.9 collective-permute-done.128
  753.5 5.8 collective-permute-done.132
  764.8 5.3 collective-permute-done.133
  774.9 5.3 collective-permute-done.136
  798.2 7.4 attend_back.7
  818.4 6.3 collective-permute-done.141
  866.0 5.9 attend.7
  875.6 6.4 collective-permute-done.30
  916.5 5.6 multiply_convert_fusion.4
  927.6 4.8 collective-permute-done.38
  947.8 5.8 collective-permute-done.76
  977.4 6.2 attend.10
  989.2 6.3 collective-permute-done.81
  1048.9 4.9 convolution_convert_fusion.1
  1059.0 9.0 collective-permute-done.149
  1070.5 6.9 collective-permute-done.91
  1080.2 6.6 collective-permute-done.150
  1092.7 5.5 collective-permute-done.153
  1102.7 7.6 broadcast_select_fusion
  1126.2 7.0 attend_back.8
  1173.3 5.3 collective-permute-done.162
  1221.0 5.3 collective-permute-done.170
  1254.2 7.0 attend_back.9
  1277.3 6.4 convolution_convert_fusion.5
  1311.1 8.1 convolution_convert_fusion.3
  1322.9 6.9 collective-permute-done.175
  1331.8 5.0 broadcast_select_fusion.1
  1338.1 5.2 collective-permute-done.176
  1363.9 7.6 collective-permute-done.219
  1386.0 13.0 collective-permute-done.222
  1403.6 44.3 %reduce-scatter.9.cloned.1.call-done = bf16[288,1152]{1,0:T(8,128)(2,1)} async-done(((bf16[1152,1152]{1,0:T(8,128)(2,1)}), bf16[288,1152]{1,0:T(8,128)(2,1)}) %reduce-scatter.9.cloned.1.call-update) | async-done | bytes 663568 | tf_op jit(solution)/shard_map/reduce_scatter | solution.py:446
  (2087 shorter events, 993.5 us)
Async XLA Ops:
  7.2 1355.5 %reduce-scatter.15.cloned.1.call-start = ((), (), s32[]{:S(2)}) async-start(), calls=%async_computation.7 | async-start | bytes 1843200
  15.3 47.6 %collective-permute-start.10 = (bf16[288,1152]{1,0:T(8,128)(2,1)}, bf16[288,1152]{1,0:T(8,128)(2,1)}, u32[]{:S(2)}, u32[]{:S(2)}) collective-permute-start(bf16[288,1152]{1,0:T(8,128)(2,1)} %bitcast.17), channel_id=1, source_target_pairs={{0,16},{16,0},{1,17},{17,1},{2,18},{18,2},{3,19},{19,3},{4,20},{20... | collective-permute-start | bytes 1990664 | tf_op jit(solution)/shard_map/ppermute | solution.py:34
  17.7 38.6 %collective-permute-start.8 = (bf16[1152,864]{0,1:T(8,128)(2,1)}, bf16[1152,864]{0,1:T(8,128)(2,1)}, u32[]{:S(2)}, u32[]{:S(2)}) collective-permute-start(bf16[1152,864]{0,1:T(8,128)(2,1)} %pad_maximum_fusion), channel_id=1, source_target_pairs={{0,16},{16,0},{1,17},{17,1},{2,18},{18,2},{3,19},{19,3},{4,20},{20... | collective-permute-start | bytes 5971976 | tf_op jit(solution)/shard_map/ppermute | solution.py:34
  35.2 9.4 collective-permute-start.43
  75.2 9.6 collective-permute-start.47
  76.7 9.4 collective-permute-start.49
  77.2 27.6 %collective-permute-start.20 = (bf16[1152,1152]{1,0:T(8,128)(2,1)}, bf16[1152,1152]{1,0:T(8,128)(2,1)}, u32[]{:S(2)}, u32[]{:S(2)}) collective-permute-start(bf16[1152,1152]{1,0:T(8,128)(2,1)} %bitcast.20), channel_id=1, source_target_pairs={{0,16},{16,0},{1,17},{17,1},{2,18},{18,2},{3,19},{19,3},{4,20},{20... | collective-permute-start | bytes 7962632 | tf_op jit(solution)/shard_map/ppermute | solution.py:34
  77.2 34.1 %collective-permute-start.19 = (bf16[1152,1152]{1,0:T(8,128)(2,1)}, bf16[1152,1152]{1,0:T(8,128)(2,1)}, u32[]{:S(2)}, u32[]{:S(2)}) collective-permute-start(bf16[1152,1152]{1,0:T(8,128)(2,1)} %bitcast.18), channel_id=1, source_target_pairs={{0,16},{16,0},{1,17},{17,1},{2,18},{18,2},{3,19},{19,3},{4,20},{20... | collective-permute-start | bytes 7962632 | tf_op jit(solution)/shard_map/ppermute | solution.py:34
  192.3 16.6 %collective-permute-start.180 = (bf16[128,1152]{1,0:T(8,128)(2,1)S(1)}, bf16[128,1152]{1,0:T(8,128)(2,1)S(1)}, u32[]{:S(2)}, u32[]{:S(2)}) collective-permute-start(bf16[128,1152]{1,0:T(8,128)(2,1)S(1)} %get-tuple-element.186), channel_id=1, source_target_pairs={{0,4},{4,0},{8,12},{12,8},{1,5},{5,1},{9,13},{13,9},{2,6},{6,2},{1... | collective-permute-start | bytes 884744 | tf_op jit(solution)/shard_map/ppermute | solution.py:38
  193.7 15.2 %collective-permute-start.179 = (bf16[128,1152]{1,0:T(8,128)(2,1)S(1)}, bf16[128,1152]{1,0:T(8,128)(2,1)S(1)}, u32[]{:S(2)}, u32[]{:S(2)}) collective-permute-start(bf16[128,1152]{1,0:T(8,128)(2,1)S(1)} %get-tuple-element.186), channel_id=1, source_target_pairs={{0,8},{8,0},{4,12},{12,4},{1,9},{9,1},{5,13},{13,5},{2,10},{10,2},... | collective-permute-start | bytes 884744 | tf_op jit(solution)/shard_map/ppermute | solution.py:42
  195.4 11.7 collective-permute-start.103
  195.9 11.1 collective-permute-start.102
  227.4 9.8 collective-permute-start.185
  230.8 9.5 collective-permute-start.106
  424.0 9.5 collective-permute-start.5
  527.0 9.9 collective-permute-start.60
  582.1 18.9 %collective-permute-start.112 = (bf16[128,1152]{1,0:T(8,128)(2,1)S(1)}, bf16[128,1152]{1,0:T(8,128)(2,1)S(1)}, u32[]{:S(2)}, u32[]{:S(2)}) collective-permute-start(bf16[128,1152]{1,0:T(8,128)(2,1)S(1)} %get-tuple-element.182), channel_id=1, source_target_pairs={{0,4},{4,0},{8,12},{12,8},{1,5},{5,1},{9,13},{13,9},{2,6},{6,2},{1... | collective-permute-start | bytes 884744 | tf_op jit(solution)/shard_map/ppermute | solution.py:38
  582.9 16.7 %collective-permute-start.111 = (bf16[128,1152]{1,0:T(8,128)(2,1)S(1)}, bf16[128,1152]{1,0:T(8,128)(2,1)S(1)}, u32[]{:S(2)}, u32[]{:S(2)}) collective-permute-start(bf16[128,1152]{1,0:T(8,128)(2,1)S(1)} %get-tuple-element.182), channel_id=1, source_target_pairs={{0,8},{8,0},{4,12},{12,4},{1,9},{9,1},{5,13},{13,5},{2,10},{10,2},... | collective-permute-start | bytes 884744 | tf_op jit(solution)/shard_map/ppermute | solution.py:42
  584.0 13.0 collective-permute-start.69
  584.8 10.9 collective-permute-start.68
  619.5 10.0 collective-permute-start.115
  620.2 9.7 collective-permute-start.117
  623.6 10.9 collective-permute-start.72
  624.4 10.3 collective-permute-start.74
  645.9 9.8 collective-permute-start.120
  658.4 720.7 %collective-permute-start.216 = (bf16[24,1152]{1,0:T(8,128)(2,1)}, bf16[24,1152]{1,0:T(8,128)(2,1)}, u32[]{:S(2)}, u32[]{:S(2)}) collective-permute-start(bf16[24,1152]{1,0:T(8,128)(2,1)} %get-tuple-element.674), channel_id=1, source_target_pairs={{0,2},{1,3},{2,0},{3,1},{4,6},{5,7},{6,4},{7,5},{8,10},{9,11},{10,... | collective-permute-start | bytes 165896 | tf_op jit(solution)/shard_map/ppermute | solution.py:117
  661.1 720.3 %collective-permute-start.215 = (bf16[24,1152]{1,0:T(8,128)(2,1)}, bf16[24,1152]{1,0:T(8,128)(2,1)}, u32[]{:S(2)}, u32[]{:S(2)}) collective-permute-start(bf16[24,1152]{1,0:T(8,128)(2,1)} %get-tuple-element.674), channel_id=1, source_target_pairs={{0,1},{1,2},{2,3},{3,0},{4,5},{5,6},{6,7},{7,4},{8,9},{9,10},{10,1... | collective-permute-start | bytes 165896 | tf_op jit(solution)/shard_map/ppermute | solution.py:117
  701.5 9.4 collective-permute-start.124
  772.1 9.5 collective-permute-start.137
  815.2 9.5 collective-permute-start.141
  836.6 9.4 collective-permute-start.26
  872.8 9.3 collective-permute-start.30
  945.0 10.0 collective-permute-start.77
  986.3 9.2 collective-permute-start.81
  1008.2 10.0 collective-permute-start.146
  1010.3 15.0 %collective-permute-start.86 = (bf16[128,1152]{1,0:T(8,128)(2,1)S(1)}, bf16[128,1152]{1,0:T(8,128)(2,1)S(1)}, u32[]{:S(2)}, u32[]{:S(2)}) collective-permute-start(bf16[128,1152]{1,0:T(8,128)(2,1)S(1)} %get-tuple-element.185), channel_id=1, source_target_pairs={{0,4},{4,0},{8,12},{12,8},{1,5},{5,1},{9,13},{13,9},{2,6},{6,2},{1... | collective-permute-start | bytes 884744 | tf_op jit(solution)/shard_map/ppermute | solution.py:38
  1018.3 9.4 collective-permute-start.147
  1055.7 14.8 %collective-permute-start.89 = (bf16[128,1152]{1,0:T(8,128)(2,1)S(1)}, bf16[128,1152]{1,0:T(8,128)(2,1)S(1)}, u32[]{:S(2)}, u32[]{:S(2)}) collective-permute-start(bf16[128,1152]{1,0:T(8,128)(2,1)S(1)} %get-tuple-element.266), channel_id=1, source_target_pairs={{0,4},{4,0},{8,12},{12,8},{1,5},{5,1},{9,13},{13,9},{2,6},{6,2},{1... | collective-permute-start | bytes 884744 | tf_op jit(solution)/shard_map/ppermute | solution.py:38
  1056.7 11.3 collective-permute-start.149
  1057.9 10.9 collective-permute-start.151
  1068.0 9.4 collective-permute-start.91
  1069.0 11.1 collective-permute-start.152
  1077.6 9.5 collective-permute-start.92
  1077.7 9.5 collective-permute-start.90
  1089.7 9.9 collective-permute-start.154
  1100.9 9.5 collective-permute-start.155
  1110.3 194.4 %collective-permute-start.228 = (bf16[1152,1152]{1,0:T(8,128)(2,1)}, bf16[1152,1152]{1,0:T(8,128)(2,1)}, u32[]{:S(2)}, u32[]{:S(2)}) collective-permute-start(bf16[1152,1152]{1,0:T(8,128)(2,1)} %get-tuple-element.710), channel_id=1, source_target_pairs={{0,16},{16,0},{1,17},{17,1},{2,18},{18,2},{3,19},{19,3},{4,20},{20... | collective-permute-start | bytes 7962632 | tf_op jit(solution)/shard_map/ppermute | solution.py:34
  1135.0 11.4 collective-permute-start.157
  1151.0 9.5 collective-permute-start.158
  1151.7 9.1 collective-permute-start.160
  1206.2 34.8 %collective-permute-start.225 = (bf16[1152,576]{0,1:T(8,128)(2,1)S(1)}, bf16[1152,576]{0,1:T(8,128)(2,1)S(1)}, u32[]{:S(2)}, u32[]{:S(2)}) collective-permute-start(bf16[1152,576]{0,1:T(8,128)(2,1)S(1)} %broadcast_select_fusion.8), channel_id=1, source_target_pairs={{0,16},{16,0},{1,17},{17,1},{2,18},{18,2},{3,19},{19,3},{4,20},{20... | collective-permute-start | bytes 3981320 | tf_op jit(solution)/shard_map/ppermute | solution.py:34
  1239.6 61.1 %collective-permute-start.110 = (f32[3,128,1152]{2,1,0:T(8,128)}, f32[3,128,1152]{2,1,0:T(8,128)}, u32[]{:S(2)}, u32[]{:S(2)}) collective-permute-start(f32[3,128,1152]{2,1,0:T(8,128)} %fusion.86), channel_id=1, source_target_pairs={{0,16},{16,0},{1,17},{17,1},{2,18},{18,2},{3,19},{19,3},{4,20},{20... | collective-permute-start | bytes 5308424 | tf_op jit(solution)/shard_map/ppermute | solution.py:34
  1246.4 155.8 %reduce-scatter.13.cloned.1.call-start = ((), (), s32[]{:S(2)}) async-start(), calls=%async_computation.6 | async-start | bytes 1843200
  1263.0 11.2 collective-permute-start.174
  1284.2 9.6 collective-permute-start.224
  1293.7 87.6 %collective-permute-start.217 = (bf16[24,1152]{1,0:T(8,128)(2,1)}, bf16[24,1152]{1,0:T(8,128)(2,1)}, u32[]{:S(2)}, u32[]{:S(2)}) collective-permute-start(bf16[24,1152]{1,0:T(8,128)(2,1)} %get-tuple-element.674), channel_id=1, source_target_pairs={{0,3},{1,0},{2,1},{3,2},{4,7},{5,4},{6,5},{7,6},{8,11},{9,8},{10,9... | collective-permute-start | bytes 165896 | tf_op jit(solution)/shard_map/ppermute | solution.py:117
  1300.6 103.0 %reduce-scatter.11.cloned.1.call-start = ((), (), s32[]{:S(2)}) async-start(), calls=%async_computation.5 | async-start | bytes 3317760 | tf_op jit(solution)/shard_map/reduce_scatter | solution.py:446
  1310.9 137.0 %reduce-scatter.9.cloned.1.call-start = ((), (), s32[]{:S(2)}) async-start(), calls=%async_computation.4 | async-start | bytes 3317760 | tf_op jit(solution)/shard_map/reduce_scatter | solution.py:446
  1336.8 14.6 %collective-permute-start.227 = (bf16[1152,1152]{1,0:T(8,128)(2,1)S(1)}, bf16[1152,1152]{1,0:T(8,128)(2,1)S(1)}, u32[]{:S(2)}, u32[]{:S(2)}) collective-permute-start(bf16[1152,1152]{1,0:T(8,128)(2,1)S(1)} %get-tuple-element.712), channel_id=1, source_target_pairs={{0,16},{16,0},{1,17},{17,1},{2,18},{18,2},{3,19},{19,3},{4,20},{20... | collective-permute-start | bytes 7962632 | tf_op jit(solution)/shard_map/ppermute | solution.py:34
  1358.7 13.8 collective-permute-start.213
  1360.8 10.7 collective-permute-start.219
  1378.4 20.6 %collective-permute-start.222 = (f32[24,1728]{1,0:T(8,128)S(1)}, f32[24,1728]{1,0:T(8,128)S(1)}, u32[]{:S(2)}, u32[]{:S(2)}) collective-permute-start(f32[24,1728]{1,0:T(8,128)S(1)} %fusion.213), channel_id=1, source_target_pairs={{0,2},{1,3},{2,0},{3,1},{4,6},{5,7},{6,4},{7,5},{8,10},{9,11},{10,... | collective-permute-start | bytes 497672 | tf_op jit(solution)/shard_map/ppermute | solution.py:117
  1379.1 19.9 %collective-permute-start.221 = (f32[24,1728]{1,0:T(8,128)S(1)}, f32[24,1728]{1,0:T(8,128)S(1)}, u32[]{:S(2)}, u32[]{:S(2)}) collective-permute-start(f32[24,1728]{1,0:T(8,128)S(1)} %fusion.213), channel_id=1, source_target_pairs={{0,1},{1,2},{2,3},{3,0},{4,5},{5,6},{6,7},{7,4},{8,9},{9,10},{10,1... | collective-permute-start | bytes 497672 | tf_op jit(solution)/shard_map/ppermute | solution.py:117
  1403.5 46.4 %collective-permute-start.226 = (bf16[288,576]{0,1:T(8,128)(2,1)S(1)}, bf16[288,576]{0,1:T(8,128)(2,1)S(1)}, u32[]{:S(2)}, u32[]{:S(2)}) collective-permute-start(bf16[288,576]{0,1:T(8,128)(2,1)S(1)} %broadcast_select_fusion.22), channel_id=1, source_target_pairs={{0,16},{16,0},{1,17},{17,1},{2,18},{18,2},{3,19},{19,3},{4,20},{20... | collective-permute-start | bytes 995336 | tf_op jit(solution)/shard_map/ppermute | solution.py:34
  (635 other events, 5504.0 us)
Sparse Core Ops, SparseCore 0:
  1246.5 32.4 reduce-scatter.14
  1300.7 30.7 reduce-scatter.12
  1333.8 56.1 reduce-scatter.10
  1392.1 55.6 reduce-scatter.8

commit v2 on v1

v2 whole, which is shorter than its diff:
```python
import functools
import math

import jax
import jax.numpy as jnp
from jax import lax
from jax.experimental import pallas as pl
from jax.experimental.pallas import tpu as pltpu
from jax.sharding import PartitionSpec as P

highest = lax.Precision.HIGHEST
epsilon = 1e-06
f32 = jnp.float32
bf16 = jnp.bfloat16
log2e = math.log2(math.e)


def normalize_keep(value):
    centered = value - jnp.mean(value, axis=-1, keepdims=True)
    factor = lax.rsqrt(jnp.mean(centered * centered, axis=-1, keepdims=True) + epsilon)
    return (centered * factor, factor)


def normalize_back(normed, factor, upstream):
    return factor * (
        upstream
        - jnp.mean(upstream, axis=-1, keepdims=True)
        - normed * jnp.mean(upstream * normed, axis=-1, keepdims=True)
    )


def swap_cores(block):
    return lax.ppermute(block, "section", [(0, 1), (1, 0)])


def along_x(block):
    return lax.ppermute(block, "tensor", [(0, 1), (1, 0), (2, 3), (3, 2)])


def along_y(block):
    return lax.ppermute(block, "tensor", [(0, 2), (2, 0), (1, 3), (3, 1)])


def square():
    return lax.axis_size("tensor") == 4


def axes_of(stream):
    return ((along_x, 1), (along_y, 2)) if stream % 2 == 0 else ((along_y, 2), (along_x, 1))


def chunk_order(stream):
    if square():
        (unused, near), (unused, far) = axes_of(stream)
        return [0, far, near, 3]
    return range(lax.axis_size("tensor"))


def gather_start(block, stream):
    if not square():
        return (lax.all_gather(block, "tensor", axis=0, tiled=True),)
    (along, unused), (across, unused) = axes_of(stream)
    from_near = along(block)
    return (block, from_near, across(jnp.concatenate([block, from_near], axis=0)))


def assemble(pieces, target):
    if len(pieces) == 1:
        target[...] = pieces[0][...]
        return
    own, near, far = pieces
    mine = own.shape[0]
    target[:mine, :] = own[...]
    target[mine : 2 * mine, :] = far[:mine, :]
    target[2 * mine : 3 * mine, :] = near[...]
    target[3 * mine :, :] = far[mine:, :]


def partial_shapes(rows, width):
    parts = 2 if square() else 1
    return [jax.ShapeDtypeStruct((rows // parts, width), bf16)] * parts


def store_partial(refs, columns, value):
    begin = 0
    for ref in refs:
        rows = ref.shape[0]
        ref[:, columns] = value[begin : begin + rows].astype(bf16)
        begin += rows


def add_first_kernel(keep, arrived, own, send):
    mine = own.shape[0]
    own[...] = keep[:mine, :].astype(f32) + arrived[:mine, :].astype(f32)
    send[...] = (keep[mine:, :].astype(f32) + arrived[mine:, :].astype(f32)).astype(bf16)


def scatter_start(parts, stream):
    if not square():
        return (lax.psum_scatter(parts[0], "tensor", scatter_dimension=0, tiled=True),)
    (along, unused), (across, unused) = axes_of(stream)
    keep, leave = parts
    rows, width = keep.shape
    own, send = run(
        add_first_kernel,
        [
            jax.ShapeDtypeStruct((rows // 2, width), f32),
            jax.ShapeDtypeStruct((rows // 2, width), bf16),
        ],
        keep,
        along(leave),
        name="add_first",
        vmem=4,
    )
    return (own, across(send))


def scattered(pieces):
    total = pieces[0][...].astype(f32)
    for piece in pieces[1:]:
        total = total + piece[...].astype(f32)
    return total


def gather_columns(block):
    if not square():
        return lax.all_gather(block, "tensor", axis=1, tiled=True)
    from_x = along_x(block)
    from_y = along_y(block)
    pieces = jnp.stack([block, from_x, from_y, along_x(from_y)])
    here = lax.axis_index("tensor")
    return jnp.concatenate(
        [lax.dynamic_index_in_dim(pieces, here ^ j, 0, keepdims=False) for j in range(4)], axis=1
    )


def scatter_columns(partial):
    if not square():
        return lax.psum_scatter(partial, "tensor", scatter_dimension=1, tiled=True)
    here = lax.axis_index("tensor")
    columns = partial.shape[1] // 4

    def piece(distance):
        return lax.dynamic_slice_in_dim(partial, (here ^ distance) * columns, columns, 1)

    arrived = along_x(jnp.stack([piece(1), piece(3)]))
    return piece(0) + arrived[0] + along_y(piece(2) + arrived[1])


def gather_dp(block):
    size = lax.axis_size("dp")
    others = [
        lax.ppermute(block, "dp", [(i, (i + step) % size) for i in range(size)])
        for step in range(1, size)
    ]
    return jnp.stack([block] + others)


def dot_last(left, right):
    return lax.dot_general(left, right, (((1,), (1,)), ((), ())), preferred_element_type=f32)


def dot_plain(left, right):
    return lax.dot_general(left, right, (((1,), (0,)), ((), ())), preferred_element_type=f32)


def dot_first(left, right):
    return lax.dot_general(left, right, (((0,), (0,)), ((), ())), preferred_element_type=f32)


def chunks(size, most=384):
    step = most if size % most == 0 else size
    return [slice(begin, begin + step) for begin in range(0, size, step)]


def run(kernel, shapes, *arrays, name, vmem, flops=0, exps=0):
    return pl.pallas_call(
        kernel,
        out_shape=tuple(shapes),
        compiler_params=pltpu.CompilerParams(vmem_limit_bytes=vmem * 1024 * 1024),
        cost_estimate=pl.CostEstimate(
            flops=flops,
            bytes_accessed=sum(x.size * x.dtype.itemsize for x in (*arrays, *shapes)),
            transcendentals=exps,
        ),
        name=name,
    )(*arrays)


def block_mod(member, mod, index):
    width = mod.shape[1] // 6
    return dot_plain(member[...], mod[:, index * width : (index + 1) * width])


def slot_sums(member_t, value):
    high = value.astype(bf16)
    low = (value - high.astype(f32)).astype(bf16)
    return dot_plain(member_t[...], high) + dot_plain(member_t[...], low)


def root_mean(value):
    return jnp.sqrt(jnp.mean(value * value, axis=1, keepdims=True))


def first_kernel(x, member, mod, out):
    normed, unused = normalize_keep(x[...])
    out[...] = (normed * (1.0 + block_mod(member, mod, 1)) + block_mod(member, mod, 0)).astype(bf16)


def upstream_kernel(g, member, mod, out):
    out[...] = (g[...] * block_mod(member, mod, 5)).astype(bf16)


def column(row):
    return columns_of(row)[:, :1]


def columns_of(rows):
    count, size = rows.shape
    if count < 8:
        rows = jnp.concatenate([rows, jnp.zeros((8 - count, size), f32)], axis=0)
    return jnp.transpose(rows)


def rows_of(columns):
    size = columns[0].shape[0]
    blank = jnp.zeros((size, 128 - len(columns)), f32)
    return jnp.transpose(jnp.concatenate([*columns, blank], axis=1))[: len(columns), :]


def qkv_kernel(count, *refs):
    pieces, (weight, rows, query, keyvalue) = refs[:count], refs[count:]
    assemble(pieces, rows)
    size, cols = query.shape
    out = dot_last(rows[...], weight[...]).astype(bf16)
    query[...] = out[:, :cols]
    keyvalue[:, : 2 * cols] = out[:, cols:]
    keyvalue[:, 2 * cols :] = jnp.zeros((size, keyvalue.shape[1] - 2 * cols), bf16)


def attention_forward_kernel(
    heads, query_ref, own_ref, other_ref, label_ref, gate_ref, weight_ref, mixed_ref, lse_ref, *parts
):
    rows, cols = query_ref.shape
    dim = cols // heads
    scale = dim ** (-0.5)
    labels = column(label_ref[:, :rows])
    gates = columns_of(gate_ref[...])
    same = [labels == label_ref[:, :rows], labels == label_ref[:, rows:]]
    mixed = []
    totals = []
    for head in range(heads):
        part = slice(head * dim, (head + 1) * dim)
        value_part = slice(cols + head * dim, cols + (head + 1) * dim)
        query = query_ref[:, part]
        keys = [own_ref[:, part], other_ref[:, part]]
        values = [own_ref[:, value_part], other_ref[:, value_part]]
        scores = [jnp.where(same[j], dot_last(query, keys[j]), -1e30) for j in range(2)]
        peak = jnp.maximum(
            jnp.max(scores[0], axis=1, keepdims=True), jnp.max(scores[1], axis=1, keepdims=True)
        )
        expos = [jnp.exp2((scores[j] - peak) * (scale * log2e)) for j in range(2)]
        total = jnp.sum(expos[0], axis=1, keepdims=True) + jnp.sum(expos[1], axis=1, keepdims=True)
        inverse = 1.0 / total
        out = dot_plain((expos[0] * inverse).astype(bf16), values[0])
        out = out + dot_plain((expos[1] * inverse).astype(bf16), values[1])
        mixed.append((out * gates[:, head : head + 1]).astype(bf16))
        totals.append(peak * scale + jnp.log(total))
    mixed_ref[...] = jnp.concatenate(mixed, axis=1)
    lse_ref[...] = rows_of(totals)
    for columns in chunks(weight_ref.shape[1]):
        store_partial(parts, columns, dot_plain(mixed_ref[...], weight_ref[:, columns]))


def after_attention_kernel(count, *refs):
    pieces = refs[:count]
    x, member, mod, attended_out, middle_out, second_out, rms_out = refs[count:]
    attended = scattered(pieces)
    middle = x[...] + block_mod(member, mod, 2) * attended
    normed, unused = normalize_keep(middle)
    attended_out[...] = attended
    middle_out[...] = middle
    rms_out[...] = root_mean(attended)
    second_out[...] = (
        normed * (1.0 + block_mod(member, mod, 4)) + block_mod(member, mod, 3)
    ).astype(bf16)


def feed_kernel(count, *refs):
    pieces = refs[:count]
    up, down, skip, rows, hidden, slope, *parts = refs[count:]
    assemble(pieces, rows)
    inner = math.sqrt(2 / math.pi)
    half_skip = 0.5 * column(skip[...])
    for columns in chunks(up.shape[1]):
        pre = dot_plain(rows[...], up[:, columns])
        square_pre = pre * pre
        tanh = jnp.tanh(inner * pre * (1.0 + 0.044715 * square_pre))
        half_gate = half_skip * (1.0 + tanh)
        hidden[:, columns] = (pre * half_gate).astype(bf16)
        slope[:, columns] = (
            half_gate * (1.0 + pre * (1.0 - tanh) * (inner * (1.0 + 3 * 0.044715 * square_pre)))
        ).astype(bf16)
    for columns in chunks(down.shape[1]):
        store_partial(parts, columns, dot_plain(hidden[...], down[:, columns]))


def after_feed_kernel(count, last, *refs):
    pieces = refs[:count]
    middle, member, mod, *rest = refs[count:]
    feed = scattered(pieces)
    out = middle[...] + block_mod(member, mod, 5) * feed
    if last:
        feed_out, x_out, rms_out = rest
    else:
        next_mod, feed_out, x_out, rms_out, first_out = rest
        first_kernel(out, member, next_mod, first_out)
    feed_out[...] = feed
    x_out[...] = out
    rms_out[...] = root_mean(feed)


def feed_back_kernel(count, *refs):
    pieces = refs[:count]
    up, down, slope, rows, pre_grad, *parts = refs[count:]
    assemble(pieces, rows)
    for columns in chunks(up.shape[1]):
        hidden_grad = dot_last(rows[...], down[columns, :])
        pre_grad[:, columns] = (hidden_grad * slope[:, columns].astype(f32)).astype(bf16)
    for columns in chunks(up.shape[0]):
        store_partial(parts, columns, dot_last(pre_grad[...], up[columns, :]))


def after_feed_back_kernel(count, *refs):
    pieces = refs[:count]
    middle, g, attended, feed, member, member_t, mod, grad_out, attn_out, sums = refs[count:]
    width = middle.shape[1]
    second_grad = scattered(pieces)
    normed, factor = normalize_keep(middle[...])
    middle_grad = g[...] + normalize_back(
        normed, factor, second_grad * (1.0 + block_mod(member, mod, 4))
    )
    grad_out[...] = middle_grad
    attn_out[...] = (middle_grad * block_mod(member, mod, 2)).astype(bf16)
    sums[:, :width] = slot_sums(member_t, middle_grad * attended[...])
    sums[:, width : 2 * width] = slot_sums(member_t, second_grad)
    sums[:, 2 * width : 3 * width] = slot_sums(member_t, second_grad * normed)
    sums[:, 3 * width :] = slot_sums(member_t, g[...] * feed[...])


def attention_back_kernel(count, heads, *refs):
    pieces = refs[:count]
    (
        weight_ref,
        query_ref,
        own_ref,
        other_ref,
        label_ref,
        gate_ref,
        lse_ref,
        upstream_rows,
        query_grad_ref,
        own_grad_ref,
        other_grad_ref,
    ) = refs[count:]
    assemble(pieces, upstream_rows)
    rows, cols = query_ref.shape
    dim = cols // heads
    scale = dim ** (-0.5)
    labels = label_ref[:, :rows]
    gates = columns_of(gate_ref[...])
    mixed_grad = dot_last(upstream_rows[...], weight_ref[...]).astype(bf16).astype(f32)
    same = [column(labels) == labels, column(label_ref[:, rows:]) == labels]
    query_grads = []
    key_grads = [[], []]
    value_grads = [[], []]
    for head in range(heads):
        part = slice(head * dim, (head + 1) * dim)
        value_part = slice(cols + head * dim, cols + (head + 1) * dim)
        query = query_ref[:, part]
        keys = [own_ref[:, part], other_ref[:, part]]
        values = [own_ref[:, value_part], other_ref[:, value_part]]
        upstream = (mixed_grad[:, part] * gates[:, head : head + 1]).astype(bf16)
        lse = lse_ref[head : head + 1, :] * log2e
        weights = []
        weight_grads = []
        for j in range(2):
            scores = jnp.where(same[j], dot_last(keys[j], query) * (scale * log2e), -1e30)
            weights.append(jnp.exp2(scores - lse))
            weight_grads.append(dot_last(values[j], upstream))
            value_grads[j].append(dot_plain(weights[j].astype(bf16), upstream))
        delta = jnp.sum(weights[0] * weight_grads[0], axis=0, keepdims=True)
        delta = delta + jnp.sum(weights[1] * weight_grads[1], axis=0, keepdims=True)
        query_grad = None
        for j in range(2):
            score_grad = (weights[j] * (weight_grads[j] - delta)).astype(bf16)
            key_grads[j].append(dot_plain(score_grad, query) * scale)
            term = dot_first(score_grad, keys[j])
            query_grad = term if query_grad is None else query_grad + term
        query_grads.append((query_grad * scale).astype(bf16))
    query_grad_ref[...] = jnp.concatenate(query_grads, axis=1)
    own_grad_ref[...] = jnp.concatenate(key_grads[0] + value_grads[0], axis=1)
    other_grad_ref[:, : 2 * cols] = jnp.concatenate(
        key_grads[1] + value_grads[1], axis=1
    ).astype(bf16)
    other_grad_ref[:, 2 * cols :] = jnp.zeros((rows, other_grad_ref.shape[1] - 2 * cols), bf16)


def qkv_back_kernel(query_grad, own_grad, arrived, weight, grad, *parts):
    cols = own_grad.shape[1]
    total = own_grad[...] + arrived[:, :cols].astype(f32)
    grad[...] = jnp.concatenate([query_grad[...], total.astype(bf16)], axis=1)
    for columns in chunks(weight.shape[1]):
        store_partial(parts, columns, dot_plain(grad[...], weight[:, columns]))


def after_attention_back_kernel(count, last, *refs):
    pieces = refs[:count]
    x, middle_grad, member, member_t, mod, *rest = refs[count:]
    width = x.shape[1]
    first_grad = scattered(pieces)
    normed, factor = normalize_keep(x[...])
    out = middle_grad[...] + normalize_back(
        normed, factor, first_grad * (1.0 + block_mod(member, mod, 1))
    )
    if last:
        grad_out, sums = rest
    else:
        next_mod, grad_out, sums, feed_out = rest
        upstream_kernel(out, member, next_mod, feed_out)
    grad_out[...] = out
    sums[:, :width] = slot_sums(member_t, first_grad)
    sums[:, width:] = slot_sums(member_t, first_grad * normed)


def outer(lefts, rights):
    left = jnp.concatenate(lefts, axis=0)
    right = jnp.concatenate(rights, axis=0)
    return jnp.einsum("nd,nf->df", left, right, preferred_element_type=f32).astype(bf16)


def three_terms(value):
    high = lax.reduce_precision(value, 8, 7)
    rest = value - high
    low = lax.reduce_precision(rest, 8, 7)
    return jnp.concatenate([high, low, rest - low], axis=0).astype(bf16)


def on_device(
    x_in, cotangent, cond, crop_len, head_mask, skip_mask, ada_w, qkv_w, proj_w, fc1_w, fc2_w
):
    micro, local, width = x_in.shape
    row = skip_mask.shape[1]
    slots = crop_len.shape[1]
    heads = head_mask.shape[2]
    mine = local // 2
    section = lax.axis_index("section")
    tensor_index = lax.axis_index("tensor")
    dp_index = lax.axis_index("dp")
    first_core = section == 0

    def choose(zero, one):
        return jax.tree.map(lambda a, b: jnp.where(first_core, a, b), zero, one)

    def both_blocks(own):
        other = swap_cores(own)
        return (choose(own, other), choose(other, own))

    def to_owner(zero, one):
        own = choose(zero, one)
        other = swap_cores(choose(one, zero))
        return (choose(own, other), choose(other, own))

    hc = qkv_w.shape[3]
    wqkv = both_blocks(jnp.transpose(qkv_w[0], (0, 2, 1)).reshape(3 * hc, width))
    wproj = both_blocks(proj_w[0])
    wup = both_blocks(fc1_w[0])
    wdown = both_blocks(fc2_w[0])

    condition = jax.nn.silu(cond.astype(f32)).astype(bf16)
    flat_condition = condition.reshape(micro * slots, width)
    mod_local = jnp.dot(flat_condition, ada_w[0], preferred_element_type=f32)
    modulation = both_blocks(gather_columns(mod_local))
    mod = [
        [three_terms(modulation[b][i * slots : (i + 1) * slots]) for i in range(micro)]
        for b in range(2)
    ]

    finish = jnp.cumsum(crop_len, axis=1)
    begin = finish - crop_len

    def layout(places):
        inside = (places[:, :, None] >= begin[:, None, :]) & (
            places[:, :, None] < finish[:, None, :]
        )
        flags = inside.astype(jnp.int32)
        labels = jnp.sum(flags * jnp.arange(slots, dtype=jnp.int32)[None, None, :], axis=2)
        labels = labels + (1 - jnp.sum(flags, axis=2)) * slots
        return (inside.astype(f32), labels.astype(f32))

    def starts(core, stream):
        return [
            (tensor_index ^ chunk if square() else chunk) * local + core * mine
            for chunk in chunk_order(stream)
        ]

    steps = jnp.arange(mine, dtype=jnp.int32)

    def row_places(core):
        return jnp.stack(
            [
                jnp.concatenate([start + steps for start in starts(core, i)])
                for i in range(micro)
            ]
        )

    my_places = tensor_index * local + section * mine + steps
    member, unused = layout(my_places[None, :])
    row_member, row_labels = layout(row_places(section))
    unused, other_labels = layout(row_places(1 - section))
    key_labels = jnp.concatenate([row_labels, other_labels], axis=1)
    head_gate = jnp.einsum("mns,msh->mhn", row_member, head_mask.astype(f32), precision=highest)
    skip = jnp.stack(
        [
            jnp.concatenate(
                [
                    lax.dynamic_slice_in_dim(skip_mask[i], start, mine, 0)
                    for start in starts(section, i)
                ]
            )
            for i in range(micro)
        ]
    ).astype(f32)

    members = jnp.concatenate([member] * 3, axis=2).astype(bf16)
    members_t = jnp.transpose(member, (0, 2, 1)).astype(bf16)
    row_count = row_labels.shape[1]
    padded = -(-2 * hc // 128) * 128
    hidden_cols = fc1_w.shape[2]

    def shape(rows, cols, kind):
        return jax.ShapeDtypeStruct((rows, cols), kind)

    latest = [None]

    def after(arrays):
        if latest[0] is None:
            return arrays
        return lax.optimization_barrier((arrays, latest[0]))[0]

    def ends(array):
        latest[0] = array

    def stream(i, x, g, results):
        of_mine = shape(mine, width, f32)
        low_mine = shape(mine, width, bf16)
        low_rows = shape(row_count, width, bf16)
        column = shape(mine, 1, f32)
        terms = partial_shapes(row_count, width)
        tokens, tokens_t = members[i], members_t[i]
        kept = []
        (first_mine,) = run(first_kernel, [low_mine], x, tokens, mod[0][i], name="first", vmem=4)
        ends(first_mine)
        for b in range(2):
            pieces = gather_start(first_mine, i)
            yield
            pieces = after(pieces)
            first, query, keyvalue = run(
                functools.partial(qkv_kernel, len(pieces)),
                [low_rows, shape(row_count, hc, bf16), shape(row_count, padded, bf16)],
                *pieces,
                wqkv[b],
                name="qkv", vmem=8,
                flops=6 * row_count * width * hc,
            )
            other = swap_cores(keyvalue)
            mixed, lse, *parts = run(
                functools.partial(attention_forward_kernel, heads),
                [shape(row_count, hc, bf16), shape(heads, row_count, f32), *terms],
                query,
                keyvalue,
                other,
                key_labels[i][None, :],
                head_gate[i],
                wproj[b],
                name="attend", vmem=24,
                flops=8 * row_count * row_count * hc + 2 * row_count * hc * width,
                exps=2 * row_count * row_count * heads,
            )
            ends(mixed)
            pieces = scatter_start(parts, i)
            yield
            pieces = after(pieces)
            attended, middle, second_mine, rms_attended = run(
                functools.partial(after_attention_kernel, len(pieces)),
                [of_mine, of_mine, low_mine, column],
                *pieces,
                x,
                tokens,
                mod[b][i],
                name="after_attend", vmem=6,
            )
            ends(second_mine)
            pieces = gather_start(second_mine, i)
            yield
            pieces = after(pieces)
            second, hidden, slope, *parts = run(
                functools.partial(feed_kernel, len(pieces)),
                [
                    low_rows,
                    shape(row_count, hidden_cols, bf16),
                    shape(row_count, hidden_cols, bf16),
                    *terms,
                ],
                *pieces,
                wup[b],
                wdown[b],
                skip[i][None, :],
                name="feed", vmem=12,
                flops=4 * row_count * width * hidden_cols,
                exps=row_count * hidden_cols,
            )
            ends(hidden)
            pieces = scatter_start(parts, i)
            yield
            pieces = after(pieces)
            x_in_block = x
            if b == 0:
                feed, x, rms_feed, first_mine = run(
                    functools.partial(after_feed_kernel, len(pieces), False),
                    [of_mine, of_mine, column, low_mine],
                    *pieces,
                    middle,
                    tokens,
                    mod[b][i],
                    mod[1][i],
                    name="after_feed", vmem=6,
                )
            else:
                feed, x, rms_feed = run(
                    functools.partial(after_feed_kernel, len(pieces), True),
                    [of_mine, of_mine, column],
                    *pieces,
                    middle,
                    tokens,
                    mod[b][i],
                    name="after_feed", vmem=6,
                )
            ends(x)
            kept.append(
                (x_in_block, first, query, keyvalue, other, lse, mixed, attended, middle)
                + (second, hidden, slope, feed)
            )
            results["out", b, i] = x
            results["rms", b, i] = (rms_attended, rms_feed)
        (feed_mine,) = run(upstream_kernel, [low_mine], g, tokens, mod[1][i], name="upstream", vmem=4)
        ends(feed_mine)
        for b in (1, 0):
            x, first, query, keyvalue, other, lse, mixed, attended, middle = kept[b][:9]
            second, hidden, slope, feed = kept[b][9:]
            pieces = gather_start(feed_mine, i)
            yield
            pieces = after(pieces)
            feed_rows, pre_grad, *parts = run(
                functools.partial(feed_back_kernel, len(pieces)),
                [low_rows, shape(row_count, hidden_cols, bf16), *terms],
                *pieces,
                wup[b],
                wdown[b],
                slope,
                name="feed_back", vmem=12,
                flops=4 * row_count * width * hidden_cols,
            )
            ends(pre_grad)
            pieces = scatter_start(parts, i)
            yield
            pieces = after(pieces)
            middle_grad, attn_mine, sums_two = run(
                functools.partial(after_feed_back_kernel, len(pieces)),
                [of_mine, low_mine, shape(slots, 4 * width, f32)],
                *pieces,
                middle,
                g,
                attended,
                feed,
                tokens,
                tokens_t,
                mod[b][i],
                name="after_feed_back", vmem=8,
            )
            ends(attn_mine)
            pieces = gather_start(attn_mine, i)
            yield
            pieces = after(pieces)
            attn_rows, query_grad, own_grad, other_grad = run(
                functools.partial(attention_back_kernel, len(pieces), heads),
                [
                    low_rows,
                    shape(row_count, hc, bf16),
                    shape(row_count, 2 * hc, f32),
                    shape(row_count, padded, bf16),
                ],
                *pieces,
                wproj[b],
                query,
                keyvalue,
                other,
                key_labels[i][None, :],
                head_gate[i],
                lse,
                name="attend_back", vmem=32,
                flops=20 * row_count * row_count * hc + 2 * row_count * hc * width,
                exps=2 * row_count * row_count * heads,
            )
            qkv_grad, *parts = run(
                qkv_back_kernel,
                [shape(row_count, 3 * hc, bf16), *terms],
                query_grad,
                own_grad,
                swap_cores(other_grad),
                wqkv[b],
                name="qkv_back", vmem=8,
                flops=6 * row_count * width * hc,
            )
            ends(qkv_grad)
            pieces = scatter_start(parts, i)
            yield
            pieces = after(pieces)
            if b == 1:
                g, sums_one, feed_mine = run(
                    functools.partial(after_attention_back_kernel, len(pieces), False),
                    [of_mine, shape(slots, 2 * width, f32), low_mine],
                    *pieces,
                    x,
                    middle_grad,
                    tokens,
                    tokens_t,
                    mod[b][i],
                    mod[0][i],
                    name="after_attend_back", vmem=8,
                )
            else:
                g, sums_one = run(
                    functools.partial(after_attention_back_kernel, len(pieces), True),
                    [of_mine, shape(slots, 2 * width, f32)],
                    *pieces,
                    x,
                    middle_grad,
                    tokens,
                    tokens_t,
                    mod[b][i],
                    name="after_attend_back", vmem=8,
                )
            ends(g)
            results["grad", b, i] = g
            results["mod", b, i] = jnp.concatenate([sums_one, sums_two], axis=1)
            results["pairs", b, i] = (
                second, pre_grad, feed_rows, hidden, first, qkv_grad, attn_rows, mixed
            )

    def weight_sums(b):
        second, pre_grad, feed_rows, hidden, first, qkv_grad, attn_rows, mixed = zip(
            *(results["pairs", b, i] for i in range(micro))
        )
        up = outer(second, pre_grad)
        down = outer(feed_rows, hidden)
        proj = outer(attn_rows, mixed)
        qkv = outer(first, qkv_grad)

        def reduced(zero, one):
            total = choose(zero, one).astype(f32) + swap_cores(choose(one, zero)).astype(f32)
            return lax.psum_scatter(total.astype(bf16), "dp", scatter_dimension=0, tiled=True)

        wide = reduced(up, down)
        fill = ((0, 0), (0, padded - 2 * hc))
        narrow = reduced(
            jnp.pad(qkv[:, : 2 * hc], fill),
            jnp.pad(jnp.concatenate([qkv[:, 2 * hc :], proj], axis=1), fill),
        )
        return (wide, narrow)

    def my_rows(array):
        block = lax.dynamic_slice_in_dim(array, section * mine, mine, 1)
        return [block[i].astype(f32) for i in range(micro)]

    results = {}
    xs = my_rows(x_in)
    gs = my_rows(cotangent)
    running = [stream(i, xs[i], gs[i], results) for i in range(micro)]
    while running:
        running = [s for s in running if next(s, "ended") != "ended"]

    def collected(name, b):
        return [results[name, b, i] for i in range(micro)]

    out_zero, out_one = collected("out", 0), collected("out", 1)
    back_zero, back_one = collected("grad", 0), collected("grad", 1)
    rms_zero, rms_one = (
        jnp.concatenate([column for pair in collected("rms", b) for column in pair], axis=1)
        .T.reshape(micro, 2, mine)
        .transpose(1, 0, 2)
        for b in range(2)
    )
    mods_zero, mods_one = (jnp.concatenate(collected("mod", b), axis=0) for b in range(2))
    weights_one = weight_sums(1)
    weights_zero = weight_sums(0)

    residual = jnp.concatenate(to_owner(jnp.stack(out_zero), jnp.stack(out_one)), axis=1)
    input_grad = jnp.concatenate(
        to_owner(jnp.stack(back_zero).astype(bf16), jnp.stack(back_one).astype(bf16)), axis=1
    )
    sublayer_rms = jnp.concatenate(to_owner(rms_zero, rms_one), axis=2)

    mod_sum = choose(mods_zero, mods_one) + swap_cores(choose(mods_one, mods_zero))
    mod_all = gather_dp(scatter_columns(mod_sum))
    condition_all = gather_dp(flat_condition)
    rows_here = width // lax.axis_size("dp")
    condition_here = lax.dynamic_slice_in_dim(condition_all, dp_index * rows_here, rows_here, 2)
    ada_grad = jnp.einsum(
        "psd,pse->de", condition_here.astype(f32), mod_all, precision=highest
    )

    wide, narrow = (
        to_owner(zero, one) for zero, one in zip(weights_zero, weights_one)
    )
    up_grad = wide[0].astype(f32)
    down_grad = wide[1].astype(f32).T
    qkv_grad = jnp.stack([narrow[0][:, :hc], narrow[0][:, hc : 2 * hc], narrow[1][:, :hc]]).astype(f32)
    proj_grad = narrow[1][:, hc : 2 * hc].astype(f32).T
    return (
        residual[None],
        input_grad[None],
        sublayer_rms[None],
        ada_grad[None],
        qkv_grad[None],
        proj_grad[None],
        up_grad[None],
        down_grad[None],
    )


def solution(mesh):
    in_specs = (
        P(None, ("dp", "tensor"), None),
        P(None, ("dp", "tensor"), None),
        P(None, "dp", None),
        P(None, "dp"),
        P(None, "dp", "tensor"),
        P(None, "dp"),
        P("section", None, "tensor"),
        P("section", None, None, "tensor"),
        P("section", "tensor", None),
        P("section", None, "tensor"),
        P("section", "tensor", None),
    )
    out_specs = (
        P("section", None, ("dp", "tensor"), None),
        P("section", None, ("dp", "tensor"), None),
        P("section", None, None, ("dp", "tensor")),
        P("section", "dp", "tensor"),
        P("section", None, "dp", "tensor"),
        P("section", "tensor", "dp"),
        P("section", "dp", "tensor"),
        P("section", "tensor", "dp"),
    )
    return jax.shard_map(
        on_device, mesh=mesh, in_specs=in_specs, out_specs=out_specs, check_vma=False
    )
```

time: 1470 us -> 974 us (0.66)
  waiting for transfers between devices: 609 us -> 438 us
  local copies, waits for them, and re-layouts: 229 us -> 73.4 us
  matrix products: 179 us -> 47.9 us
  Pallas kernels: 78.3 us -> 207 us
  starting transfers between devices: 214 us -> 120 us
  other arithmetic: 130 us -> 57.6 us
    pallas_call x12 -> x90, Pallas kernels: 78.3 us -> 207 us  [run(): pl.pallas_call(kernel, out_shape=tuple(shapes), compiler_params=pltpu.Com...]
    dot_general x61 -> x1, matrix products: 128 us -> 0.21 us  [on_device(): jnp.einsum('mns,msh->mhn', row_member, head_mask.astype(f32), precision=h...]
    unnamed x1159 -> x455, local copies, waits for them, and re-layouts: 179 us -> 56.4 us
    ppermute x99 -> x51, waiting for transfers between devices: 261 us -> 181 us  [along_x(): return lax.ppermute(block, 'tensor', [(0, 1), (1, 0), (2, 3), (3, 2)])]
    ppermute x98 -> x50, waiting for transfers between devices: 273 us -> 212 us  [along_y(): return lax.ppermute(block, 'tensor', [(0, 2), (2, 0), (1, 3), (3, 1)])]
    ppermute x99 -> x51, starting transfers between devices: 104 us -> 51.8 us  [along_x(): return lax.ppermute(block, 'tensor', [(0, 1), (1, 0), (2, 3), (3, 2)])]
    ppermute x98 -> x50, starting transfers between devices: 98.5 us -> 56 us  [along_y(): return lax.ppermute(block, 'tensor', [(0, 2), (2, 0), (1, 3), (3, 1)])]
    reduce_scatter x2, waiting for transfers between devices: 44.3 us -> 6.34 us  [reduced(): lax.psum_scatter(total.astype(bf16), 'dp', scatter_dimension=0, tiled=True)]
  transfers between devices with their start and end apart: 234 -> 138, of which waited for: 165 -> 63; matrix products, arithmetic and copies ran while one was open for 26% -> 12% of each run, Pallas kernels for 3% -> 20%
where the time goes in v2:
time: 974 us; the launch traced here: 961 us
  waiting for transfers between devices  438 us (45%)
  Pallas kernels  207 us (21%)
  starting transfers between devices  120 us (12%)
  local copies, waits for them, and re-layouts  73.4 us (8%)
  other arithmetic  57.6 us (6%)
  matrix products  47.9 us (5%)
  between operations  17.1 us (2%)
    ppermute x50, waiting for transfers between devices, along_y(): return lax.ppermute(block, 'tensor', [(0, 2), (2, 0), (1, 3), (3, 1)])  212 us
    pallas_call x90, Pallas kernels, run(): pl.pallas_call(kernel, out_shape=tuple(shapes), compiler_params=pltpu.Com...  207 us
    ppermute x51, waiting for transfers between devices, along_x(): return lax.ppermute(block, 'tensor', [(0, 1), (1, 0), (2, 3), (3, 2)])  181 us
    unnamed x455, local copies, waits for them, and re-layouts  56.4 us
    ppermute x50, starting transfers between devices, along_y(): return lax.ppermute(block, 'tensor', [(0, 2), (2, 0), (1, 3), (3, 1)])  56 us
    ppermute x51, starting transfers between devices, along_x(): return lax.ppermute(block, 'tensor', [(0, 1), (1, 0), (2, 3), (3, 2)])  51.8 us
    dot_general x8, matrix products, outer(): jnp.einsum('nd,nf->df', left, right, preferred_element_type=f32)  41.1 us
    ppermute x6, waiting for transfers between devices, gather_dp(): lax.ppermute(block, 'dp', [(i, (i + step) % size) for i in range(size)])  32.5 us
  transfers between devices with their start and end apart: 138, of which 63 were waited for; matrix products, arithmetic and copies ran while one was open for 12% of the time, Pallas kernels for 20%

profile of v2, /device:TPU:0, one launch (start us, length us, event | category | flops | bytes accessed | tf_op | source)
XLA Modules:
  0.0 961.4 jit_solution(6654815127244322520)
XLA Ops:
  32.4 5.9 collective-permute-done.4.refs_1_
  40.3 13.0 %collective-permute-done.5.refs_2_ = bf16[256,1152]{1,0:T(8,128)(2,1)S(1)} collective-permute-done((bf16[256,1152]{1,0:T(8,128)(2,1)S(1)}, bf16[256,1152]{1,0:T(8,128)(2,1)S(1)}, u32[]{:S(2)}, u32[]{:S(2)}) %collective-permute-start.5) | collective-permute-done | bytes 589856 | tf_op jit(solution)/shard_map/ppermute | solution.py:41
  64.2 9.9 %attend.6 = (bf16[512,288]{1,0:T(8,128)(2,1)S(1)}, f32[4,512]{1,0:T(4,128)S(1)}, bf16[256,1152]{1,0:T(8,128)(2,1)S(1)}, bf16[256,1152]{1,0:T(8,128)(2,1)}) custom-call(bf16[512,288]{1,0:T(8,128)(2,1)S(1)} %get-tuple-element.395.query_ref.refs_4_, bf16[512,640]{1,0:T(8,128)(2,1)S(1)} %get-tuple-element.396.own_ref.refs_5_, ...), custom_call_target="tpu_custom_call" | custom-call | flops 943718400 | bytes 3764224 | tf_op jit(solution)/shard_map/attend/pallas_call | solution.py:177
  86.0 9.4 attend.7
  106.3 7.1 collective-permute-done.21.arrived
  115.3 8.7 attend.8
  131.7 13.2 %collective-permute-done.17.refs_1_ = bf16[128,1152]{1,0:T(8,128)(2,1)S(1)} collective-permute-done((bf16[128,1152]{1,0:T(8,128)(2,1)S(1)}, bf16[128,1152]{1,0:T(8,128)(2,1)S(1)}, u32[]{:S(2)}, u32[]{:S(2)}) %collective-permute-start.17) | collective-permute-done | bytes 294944 | tf_op jit(solution)/shard_map/ppermute | solution.py:37
  151.9 12.2 %collective-permute-done.20.refs_1_ = bf16[128,1152]{1,0:T(8,128)(2,1)S(1)} collective-permute-done((bf16[128,1152]{1,0:T(8,128)(2,1)S(1)}, bf16[128,1152]{1,0:T(8,128)(2,1)S(1)}, u32[]{:S(2)}, u32[]{:S(2)}) %collective-permute-start.20) | collective-permute-done | bytes 294944 | tf_op jit(solution)/shard_map/ppermute | solution.py:41
  164.6 5.2 feed.6
  174.9 5.0 feed.7
  182.2 8.8 collective-permute-done.27.refs_1_
  196.9 10.8 %collective-permute-done.28.refs_2_ = bf16[256,1152]{1,0:T(8,128)(2,1)S(1)} collective-permute-done((bf16[256,1152]{1,0:T(8,128)(2,1)S(1)}, bf16[256,1152]{1,0:T(8,128)(2,1)S(1)}, u32[]{:S(2)}, u32[]{:S(2)}) %collective-permute-start.28) | collective-permute-done | bytes 589856 | tf_op jit(solution)/shard_map/ppermute | solution.py:41
  207.7 5.0 feed.8
  219.9 11.1 %collective-permute-done.35.refs_1_ = bf16[128,1152]{1,0:T(8,128)(2,1)S(1)} collective-permute-done((bf16[128,1152]{1,0:T(8,128)(2,1)S(1)}, bf16[128,1152]{1,0:T(8,128)(2,1)S(1)}, u32[]{:S(2)}, u32[]{:S(2)}) %collective-permute-start.35) | collective-permute-done | bytes 294944 | tf_op jit(solution)/shard_map/ppermute | solution.py:37
  233.4 13.4 %collective-permute-done.34.refs_1_ = bf16[128,1152]{1,0:T(8,128)(2,1)S(1)} collective-permute-done((bf16[128,1152]{1,0:T(8,128)(2,1)S(1)}, bf16[128,1152]{1,0:T(8,128)(2,1)S(1)}, u32[]{:S(2)}, u32[]{:S(2)}) %collective-permute-start.34) | collective-permute-done | bytes 294944 | tf_op jit(solution)/shard_map/ppermute | solution.py:41
  251.4 8.6 attend.9
  260.0 5.5 collective-permute-done.43.refs_2_
  273.5 8.7 attend.10
  292.4 12.8 %collective-permute-done.50.arrived = bf16[256,1152]{1,0:T(8,128)(2,1)S(1)} collective-permute-done((bf16[256,1152]{1,0:T(8,128)(2,1)S(1)}, bf16[256,1152]{1,0:T(8,128)(2,1)S(1)}, u32[]{:S(2)}, u32[]{:S(2)}) %collective-permute-start.50) | collective-permute-done | bytes 589856 | tf_op jit(solution)/shard_map/ppermute | solution.py:41
  306.3 8.8 attend.11
  329.9 13.4 %collective-permute-done.48.arrived = bf16[256,1152]{1,0:T(8,128)(2,1)S(1)} collective-permute-done((bf16[256,1152]{1,0:T(8,128)(2,1)S(1)}, bf16[256,1152]{1,0:T(8,128)(2,1)S(1)}, u32[]{:S(2)}, u32[]{:S(2)}) %collective-permute-start.48) | collective-permute-done | bytes 589856 | tf_op jit(solution)/shard_map/ppermute | solution.py:37
  348.0 18.0 %collective-permute-done.49.refs_1_ = bf16[128,1152]{1,0:T(8,128)(2,1)S(1)} collective-permute-done((bf16[128,1152]{1,0:T(8,128)(2,1)S(1)}, bf16[128,1152]{1,0:T(8,128)(2,1)S(1)}, u32[]{:S(2)}, u32[]{:S(2)}) %collective-permute-start.49) | collective-permute-done | bytes 294944 | tf_op jit(solution)/shard_map/ppermute | solution.py:41
  367.5 5.0 feed.9
  374.8 4.5 feed_back.6
  382.8 5.0 feed.10
  393.8 7.2 collective-permute-done.65.arrived
  402.6 5.2 feed.11
  422.0 4.3 collective-permute-done.71.refs_1_
  427.1 7.1 collective-permute-done.58.arrived
  434.9 12.0 %collective-permute-done.75.arrived = bf16[256,1152]{1,0:T(8,128)(2,1)S(1)} collective-permute-done((bf16[256,1152]{1,0:T(8,128)(2,1)S(1)}, bf16[256,1152]{1,0:T(8,128)(2,1)S(1)}, u32[]{:S(2)}, u32[]{:S(2)}) %collective-permute-start.75) | collective-permute-done | bytes 589856 | tf_op jit(solution)/shard_map/ppermute | solution.py:41
  452.5 4.5 collective-permute-done.59.refs_1_
  465.8 5.1 collective-permute-done.74.refs_1_
  473.8 8.1 attend_back.6
  486.9 11.3 %collective-permute-done.83.refs_2_ = bf16[256,1152]{1,0:T(8,128)(2,1)S(1)} collective-permute-done((bf16[256,1152]{1,0:T(8,128)(2,1)S(1)}, bf16[256,1152]{1,0:T(8,128)(2,1)S(1)}, u32[]{:S(2)}, u32[]{:S(2)}) %collective-permute-start.83) | collective-permute-done | bytes 589856 | tf_op jit(solution)/shard_map/ppermute | solution.py:37
  498.3 8.2 attend_back.7
  511.4 11.0 %collective-permute-done.81.refs_2_ = bf16[256,1152]{1,0:T(8,128)(2,1)S(1)} collective-permute-done((bf16[256,1152]{1,0:T(8,128)(2,1)S(1)}, bf16[256,1152]{1,0:T(8,128)(2,1)S(1)}, u32[]{:S(2)}, u32[]{:S(2)}) %collective-permute-start.81) | collective-permute-done | bytes 589856 | tf_op jit(solution)/shard_map/ppermute | solution.py:41
  524.5 7.9 attend_back.8
  537.2 17.3 %collective-permute-done.79.refs_1_ = bf16[128,1152]{1,0:T(8,128)(2,1)S(1)} collective-permute-done((bf16[128,1152]{1,0:T(8,128)(2,1)S(1)}, bf16[128,1152]{1,0:T(8,128)(2,1)S(1)}, u32[]{:S(2)}, u32[]{:S(2)}) %collective-permute-start.79) | collective-permute-done | bytes 294944 | tf_op jit(solution)/shard_map/ppermute | solution.py:41
  557.5 7.7 collective-permute-done.86.refs_1_
  571.9 15.6 %collective-permute-done.89.refs_1_ = bf16[128,1152]{1,0:T(8,128)(2,1)S(1)} collective-permute-done((bf16[128,1152]{1,0:T(8,128)(2,1)S(1)}, bf16[128,1152]{1,0:T(8,128)(2,1)S(1)}, u32[]{:S(2)}, u32[]{:S(2)}) %collective-permute-start.89) | collective-permute-done | bytes 294944 | tf_op jit(solution)/shard_map/ppermute | solution.py:41
  598.6 12.2 %collective-permute-done.97.refs_2_ = bf16[256,1152]{1,0:T(8,128)(2,1)S(1)} collective-permute-done((bf16[256,1152]{1,0:T(8,128)(2,1)S(1)}, bf16[256,1152]{1,0:T(8,128)(2,1)S(1)}, u32[]{:S(2)}, u32[]{:S(2)}) %collective-permute-start.97) | collective-permute-done | bytes 589856 | tf_op jit(solution)/shard_map/ppermute | solution.py:37
  610.8 7.4 collective-permute-done.92.arrived
  635.9 6.2 collective-permute-done.98.refs_1_
  643.9 5.3 collective-permute-done.102.arrived
  660.1 4.6 collective-permute-done.101.refs_1_
  667.3 8.2 attend_back.9
  681.2 10.6 %collective-permute-done.110.refs_2_ = bf16[256,1152]{1,0:T(8,128)(2,1)S(1)} collective-permute-done((bf16[256,1152]{1,0:T(8,128)(2,1)S(1)}, bf16[256,1152]{1,0:T(8,128)(2,1)S(1)}, u32[]{:S(2)}, u32[]{:S(2)}) %collective-permute-start.110) | collective-permute-done | bytes 589856 | tf_op jit(solution)/shard_map/ppermute | solution.py:37
  691.9 7.9 attend_back.10
  706.5 9.2 collective-permute-done.108.refs_2_
  715.8 8.0 attend_back.11
  746.1 5.0 add_convert_fusion.3
  755.4 7.7 convolution_convert_fusion.1
  763.2 7.4 broadcast_select_fusion
  794.7 4.3 add_convert_fusion
  799.2 8.0 convolution_convert_fusion.3
  807.3 7.4 broadcast_select_fusion.1
  827.6 12.4 %collective-permute-done.105.arrived = bf16[256,1152]{1,0:T(8,128)(2,1)S(1)} collective-permute-done((bf16[256,1152]{1,0:T(8,128)(2,1)S(1)}, bf16[256,1152]{1,0:T(8,128)(2,1)S(1)}, u32[]{:S(2)}, u32[]{:S(2)}) %collective-permute-start.105) | collective-permute-done | bytes 589856 | tf_op jit(solution)/shard_map/ppermute | solution.py:37
  848.8 13.4 %collective-permute-done.113.arrived = bf16[256,1152]{1,0:T(8,128)(2,1)S(1)} collective-permute-done((bf16[256,1152]{1,0:T(8,128)(2,1)}, bf16[256,1152]{1,0:T(8,128)(2,1)S(1)}, u32[]{:S(2)}, u32[]{:S(2)}) %collective-permute-start.113) | collective-permute-done | bytes 589856 | tf_op jit(solution)/shard_map/ppermute | solution.py:41
  873.1 6.3 collective-permute-done.116.refs_1_
  885.5 7.4 collective-permute-done.123
  893.8 5.0 collective-permute-done.124
  902.4 10.0 %collective-permute-done.127 = f32[24,1728]{1,0:T(8,128)S(1)} collective-permute-done((f32[24,1728]{1,0:T(8,128)S(1)}, f32[24,1728]{1,0:T(8,128)S(1)}, u32[]{:S(2)}, u32[]{:S(2)}) %collective-permute-start.127) | collective-permute-done | bytes 165920 | tf_op jit(solution)/shard_map/ppermute | solution.py:153
  912.4 22.5 %collective-permute-done.126 = f32[24,1728]{1,0:T(8,128)S(1)} collective-permute-done((f32[24,1728]{1,0:T(8,128)S(1)}, f32[24,1728]{1,0:T(8,128)S(1)}, u32[]{:S(2)}, u32[]{:S(2)}) %collective-permute-start.126) | collective-permute-done | bytes 165920 | tf_op jit(solution)/shard_map/ppermute | solution.py:153
  940.8 6.3 reduce-scatter.9.cloned.1.call-done
  (892 shorter events, 379.7 us)
Async XLA Ops:
  7.2 930.8 %reduce-scatter.13.cloned.1.call-start = ((), (), s32[]{:S(2)}) async-start(), calls=%async_computation.6 | async-start | bytes 1843200
  15.2 46.3 %collective-permute-start.8 = (bf16[288,1152]{1,0:T(8,128)(2,1)}, bf16[288,1152]{1,0:T(8,128)(2,1)}, u32[]{:S(2)}, u32[]{:S(2)}) collective-permute-start(bf16[288,1152]{1,0:T(8,128)(2,1)} %bitcast.25), channel_id=1, source_target_pairs={{0,16},{16,0},{1,17},{17,1},{2,18},{18,2},{3,19},{19,3},{4,20},{20... | collective-permute-start | bytes 1990664 | tf_op jit(solution)/shard_map/ppermute | solution.py:33
  15.2 38.2 %collective-permute-start.6 = (bf16[864,1152]{1,0:T(8,128)(2,1)}, bf16[864,1152]{1,0:T(8,128)(2,1)}, u32[]{:S(2)}, u32[]{:S(2)}) collective-permute-start(bf16[864,1152]{1,0:T(8,128)(2,1)} %bitcast.16), channel_id=1, source_target_pairs={{0,16},{16,0},{1,17},{17,1},{2,18},{18,2},{3,19},{19,3},{4,20},{20... | collective-permute-start | bytes 5971976 | tf_op jit(solution)/shard_map/ppermute | solution.py:33
  15.7 112.9 %collective-permute-start.24 = (bf16[1152,1152]{1,0:T(8,128)(2,1)}, bf16[1152,1152]{1,0:T(8,128)(2,1)}, u32[]{:S(2)}, u32[]{:S(2)}) collective-permute-start(bf16[1152,1152]{1,0:T(8,128)(2,1)} %bitcast.33), channel_id=1, source_target_pairs={{0,16},{16,0},{1,17},{17,1},{2,18},{18,2},{3,19},{19,3},{4,20},{20... | collective-permute-start | bytes 7962632 | tf_op jit(solution)/shard_map/ppermute | solution.py:33
  30.8 29.0 %collective-permute-start.13 = (bf16[128,1152]{1,0:T(8,128)(2,1)S(1)}, bf16[128,1152]{1,0:T(8,128)(2,1)S(1)}, u32[]{:S(2)}, u32[]{:S(2)}) collective-permute-start(bf16[128,1152]{1,0:T(8,128)(2,1)S(1)} %first.5.refs_0_), channel_id=1, source_target_pairs={{0,8},{8,0},{4,12},{12,4},{1,9},{9,1},{5,13},{13,5},{2,10},{10,2},... | collective-permute-start | bytes 884744 | tf_op jit(solution)/shard_map/ppermute | solution.py:41
  84.5 64.4 %collective-permute-start.23 = (bf16[1152,1152]{1,0:T(8,128)(2,1)}, bf16[1152,1152]{1,0:T(8,128)(2,1)}, u32[]{:S(2)}, u32[]{:S(2)}) collective-permute-start(bf16[1152,1152]{1,0:T(8,128)(2,1)} %bitcast.32), channel_id=1, source_target_pairs={{0,16},{16,0},{1,17},{17,1},{2,18},{18,2},{3,19},{19,3},{4,20},{20... | collective-permute-start | bytes 7962632 | tf_op jit(solution)/shard_map/ppermute | solution.py:33
  104.7 20.2 %collective-permute-start.10 = (bf16[128,1152]{1,0:T(8,128)(2,1)S(1)}, bf16[128,1152]{1,0:T(8,128)(2,1)S(1)}, u32[]{:S(2)}, u32[]{:S(2)}) collective-permute-start(bf16[128,1152]{1,0:T(8,128)(2,1)S(1)} %get-tuple-element.400), channel_id=1, source_target_pairs={{0,8},{8,0},{4,12},{12,4},{1,9},{9,1},{5,13},{13,5},{2,10},{10,2},... | collective-permute-start | bytes 884744 | tf_op jit(solution)/shard_map/ppermute | solution.py:41
  124.9 22.2 %collective-permute-start.19 = (bf16[256,1152]{1,0:T(8,128)(2,1)S(1)}, bf16[256,1152]{1,0:T(8,128)(2,1)S(1)}, u32[]{:S(2)}, u32[]{:S(2)}) collective-permute-start(bf16[256,1152]{1,0:T(8,128)(2,1)S(1)} %get-tuple-element.418), channel_id=1, source_target_pairs={{0,4},{4,0},{8,12},{12,8},{1,5},{5,1},{9,13},{13,9},{2,6},{6,2},{1... | collective-permute-start | bytes 1769480 | tf_op jit(solution)/shard_map/ppermute | solution.py:37
  144.9 19.7 %collective-permute-start.18 = (bf16[256,1152]{1,0:T(8,128)(2,1)S(1)}, bf16[256,1152]{1,0:T(8,128)(2,1)S(1)}, u32[]{:S(2)}, u32[]{:S(2)}) collective-permute-start(bf16[256,1152]{1,0:T(8,128)(2,1)S(1)} %pad_maximum_fusion.8), channel_id=1, source_target_pairs={{0,8},{8,0},{4,12},{12,4},{1,9},{9,1},{5,13},{13,5},{2,10},{10,2},... | collective-permute-start | bytes 1769480 | tf_op jit(solution)/shard_map/ppermute | solution.py:41
  145.8 29.1 %collective-permute-start.30 = (bf16[256,1152]{1,0:T(8,128)(2,1)S(1)}, bf16[256,1152]{1,0:T(8,128)(2,1)S(1)}, u32[]{:S(2)}, u32[]{:S(2)}) collective-permute-start(bf16[256,1152]{1,0:T(8,128)(2,1)S(1)} %pad_maximum_fusion.10), channel_id=1, source_target_pairs={{0,4},{4,0},{8,12},{12,8},{1,5},{5,1},{9,13},{13,9},{2,6},{6,2},{1... | collective-permute-start | bytes 1769480 | tf_op jit(solution)/shard_map/ppermute | solution.py:37
  172.8 19.8 %collective-permute-start.25 = (bf16[256,1152]{1,0:T(8,128)(2,1)S(1)}, bf16[256,1152]{1,0:T(8,128)(2,1)S(1)}, u32[]{:S(2)}, u32[]{:S(2)}) collective-permute-start(bf16[256,1152]{1,0:T(8,128)(2,1)S(1)} %get-tuple-element.435), channel_id=1, source_target_pairs={{0,4},{4,0},{8,12},{12,8},{1,5},{5,1},{9,13},{13,9},{2,6},{6,2},{1... | collective-permute-start | bytes 1769480 | tf_op jit(solution)/shard_map/ppermute | solution.py:37
  192.7 22.1 %collective-permute-start.26 = (bf16[128,1152]{1,0:T(8,128)(2,1)S(1)}, bf16[128,1152]{1,0:T(8,128)(2,1)S(1)}, u32[]{:S(2)}, u32[]{:S(2)}) collective-permute-start(bf16[128,1152]{1,0:T(8,128)(2,1)S(1)} %get-tuple-element.437), channel_id=1, source_target_pairs={{0,8},{8,0},{4,12},{12,4},{1,9},{9,1},{5,13},{13,5},{2,10},{10,2},... | collective-permute-start | bytes 884744 | tf_op jit(solution)/shard_map/ppermute | solution.py:41
  195.2 22.4 %collective-permute-start.32 = (bf16[128,1152]{1,0:T(8,128)(2,1)S(1)}, bf16[128,1152]{1,0:T(8,128)(2,1)S(1)}, u32[]{:S(2)}, u32[]{:S(2)}) collective-permute-start(bf16[128,1152]{1,0:T(8,128)(2,1)S(1)} %get-tuple-element.454), channel_id=1, source_target_pairs={{0,4},{4,0},{8,12},{12,8},{1,5},{5,1},{9,13},{13,9},{2,6},{6,2},{1... | collective-permute-start | bytes 884744 | tf_op jit(solution)/shard_map/ppermute | solution.py:37
  218.7 30.5 %collective-permute-start.42 = (bf16[128,1152]{1,0:T(8,128)(2,1)S(1)}, bf16[128,1152]{1,0:T(8,128)(2,1)S(1)}, u32[]{:S(2)}, u32[]{:S(2)}) collective-permute-start(bf16[128,1152]{1,0:T(8,128)(2,1)S(1)} %get-tuple-element.480.refs_0_), channel_id=1, source_target_pairs={{0,8},{8,0},{4,12},{12,4},{1,9},{9,1},{5,13},{13,5},{2,10},{10,2},... | collective-permute-start | bytes 884744 | tf_op jit(solution)/shard_map/ppermute | solution.py:41
  250.2 21.2 %collective-permute-start.40 = (bf16[128,1152]{1,0:T(8,128)(2,1)S(1)}, bf16[128,1152]{1,0:T(8,128)(2,1)S(1)}, u32[]{:S(2)}, u32[]{:S(2)}) collective-permute-start(bf16[128,1152]{1,0:T(8,128)(2,1)S(1)} %get-tuple-element.486.refs_0_), channel_id=1, source_target_pairs={{0,4},{4,0},{8,12},{12,8},{1,5},{5,1},{9,13},{13,9},{2,6},{6,2},{1... | collective-permute-start | bytes 884744 | tf_op jit(solution)/shard_map/ppermute | solution.py:37
  291.0 24.8 %collective-permute-start.39 = (bf16[128,1152]{1,0:T(8,128)(2,1)S(1)}, bf16[128,1152]{1,0:T(8,128)(2,1)S(1)}, u32[]{:S(2)}, u32[]{:S(2)}) collective-permute-start(bf16[128,1152]{1,0:T(8,128)(2,1)S(1)} %get-tuple-element.476), channel_id=1, source_target_pairs={{0,8},{8,0},{4,12},{12,4},{1,9},{9,1},{5,13},{13,5},{2,10},{10,2},... | collective-permute-start | bytes 884744 | tf_op jit(solution)/shard_map/ppermute | solution.py:41
  291.5 28.8 %collective-permute-start.63 = (bf16[128,1152]{1,0:T(8,128)(2,1)S(1)}, bf16[128,1152]{1,0:T(8,128)(2,1)S(1)}, u32[]{:S(2)}, u32[]{:S(2)}) collective-permute-start(bf16[128,1152]{1,0:T(8,128)(2,1)S(1)} %upstream.3.refs_0_), channel_id=1, source_target_pairs={{0,4},{4,0},{8,12},{12,8},{1,5},{5,1},{9,13},{13,9},{2,6},{6,2},{1... | collective-permute-start | bytes 884744 | tf_op jit(solution)/shard_map/ppermute | solution.py:37
  319.9 24.8 %collective-permute-start.67 = (bf16[128,1152]{1,0:T(8,128)(2,1)S(1)}, bf16[128,1152]{1,0:T(8,128)(2,1)S(1)}, u32[]{:S(2)}, u32[]{:S(2)}) collective-permute-start(bf16[128,1152]{1,0:T(8,128)(2,1)S(1)} %upstream.5.refs_0_), channel_id=1, source_target_pairs={{0,4},{4,0},{8,12},{12,8},{1,5},{5,1},{9,13},{13,9},{2,6},{6,2},{1... | collective-permute-start | bytes 884744 | tf_op jit(solution)/shard_map/ppermute | solution.py:37
  320.4 23.0 %collective-permute-start.48 = (bf16[256,1152]{1,0:T(8,128)(2,1)S(1)}, bf16[256,1152]{1,0:T(8,128)(2,1)S(1)}, u32[]{:S(2)}, u32[]{:S(2)}) collective-permute-start(bf16[256,1152]{1,0:T(8,128)(2,1)S(1)} %get-tuple-element.496), channel_id=1, source_target_pairs={{0,4},{4,0},{8,12},{12,8},{1,5},{5,1},{9,13},{13,9},{2,6},{6,2},{1... | collective-permute-start | bytes 1769480 | tf_op jit(solution)/shard_map/ppermute | solution.py:37
  322.0 24.5 %collective-permute-start.64 = (bf16[256,1152]{1,0:T(8,128)(2,1)S(1)}, bf16[256,1152]{1,0:T(8,128)(2,1)S(1)}, u32[]{:S(2)}, u32[]{:S(2)}) collective-permute-start(bf16[256,1152]{1,0:T(8,128)(2,1)S(1)} %pad_maximum_fusion.17), channel_id=1, source_target_pairs={{0,8},{8,0},{4,12},{12,4},{1,9},{9,1},{5,13},{13,5},{2,10},{10,2},... | collective-permute-start | bytes 1769480 | tf_op jit(solution)/shard_map/ppermute | solution.py:41
  326.4 20.7 %collective-permute-start.56 = (bf16[128,1152]{1,0:T(8,128)(2,1)S(1)}, bf16[128,1152]{1,0:T(8,128)(2,1)S(1)}, u32[]{:S(2)}, u32[]{:S(2)}) collective-permute-start(bf16[128,1152]{1,0:T(8,128)(2,1)S(1)} %get-tuple-element.517.refs_0_), channel_id=1, source_target_pairs={{0,8},{8,0},{4,12},{12,4},{1,9},{9,1},{5,13},{13,5},{2,10},{10,2},... | collective-permute-start | bytes 884744 | tf_op jit(solution)/shard_map/ppermute | solution.py:41
  328.1 39.4 %collective-permute-start.47 = (bf16[256,1152]{1,0:T(8,128)(2,1)S(1)}, bf16[256,1152]{1,0:T(8,128)(2,1)S(1)}, u32[]{:S(2)}, u32[]{:S(2)}) collective-permute-start(bf16[256,1152]{1,0:T(8,128)(2,1)S(1)} %pad_maximum_fusion.14), channel_id=1, source_target_pairs={{0,8},{8,0},{4,12},{12,4},{1,9},{9,1},{5,13},{13,5},{2,10},{10,2},... | collective-permute-start | bytes 1769480 | tf_op jit(solution)/shard_map/ppermute | solution.py:41
  343.4 37.9 %collective-permute-start.70 = (bf16[256,1152]{1,0:T(8,128)(2,1)S(1)}, bf16[256,1152]{1,0:T(8,128)(2,1)S(1)}, u32[]{:S(2)}, u32[]{:S(2)}) collective-permute-start(bf16[256,1152]{1,0:T(8,128)(2,1)S(1)} %pad_maximum_fusion.19), channel_id=1, source_target_pairs={{0,4},{4,0},{8,12},{12,8},{1,5},{5,1},{9,13},{13,9},{2,6},{6,2},{1... | collective-permute-start | bytes 1769480 | tf_op jit(solution)/shard_map/ppermute | solution.py:37
  344.7 21.4 %collective-permute-start.49 = (bf16[128,1152]{1,0:T(8,128)(2,1)S(1)}, bf16[128,1152]{1,0:T(8,128)(2,1)S(1)}, u32[]{:S(2)}, u32[]{:S(2)}) collective-permute-start(bf16[128,1152]{1,0:T(8,128)(2,1)S(1)} %get-tuple-element.498), channel_id=1, source_target_pairs={{0,8},{8,0},{4,12},{12,4},{1,9},{9,1},{5,13},{13,5},{2,10},{10,2},... | collective-permute-start | bytes 884744 | tf_op jit(solution)/shard_map/ppermute | solution.py:41
  346.6 46.4 %collective-permute-start.68 = (bf16[256,1152]{1,0:T(8,128)(2,1)S(1)}, bf16[256,1152]{1,0:T(8,128)(2,1)S(1)}, u32[]{:S(2)}, u32[]{:S(2)}) collective-permute-start(bf16[256,1152]{1,0:T(8,128)(2,1)S(1)} %pad_maximum_fusion.18), channel_id=1, source_target_pairs={{0,8},{8,0},{4,12},{12,4},{1,9},{9,1},{5,13},{13,5},{2,10},{10,2},... | collective-permute-start | bytes 1769480 | tf_op jit(solution)/shard_map/ppermute | solution.py:41
  347.2 35.6 %collective-permute-start.57 = (bf16[256,1152]{1,0:T(8,128)(2,1)S(1)}, bf16[256,1152]{1,0:T(8,128)(2,1)S(1)}, u32[]{:S(2)}, u32[]{:S(2)}) collective-permute-start(bf16[256,1152]{1,0:T(8,128)(2,1)S(1)} %pad_maximum_fusion.16), channel_id=1, source_target_pairs={{0,4},{4,0},{8,12},{12,8},{1,5},{5,1},{9,13},{13,9},{2,6},{6,2},{1... | collective-permute-start | bytes 1769480 | tf_op jit(solution)/shard_map/ppermute | solution.py:37
  373.6 19.3 %collective-permute-start.52 = (bf16[256,1152]{1,0:T(8,128)(2,1)S(1)}, bf16[256,1152]{1,0:T(8,128)(2,1)S(1)}, u32[]{:S(2)}, u32[]{:S(2)}) collective-permute-start(bf16[256,1152]{1,0:T(8,128)(2,1)S(1)} %get-tuple-element.513), channel_id=1, source_target_pairs={{0,4},{4,0},{8,12},{12,8},{1,5},{5,1},{9,13},{13,9},{2,6},{6,2},{1... | collective-permute-start | bytes 1769480 | tf_op jit(solution)/shard_map/ppermute | solution.py:37
  380.4 20.6 %collective-permute-start.65 = (bf16[256,1152]{1,0:T(8,128)(2,1)S(1)}, bf16[256,1152]{1,0:T(8,128)(2,1)S(1)}, u32[]{:S(2)}, u32[]{:S(2)}) collective-permute-start(bf16[256,1152]{1,0:T(8,128)(2,1)S(1)} %get-tuple-element.550), channel_id=1, source_target_pairs={{0,4},{4,0},{8,12},{12,8},{1,5},{5,1},{9,13},{13,9},{2,6},{6,2},{1... | collective-permute-start | bytes 1769480 | tf_op jit(solution)/shard_map/ppermute | solution.py:37
  381.3 21.2 %collective-permute-start.55 = (bf16[256,1152]{1,0:T(8,128)(2,1)S(1)}, bf16[256,1152]{1,0:T(8,128)(2,1)S(1)}, u32[]{:S(2)}, u32[]{:S(2)}) collective-permute-start(bf16[256,1152]{1,0:T(8,128)(2,1)S(1)} %pad_maximum_fusion.15), channel_id=1, source_target_pairs={{0,8},{8,0},{4,12},{12,4},{1,9},{9,1},{5,13},{13,5},{2,10},{10,2},... | collective-permute-start | bytes 1769480 | tf_op jit(solution)/shard_map/ppermute | solution.py:41
  393.1 20.9 %collective-permute-start.53 = (bf16[128,1152]{1,0:T(8,128)(2,1)S(1)}, bf16[128,1152]{1,0:T(8,128)(2,1)S(1)}, u32[]{:S(2)}, u32[]{:S(2)}) collective-permute-start(bf16[128,1152]{1,0:T(8,128)(2,1)S(1)} %get-tuple-element.515), channel_id=1, source_target_pairs={{0,8},{8,0},{4,12},{12,4},{1,9},{9,1},{5,13},{13,5},{2,10},{10,2},... | collective-permute-start | bytes 884744 | tf_op jit(solution)/shard_map/ppermute | solution.py:41
  418.2 28.6 %collective-permute-start.75 = (bf16[256,1152]{1,0:T(8,128)(2,1)S(1)}, bf16[256,1152]{1,0:T(8,128)(2,1)S(1)}, u32[]{:S(2)}, u32[]{:S(2)}) collective-permute-start(bf16[256,1152]{1,0:T(8,128)(2,1)S(1)} %get-tuple-element.574), channel_id=1, source_target_pairs={{0,8},{8,0},{4,12},{12,4},{1,9},{9,1},{5,13},{13,5},{2,10},{10,2},... | collective-permute-start | bytes 1769480 | tf_op jit(solution)/shard_map/ppermute | solution.py:41
  420.0 27.6 %collective-permute-start.60 = (bf16[256,1152]{1,0:T(8,128)(2,1)S(1)}, bf16[256,1152]{1,0:T(8,128)(2,1)S(1)}, u32[]{:S(2)}, u32[]{:S(2)}) collective-permute-start(bf16[256,1152]{1,0:T(8,128)(2,1)S(1)} %get-tuple-element.538), channel_id=1, source_target_pairs={{0,4},{4,0},{8,12},{12,8},{1,5},{5,1},{9,13},{13,9},{2,6},{6,2},{1... | collective-permute-start | bytes 1769480 | tf_op jit(solution)/shard_map/ppermute | solution.py:37
  420.4 31.2 %collective-permute-start.73 = (bf16[256,1152]{1,0:T(8,128)(2,1)S(1)}, bf16[256,1152]{1,0:T(8,128)(2,1)S(1)}, u32[]{:S(2)}, u32[]{:S(2)}) collective-permute-start(bf16[256,1152]{1,0:T(8,128)(2,1)S(1)} %get-tuple-element.570), channel_id=1, source_target_pairs={{0,4},{4,0},{8,12},{12,8},{1,5},{5,1},{9,13},{13,9},{2,6},{6,2},{1... | collective-permute-start | bytes 1769480 | tf_op jit(solution)/shard_map/ppermute | solution.py:37
  426.4 47.4 %collective-permute-start.72 = (bf16[256,1152]{1,0:T(8,128)(2,1)S(1)}, bf16[256,1152]{1,0:T(8,128)(2,1)S(1)}, u32[]{:S(2)}, u32[]{:S(2)}) collective-permute-start(bf16[256,1152]{1,0:T(8,128)(2,1)S(1)} %pad_maximum_fusion.20), channel_id=1, source_target_pairs={{0,8},{8,0},{4,12},{12,4},{1,9},{9,1},{5,13},{13,5},{2,10},{10,2},... | collective-permute-start | bytes 1769480 | tf_op jit(solution)/shard_map/ppermute | solution.py:41
  434.4 22.6 %collective-permute-start.59 = (bf16[128,1152]{1,0:T(8,128)(2,1)S(1)}, bf16[128,1152]{1,0:T(8,128)(2,1)S(1)}, u32[]{:S(2)}, u32[]{:S(2)}) collective-permute-start(bf16[128,1152]{1,0:T(8,128)(2,1)S(1)} %get-tuple-element.532), channel_id=1, source_target_pairs={{0,4},{4,0},{8,12},{12,8},{1,5},{5,1},{9,13},{13,9},{2,6},{6,2},{1... | collective-permute-start | bytes 884744 | tf_op jit(solution)/shard_map/ppermute | solution.py:37
  451.7 19.2 %collective-permute-start.74 = (bf16[128,1152]{1,0:T(8,128)(2,1)S(1)}, bf16[128,1152]{1,0:T(8,128)(2,1)S(1)}, u32[]{:S(2)}, u32[]{:S(2)}) collective-permute-start(bf16[128,1152]{1,0:T(8,128)(2,1)S(1)} %get-tuple-element.572), channel_id=1, source_target_pairs={{0,8},{8,0},{4,12},{12,4},{1,9},{9,1},{5,13},{13,5},{2,10},{10,2},... | collective-permute-start | bytes 884744 | tf_op jit(solution)/shard_map/ppermute | solution.py:41
  482.6 24.0 %collective-permute-start.80 = (bf16[128,1152]{1,0:T(8,128)(2,1)S(1)}, bf16[128,1152]{1,0:T(8,128)(2,1)S(1)}, u32[]{:S(2)}, u32[]{:S(2)}) collective-permute-start(bf16[128,1152]{1,0:T(8,128)(2,1)S(1)} %get-tuple-element.607.refs_0_), channel_id=1, source_target_pairs={{0,4},{4,0},{8,12},{12,8},{1,5},{5,1},{9,13},{13,9},{2,6},{6,2},{1... | collective-permute-start | bytes 884744 | tf_op jit(solution)/shard_map/ppermute | solution.py:37
  507.0 25.8 %collective-permute-start.78 = (bf16[256,1152]{1,0:T(8,128)(2,1)S(1)}, bf16[256,1152]{1,0:T(8,128)(2,1)S(1)}, u32[]{:S(2)}, u32[]{:S(2)}) collective-permute-start(bf16[256,1152]{1,0:T(8,128)(2,1)S(1)} %get-tuple-element.595), channel_id=1, source_target_pairs={{0,4},{4,0},{8,12},{12,8},{1,5},{5,1},{9,13},{13,9},{2,6},{6,2},{1... | collective-permute-start | bytes 1769480 | tf_op jit(solution)/shard_map/ppermute | solution.py:37
  532.5 23.2 %collective-permute-start.90 = (bf16[256,1152]{1,0:T(8,128)(2,1)S(1)}, bf16[256,1152]{1,0:T(8,128)(2,1)S(1)}, u32[]{:S(2)}, u32[]{:S(2)}) collective-permute-start(bf16[256,1152]{1,0:T(8,128)(2,1)S(1)} %get-tuple-element.624), channel_id=1, source_target_pairs={{0,8},{8,0},{4,12},{12,4},{1,9},{9,1},{5,13},{13,5},{2,10},{10,2},... | collective-permute-start | bytes 1769480 | tf_op jit(solution)/shard_map/ppermute | solution.py:41
  533.0 21.5 %collective-permute-start.79 = (bf16[128,1152]{1,0:T(8,128)(2,1)S(1)}, bf16[128,1152]{1,0:T(8,128)(2,1)S(1)}, u32[]{:S(2)}, u32[]{:S(2)}) collective-permute-start(bf16[128,1152]{1,0:T(8,128)(2,1)S(1)} %get-tuple-element.597), channel_id=1, source_target_pairs={{0,8},{8,0},{4,12},{12,4},{1,9},{9,1},{5,13},{13,5},{2,10},{10,2},... | collective-permute-start | bytes 884744 | tf_op jit(solution)/shard_map/ppermute | solution.py:41
  536.7 28.9 %collective-permute-start.88 = (bf16[256,1152]{1,0:T(8,128)(2,1)S(1)}, bf16[256,1152]{1,0:T(8,128)(2,1)S(1)}, u32[]{:S(2)}, u32[]{:S(2)}) collective-permute-start(bf16[256,1152]{1,0:T(8,128)(2,1)S(1)} %get-tuple-element.620), channel_id=1, source_target_pairs={{0,4},{4,0},{8,12},{12,8},{1,5},{5,1},{9,13},{13,9},{2,6},{6,2},{1... | collective-permute-start | bytes 1769480 | tf_op jit(solution)/shard_map/ppermute | solution.py:37
  565.3 25.9 %collective-permute-start.87 = (bf16[256,1152]{1,0:T(8,128)(2,1)S(1)}, bf16[256,1152]{1,0:T(8,128)(2,1)S(1)}, u32[]{:S(2)}, u32[]{:S(2)}) collective-permute-start(bf16[256,1152]{1,0:T(8,128)(2,1)S(1)} %pad_maximum_fusion.23), channel_id=1, source_target_pairs={{0,8},{8,0},{4,12},{12,4},{1,9},{9,1},{5,13},{13,5},{2,10},{10,2},... | collective-permute-start | bytes 1769480 | tf_op jit(solution)/shard_map/ppermute | solution.py:41
  565.8 21.7 %collective-permute-start.89 = (bf16[128,1152]{1,0:T(8,128)(2,1)S(1)}, bf16[128,1152]{1,0:T(8,128)(2,1)S(1)}, u32[]{:S(2)}, u32[]{:S(2)}) collective-permute-start(bf16[128,1152]{1,0:T(8,128)(2,1)S(1)} %get-tuple-element.622), channel_id=1, source_target_pairs={{0,8},{8,0},{4,12},{12,4},{1,9},{9,1},{5,13},{13,5},{2,10},{10,2},... | collective-permute-start | bytes 884744 | tf_op jit(solution)/shard_map/ppermute | solution.py:41
  571.6 19.1 %collective-permute-start.96 = (bf16[128,1152]{1,0:T(8,128)(2,1)S(1)}, bf16[128,1152]{1,0:T(8,128)(2,1)S(1)}, u32[]{:S(2)}, u32[]{:S(2)}) collective-permute-start(bf16[128,1152]{1,0:T(8,128)(2,1)S(1)} %get-tuple-element.647.refs_0_), channel_id=1, source_target_pairs={{0,8},{8,0},{4,12},{12,4},{1,9},{9,1},{5,13},{13,5},{2,10},{10,2},... | collective-permute-start | bytes 884744 | tf_op jit(solution)/shard_map/ppermute | solution.py:41
  590.7 20.1 %collective-permute-start.97 = (bf16[256,1152]{1,0:T(8,128)(2,1)S(1)}, bf16[256,1152]{1,0:T(8,128)(2,1)S(1)}, u32[]{:S(2)}, u32[]{:S(2)}) collective-permute-start(bf16[256,1152]{1,0:T(8,128)(2,1)S(1)} %pad_maximum_fusion.25), channel_id=1, source_target_pairs={{0,4},{4,0},{8,12},{12,8},{1,5},{5,1},{9,13},{13,9},{2,6},{6,2},{1... | collective-permute-start | bytes 1769480 | tf_op jit(solution)/shard_map/ppermute | solution.py:37
  595.3 23.0 %collective-permute-start.92 = (bf16[256,1152]{1,0:T(8,128)(2,1)S(1)}, bf16[256,1152]{1,0:T(8,128)(2,1)S(1)}, u32[]{:S(2)}, u32[]{:S(2)}) collective-permute-start(bf16[256,1152]{1,0:T(8,128)(2,1)S(1)} %get-tuple-element.641), channel_id=1, source_target_pairs={{0,4},{4,0},{8,12},{12,8},{1,5},{5,1},{9,13},{13,9},{2,6},{6,2},{1... | collective-permute-start | bytes 1769480 | tf_op jit(solution)/shard_map/ppermute | solution.py:37
  598.2 26.7 %collective-permute-start.95 = (bf16[256,1152]{1,0:T(8,128)(2,1)S(1)}, bf16[256,1152]{1,0:T(8,128)(2,1)S(1)}, u32[]{:S(2)}, u32[]{:S(2)}) collective-permute-start(bf16[256,1152]{1,0:T(8,128)(2,1)S(1)} %pad_maximum_fusion.24), channel_id=1, source_target_pairs={{0,8},{8,0},{4,12},{12,4},{1,9},{9,1},{5,13},{13,5},{2,10},{10,2},... | collective-permute-start | bytes 1769480 | tf_op jit(solution)/shard_map/ppermute | solution.py:41
  642.1 25.1 %collective-permute-start.99 = (bf16[256,1152]{1,0:T(8,128)(2,1)S(1)}, bf16[256,1152]{1,0:T(8,128)(2,1)S(1)}, u32[]{:S(2)}, u32[]{:S(2)}) collective-permute-start(bf16[256,1152]{1,0:T(8,128)(2,1)S(1)} %pad_maximum_fusion.26), channel_id=1, source_target_pairs={{0,8},{8,0},{4,12},{12,4},{1,9},{9,1},{5,13},{13,5},{2,10},{10,2},... | collective-permute-start | bytes 1769480 | tf_op jit(solution)/shard_map/ppermute | solution.py:41
  676.9 23.0 %collective-permute-start.107 = (bf16[128,1152]{1,0:T(8,128)(2,1)S(1)}, bf16[128,1152]{1,0:T(8,128)(2,1)S(1)}, u32[]{:S(2)}, u32[]{:S(2)}) collective-permute-start(bf16[128,1152]{1,0:T(8,128)(2,1)S(1)} %get-tuple-element.700.refs_0_), channel_id=1, source_target_pairs={{0,4},{4,0},{8,12},{12,8},{1,5},{5,1},{9,13},{13,9},{2,6},{6,2},{1... | collective-permute-start | bytes 884744 | tf_op jit(solution)/shard_map/ppermute | solution.py:37
  754.9 184.4 %reduce-scatter.15.cloned.1.call-start = ((), (), s32[]{:S(2)}) async-start(), calls=%async_computation.7 | async-start | bytes 1843200
  770.6 24.0 %collective-permute-start.132 = (bf16[1152,1152]{1,0:T(8,128)(2,1)}, bf16[1152,1152]{1,0:T(8,128)(2,1)}, u32[]{:S(2)}, u32[]{:S(2)}) collective-permute-start(bf16[1152,1152]{1,0:T(8,128)(2,1)} %get-tuple-element.902), channel_id=1, source_target_pairs={{0,16},{16,0},{1,17},{17,1},{2,18},{18,2},{3,19},{19,3},{4,20},{20... | collective-permute-start | bytes 7962632 | tf_op jit(solution)/shard_map/ppermute | solution.py:33
  774.7 166.1 %reduce-scatter.11.cloned.1.call-start = ((), (), s32[]{:S(2)}) async-start(), calls=%async_computation.5 | async-start | bytes 3317760 | tf_op jit(solution)/shard_map/reduce_scatter | solution.py:772
  791.1 28.6 %collective-permute-start.118 = (f32[2,3,128]{2,0,1:T(2,128)S(1)}, f32[2,3,128]{2,0,1:T(2,128)S(1)}, u32[]{:S(2)}, u32[]{:S(2)}) collective-permute-start(f32[2,3,128]{2,0,1:T(2,128)S(1)} %bitcast.217), channel_id=1, source_target_pairs={{0,16},{16,0},{1,17},{17,1},{2,18},{18,2},{3,19},{19,3},{4,20},{20... | collective-permute-start | bytes 9224 | tf_op jit(solution)/shard_map/ppermute | solution.py:33
  794.2 26.1 %collective-permute-start.62 = (f32[3,128,1152]{2,1,0:T(8,128)}, f32[3,128,1152]{2,1,0:T(8,128)}, u32[]{:S(2)}, u32[]{:S(2)}) collective-permute-start(f32[3,128,1152]{2,1,0:T(8,128)} %fusion.94), channel_id=1, source_target_pairs={{0,16},{16,0},{1,17},{17,1},{2,18},{18,2},{3,19},{19,3},{4,20},{20... | collective-permute-start | bytes 5308424 | tf_op jit(solution)/shard_map/ppermute | solution.py:33
  799.1 148.0 %reduce-scatter.9.cloned.1.call-start = ((), (), s32[]{:S(2)}) async-start(), calls=%async_computation.4 | async-start | bytes 3317760 | tf_op jit(solution)/shard_map/reduce_scatter | solution.py:772
  814.7 29.0 %collective-permute-start.131 = (bf16[1152,1152]{1,0:T(8,128)(2,1)}, bf16[1152,1152]{1,0:T(8,128)(2,1)}, u32[]{:S(2)}, u32[]{:S(2)}) collective-permute-start(bf16[1152,1152]{1,0:T(8,128)(2,1)} %get-tuple-element.904), channel_id=1, source_target_pairs={{0,16},{16,0},{1,17},{17,1},{2,18},{18,2},{3,19},{19,3},{4,20},{20... | collective-permute-start | bytes 7962632 | tf_op jit(solution)/shard_map/ppermute | solution.py:33
  815.8 84.0 %collective-permute-start.120 = (bf16[24,1152]{1,0:T(8,128)(2,1)}, bf16[24,1152]{1,0:T(8,128)(2,1)}, u32[]{:S(2)}, u32[]{:S(2)}) collective-permute-start(bf16[24,1152]{1,0:T(8,128)(2,1)} %get-tuple-element.861), channel_id=1, source_target_pairs={{0,2},{1,3},{2,0},{3,1},{4,6},{5,7},{6,4},{7,5},{8,10},{9,11},{10,... | collective-permute-start | bytes 165896 | tf_op jit(solution)/shard_map/ppermute | solution.py:153
  818.3 84.0 %collective-permute-start.119 = (bf16[24,1152]{1,0:T(8,128)(2,1)}, bf16[24,1152]{1,0:T(8,128)(2,1)}, u32[]{:S(2)}, u32[]{:S(2)}) collective-permute-start(bf16[24,1152]{1,0:T(8,128)(2,1)} %get-tuple-element.861), channel_id=1, source_target_pairs={{0,1},{1,2},{2,3},{3,0},{4,5},{5,6},{6,7},{7,4},{8,9},{9,10},{10,1... | collective-permute-start | bytes 165896 | tf_op jit(solution)/shard_map/ppermute | solution.py:153
  841.7 23.2 %collective-permute-start.106 = (bf16[128,1152]{1,0:T(8,128)(2,1)}, bf16[128,1152]{1,0:T(8,128)(2,1)}, u32[]{:S(2)}, u32[]{:S(2)}) collective-permute-start(bf16[128,1152]{1,0:T(8,128)(2,1)} %get-tuple-element.690), channel_id=1, source_target_pairs={{0,8},{8,0},{4,12},{12,4},{1,9},{9,1},{5,13},{13,5},{2,10},{10,2},... | collective-permute-start | bytes 884744 | tf_op jit(solution)/shard_map/ppermute | solution.py:41
  842.3 19.9 %collective-permute-start.113 = (bf16[256,1152]{1,0:T(8,128)(2,1)}, bf16[256,1152]{1,0:T(8,128)(2,1)S(1)}, u32[]{:S(2)}, u32[]{:S(2)}) collective-permute-start(bf16[256,1152]{1,0:T(8,128)(2,1)} %get-tuple-element.713), channel_id=1, source_target_pairs={{0,8},{8,0},{4,12},{12,4},{1,9},{9,1},{5,13},{13,5},{2,10},{10,2},... | collective-permute-start | bytes 1769480 | tf_op jit(solution)/shard_map/ppermute | solution.py:41
  843.7 28.7 %collective-permute-start.115 = (bf16[256,1152]{1,0:T(8,128)(2,1)}, bf16[256,1152]{1,0:T(8,128)(2,1)S(1)}, u32[]{:S(2)}, u32[]{:S(2)}) collective-permute-start(bf16[256,1152]{1,0:T(8,128)(2,1)} %get-tuple-element.721), channel_id=1, source_target_pairs={{0,4},{4,0},{8,12},{12,8},{1,5},{5,1},{9,13},{13,9},{2,6},{6,2},{1... | collective-permute-start | bytes 1769480 | tf_op jit(solution)/shard_map/ppermute | solution.py:37
  862.2 40.2 %collective-permute-start.121 = (bf16[24,1152]{1,0:T(8,128)(2,1)}, bf16[24,1152]{1,0:T(8,128)(2,1)S(1)}, u32[]{:S(2)}, u32[]{:S(2)}) collective-permute-start(bf16[24,1152]{1,0:T(8,128)(2,1)} %get-tuple-element.861), channel_id=1, source_target_pairs={{0,3},{1,0},{2,1},{3,2},{4,7},{5,4},{6,5},{7,6},{8,11},{9,8},{10,9... | collective-permute-start | bytes 165896 | tf_op jit(solution)/shard_map/ppermute | solution.py:153
  899.0 35.9 %collective-permute-start.126 = (f32[24,1728]{1,0:T(8,128)S(1)}, f32[24,1728]{1,0:T(8,128)S(1)}, u32[]{:S(2)}, u32[]{:S(2)}) collective-permute-start(f32[24,1728]{1,0:T(8,128)S(1)} %fusion.127), channel_id=1, source_target_pairs={{0,2},{1,3},{2,0},{3,1},{4,6},{5,7},{6,4},{7,5},{8,10},{9,11},{10,... | collective-permute-start | bytes 497672 | tf_op jit(solution)/shard_map/ppermute | solution.py:153
  899.8 35.1 %collective-permute-start.125 = (f32[24,1728]{1,0:T(8,128)S(1)}, f32[24,1728]{1,0:T(8,128)S(1)}, u32[]{:S(2)}, u32[]{:S(2)}) collective-permute-start(f32[24,1728]{1,0:T(8,128)S(1)} %fusion.127), channel_id=1, source_target_pairs={{0,1},{1,2},{2,3},{3,0},{4,5},{5,6},{6,7},{7,4},{8,9},{9,10},{10,1... | collective-permute-start | bytes 497672 | tf_op jit(solution)/shard_map/ppermute | solution.py:153
  (299 other events, 3713.2 us)
Sparse Core Ops, SparseCore 0:
  755.0 33.8 reduce-scatter.12
  791.3 34.5 reduce-scatter.14
  828.2 53.3 reduce-scatter.10
  883.8 63.2 reduce-scatter.8

commit v3 on v2

--- a/solution.py
+++ b/solution.py
@@ -13,6 +13,8 @@
 f32 = jnp.float32
 bf16 = jnp.bfloat16
 log2e = math.log2(math.e)
+brief = pl.CostEstimate(flops=1000000000, bytes_accessed=1, transcendentals=0)
+lengthy = pl.CostEstimate(flops=12000000000, bytes_accessed=1, transcendentals=0)
 
 
 def normalize_keep(value):
@@ -56,70 +58,104 @@
     return range(lax.axis_size("tensor"))
 
 
+def halves_kernel(near, far, near_half, far_half):
+    half = near_half.shape[0]
+    near_half[...] = near[:half, :]
+    far_half[...] = far[half:, :]
+
+
 def gather_start(block, stream):
     if not square():
-        return (lax.all_gather(block, "tensor", axis=0, tiled=True),)
+        return ((lax.all_gather(block, "tensor", axis=0, tiled=True),), ())
     (along, unused), (across, unused) = axes_of(stream)
-    from_near = along(block)
-    return (block, from_near, across(jnp.concatenate([block, from_near], axis=0)))
+    near = along(block)
+    far = across(block)
+    half = block.shape[0] // 2
+    near_half, far_half = run(
+        halves_kernel,
+        [jax.ShapeDtypeStruct((half, block.shape[1]), bf16)] * 2,
+        near,
+        far,
+        name="halves",
+        vmem=4,
+    )
+    return ((block, far, near, across(near_half), along(far_half)), (near_half, far_half))
 
 
 def assemble(pieces, target):
-    if len(pieces) == 1:
-        target[...] = pieces[0][...]
+    begin = 0
+    for piece in pieces:
+        target[begin : begin + piece.shape[0], :] = piece[...]
+        begin += piece.shape[0]
+
+
+def partial_shapes(rows, width):
+    parts = 4 if square() else 1
+    return [jax.ShapeDtypeStruct((rows // parts, width), bf16)] * parts
+
+
+def store_partial(refs, columns, value):
+    value = value.astype(bf16)
+    if len(refs) == 1:
+        refs[0][:, columns] = value
         return
-    own, near, far = pieces
-    mine = own.shape[0]
-    target[:mine, :] = own[...]
-    target[mine : 2 * mine, :] = far[:mine, :]
-    target[2 * mine : 3 * mine, :] = near[...]
-    target[3 * mine :, :] = far[mine:, :]
-
-
-def partial_shapes(rows, width):
-    parts = 2 if square() else 1
-    return [jax.ShapeDtypeStruct((rows // parts, width), bf16)] * parts
-
-
-def store_partial(refs, columns, value):
-    begin = 0
-    for ref in refs:
-        rows = ref.shape[0]
-        ref[:, columns] = value[begin : begin + rows].astype(bf16)
-        begin += rows
-
-
-def add_first_kernel(keep, arrived, own, send):
-    mine = own.shape[0]
-    own[...] = keep[:mine, :].astype(f32) + arrived[:mine, :].astype(f32)
-    send[...] = (keep[mine:, :].astype(f32) + arrived[mine:, :].astype(f32)).astype(bf16)
+    mine = refs[0].shape[0]
+    half = mine // 2
+    own, stay, leave_along, leave_across = refs
+    own[:, columns] = value[:mine]
+    stay[:half, columns] = value[mine : mine + half]
+    stay[half:, columns] = value[2 * mine + half : 3 * mine]
+    leave_along[:half, columns] = value[2 * mine : 2 * mine + half]
+    leave_along[half:, columns] = value[3 * mine : 3 * mine + half]
+    leave_across[:half, columns] = value[mine + half : 2 * mine]
+    leave_across[half:, columns] = value[3 * mine + half :]
+
+
+def add_kernel(left, right, out):
+    out[...] = (left[...].astype(f32) + right[...].astype(f32)).astype(bf16)
+
+
+def add(left, right, vmem=4):
+    (total,) = run(
+        add_kernel, [jax.ShapeDtypeStruct(left.shape, bf16)], left, right, name="add", vmem=vmem
+    )
+    return total
+
+
+def add_halves_kernel(stay, first, second, far, near):
+    half = far.shape[0]
+    far[...] = (stay[:half, :].astype(f32) + first[half:, :].astype(f32)).astype(bf16)
+    near[...] = (stay[half:, :].astype(f32) + second[half:, :].astype(f32)).astype(bf16)
 
 
 def scatter_start(parts, stream):
     if not square():
-        return (lax.psum_scatter(parts[0], "tensor", scatter_dimension=0, tiled=True),)
+        total = lax.psum_scatter(parts[0], "tensor", scatter_dimension=0, tiled=True)
+        return ((total,), ())
     (along, unused), (across, unused) = axes_of(stream)
-    keep, leave = parts
-    rows, width = keep.shape
-    own, send = run(
-        add_first_kernel,
-        [
-            jax.ShapeDtypeStruct((rows // 2, width), f32),
-            jax.ShapeDtypeStruct((rows // 2, width), bf16),
-        ],
-        keep,
-        along(leave),
-        name="add_first",
+    own, stay, leave_along, leave_across = parts
+    half = own.shape[0] // 2
+    first, second = along(leave_along), across(leave_across)
+    far, near = run(
+        add_halves_kernel,
+        [jax.ShapeDtypeStruct((half, own.shape[1]), bf16)] * 2,
+        stay,
+        first,
+        second,
+        name="add_halves",
         vmem=4,
     )
-    return (own, across(send))
+    return ((own, first, second, across(far), along(near)), (far, near))
 
 
 def scattered(pieces):
-    total = pieces[0][...].astype(f32)
-    for piece in pieces[1:]:
-        total = total + piece[...].astype(f32)
-    return total
+    if len(pieces) == 1:
+        return pieces[0][...].astype(f32)
+    own, first, second, far, near = pieces
+    half = far.shape[0]
+    upper = own[:half, :].astype(f32) + first[:half, :].astype(f32) + far[...].astype(f32)
+    lower = own[half:, :].astype(f32) + second[:half, :].astype(f32) + near[...].astype(f32)
+    return jnp.concatenate([upper, lower], axis=0)
 
 
 def gather_columns(block):
@@ -143,8 +179,9 @@
     def piece(distance):
         return lax.dynamic_slice_in_dim(partial, (here ^ distance) * columns, columns, 1)
 
-    arrived = along_x(jnp.stack([piece(1), piece(3)]))
-    return piece(0) + arrived[0] + along_y(piece(2) + arrived[1])
+    arrived = along_x(jnp.stack([piece(1), piece(3)])).astype(f32)
+    passed = along_y((piece(2).astype(f32) + arrived[1]).astype(partial.dtype))
+    return (piece(0).astype(f32) + arrived[0] + passed.astype(f32)).astype(partial.dtype)
 
 
 def gather_dp(block):
@@ -173,16 +210,15 @@
     return [slice(begin, begin + step) for begin in range(0, size, step)]
 
 
-def run(kernel, shapes, *arrays, name, vmem, flops=0, exps=0):
+matmuls = ("qkv", "attend", "feed", "feed_back", "attend_back", "qkv_back")
+
+
+def run(kernel, shapes, *arrays, name, vmem):
     return pl.pallas_call(
         kernel,
         out_shape=tuple(shapes),
         compiler_params=pltpu.CompilerParams(vmem_limit_bytes=vmem * 1024 * 1024),
-        cost_estimate=pl.CostEstimate(
-            flops=flops,
-            bytes_accessed=sum(x.size * x.dtype.itemsize for x in (*arrays, *shapes)),
-            transcendentals=exps,
-        ),
+        cost_estimate=lengthy if name in matmuls else brief,
         name=name,
     )(*arrays)
 
@@ -199,7 +235,7 @@
 
 
 def root_mean(value):
-    return jnp.sqrt(jnp.mean(value * value, axis=1, keepdims=True))
+    return rows_of([jnp.sqrt(jnp.mean(value * value, axis=1, keepdims=True))])
 
 
 def first_kernel(x, member, mod, out):
@@ -228,9 +264,23 @@
     return jnp.transpose(jnp.concatenate([*columns, blank], axis=1))[: len(columns), :]
 
 
+def qkv_first_kernel(count, *refs):
+    pieces, (member, mod, weight, rows, query, keyvalue) = refs[:count], refs[count:]
+    begin = 0
+    for piece in pieces:
+        part = slice(begin, begin + piece.shape[0])
+        first_kernel(piece[...].astype(f32), member[part, :], mod, rows.at[part, :])
+        begin += piece.shape[0]
+    project(rows, weight, query, keyvalue)
+
+
 def qkv_kernel(count, *refs):
     pieces, (weight, rows, query, keyvalue) = refs[:count], refs[count:]
     assemble(pieces, rows)
+    project(rows, weight, query, keyvalue)
+
+
+def project(rows, weight, query, keyvalue):
     size, cols = query.shape
     out = dot_last(rows[...], weight[...]).astype(bf16)
     query[...] = out[:, :cols]
@@ -433,10 +483,54 @@
     sums[:, width:] = slot_sums(member_t, first_grad * normed)
 
 
-def outer(lefts, rights):
-    left = jnp.concatenate(lefts, axis=0)
-    right = jnp.concatenate(rights, axis=0)
-    return jnp.einsum("nd,nf->df", left, right, preferred_element_type=f32).astype(bf16)
+def wide_kernel(count, flag, *refs):
+    seconds, uppers, pres, hiddens = (refs[k * count : (k + 1) * count] for k in range(4))
+    keep, send = refs[4 * count :]
+    first_core = flag[0] == 0
+    for columns in chunks(keep.shape[1]):
+        up = sum(dot_first(a[...], b[:, columns]) for a, b in zip(seconds, pres)).astype(bf16)
+        down = sum(dot_first(a[...], b[:, columns]) for a, b in zip(uppers, hiddens)).astype(bf16)
+        keep[:, columns] = jnp.where(first_core, up, down)
+        send[:, columns] = jnp.where(first_core, down, up)
+
+
+def narrow_kernel(count, flag, *refs):
+    firsts, uppers, grads, mixeds = (refs[k * count : (k + 1) * count] for k in range(4))
+    keep, send = refs[4 * count :]
+    first_core = flag[0] == 0
+    qkv = sum(dot_first(a[...], b[...]) for a, b in zip(firsts, grads)).astype(bf16)
+    proj = sum(dot_first(a[...], b[...]) for a, b in zip(uppers, mixeds)).astype(bf16)
+    cols = proj.shape[1]
+    fill = [jnp.zeros((qkv.shape[0], keep.shape[1] - 2 * cols), bf16)]
+    if not fill[0].shape[1]:
+        fill = []
+    zero = jnp.concatenate([qkv[:, : 2 * cols], *fill], axis=1)
+    one = jnp.concatenate([qkv[:, 2 * cols :], proj, *fill], axis=1)
+    keep[...] = jnp.where(first_core, zero, one)
+    send[...] = jnp.where(first_core, one, zero)
+
+
+def weight_sums(kernel, flag, lefts, rights, width, name):
+    rows, depth = lefts[0].shape
+    step = chunks(depth)[0].stop
+
+    def whole(array):
+        return pl.BlockSpec(array.shape, lambda j: (0, 0))
+
+    return pl.pallas_call(
+        kernel,
+        grid=(depth // step,),
+        in_specs=[
+            pl.BlockSpec(memory_space=pltpu.SMEM),
+            *(pl.BlockSpec((rows, step), lambda j: (0, j)) for unused in lefts),
+            *(whole(array) for array in rights),
+        ],
+        out_specs=[pl.BlockSpec((step, width), lambda j: (j, 0))] * 2,
+        out_shape=[jax.ShapeDtypeStruct((depth, width), bf16)] * 2,
+        compiler_params=pltpu.CompilerParams(vmem_limit_bytes=32 * 1024 * 1024),
+        cost_estimate=lengthy,
+        name=name,
+    )(flag, *lefts, *rights)
 
 
 def three_terms(value):
@@ -533,6 +627,7 @@
     ).astype(f32)
 
     members = jnp.concatenate([member] * 3, axis=2).astype(bf16)
+    row_members = jnp.concatenate([row_member] * 3, axis=2).astype(bf16)
     members_t = jnp.transpose(member, (0, 2, 1)).astype(bf16)
     row_count = row_labels.shape[1]
     padded = -(-2 * hc // 128) * 128
@@ -542,38 +637,49 @@
         return jax.ShapeDtypeStruct((rows, cols), kind)
 
     latest = [None]
+    begun = []
 
     def after(arrays):
         if latest[0] is None:
             return arrays
-        return lax.optimization_barrier((arrays, latest[0]))[0]
+        settled = begun[-2] if len(begun) >= 2 else ()
+        return lax.optimization_barrier((arrays, latest[0], settled))[0]
 
     def ends(array):
         latest[0] = array
+
+    def begins(pieces, first):
+        begun.append(first)
+        return pieces
 
     def stream(i, x, g, results):
         of_mine = shape(mine, width, f32)
         low_mine = shape(mine, width, bf16)
         low_rows = shape(row_count, width, bf16)
-        column = shape(mine, 1, f32)
+        row_shape = shape(1, mine, f32)
         terms = partial_shapes(row_count, width)
         tokens, tokens_t = members[i], members_t[i]
         kept = []
-        (first_mine,) = run(first_kernel, [low_mine], x, tokens, mod[0][i], name="first", vmem=4)
-        ends(first_mine)
+        first_mine = x
+        x = x.astype(f32)
+        g = g.astype(f32)
         for b in range(2):
-            pieces = gather_start(first_mine, i)
+            pieces = begins(*gather_start(first_mine, i))
             yield
             pieces = after(pieces)
+            more = [row_members[i], mod[0][i]] if b == 0 else []
             first, query, keyvalue = run(
-                functools.partial(qkv_kernel, len(pieces)),
+                functools.partial(qkv_kernel if more == [] else qkv_first_kernel, len(pieces)),
                 [low_rows, shape(row_count, hc, bf16), shape(row_count, padded, bf16)],
                 *pieces,
+                *more,
                 wqkv[b],
-                name="qkv", vmem=8,
-                flops=6 * row_count * width * hc,
+                name="qkv", vmem=10,
             )
-            other = swap_cores(keyvalue)
+            ends(query)
+            other = begins(swap_cores(keyvalue), ())
+            yield
+            other = after(other)
             mixed, lse, *parts = run(
                 functools.partial(attention_forward_kernel, heads),
                 [shape(row_count, hc, bf16), shape(heads, row_count, f32), *terms],
@@ -583,17 +689,15 @@
                 key_labels[i][None, :],
                 head_gate[i],
                 wproj[b],
-                name="attend", vmem=24,
-                flops=8 * row_count * row_count * hc + 2 * row_count * hc * width,
-                exps=2 * row_count * row_count * heads,
+                name="attend", vmem=10,
             )
             ends(mixed)
-            pieces = scatter_start(parts, i)
+            pieces = begins(*scatter_start(parts, i))
             yield
             pieces = after(pieces)
             attended, middle, second_mine, rms_attended = run(
                 functools.partial(after_attention_kernel, len(pieces)),
-                [of_mine, of_mine, low_mine, column],
+                [of_mine, of_mine, low_mine, row_shape],
                 *pieces,
                 x,
                 tokens,
@@ -601,7 +705,7 @@
                 name="after_attend", vmem=6,
             )
             ends(second_mine)
-            pieces = gather_start(second_mine, i)
+            pieces = begins(*gather_start(second_mine, i))
             yield
             pieces = after(pieces)
             second, hidden, slope, *parts = run(
@@ -616,19 +720,17 @@
                 wup[b],
                 wdown[b],
                 skip[i][None, :],
-                name="feed", vmem=12,
-                flops=4 * row_count * width * hidden_cols,
-                exps=row_count * hidden_cols,
+                name="feed", vmem=7,
             )
             ends(hidden)
-            pieces = scatter_start(parts, i)
+            pieces = begins(*scatter_start(parts, i))
             yield
             pieces = after(pieces)
             x_in_block = x
             if b == 0:
                 feed, x, rms_feed, first_mine = run(
                     functools.partial(after_feed_kernel, len(pieces), False),
-                    [of_mine, of_mine, column, low_mine],
+                    [of_mine, of_mine, row_shape, low_mine],
                     *pieces,
                     middle,
                     tokens,
@@ -639,7 +741,7 @@
             else:
                 feed, x, rms_feed = run(
                     functools.partial(after_feed_kernel, len(pieces), True),
-                    [of_mine, of_mine, column],
+                    [of_mine, of_mine, row_shape],
                     *pieces,
                     middle,
                     tokens,
@@ -658,9 +760,11 @@
         for b in (1, 0):
             x, first, query, keyvalue, other, lse, mixed, attended, middle = kept[b][:9]
             second, hidden, slope, feed = kept[b][9:]
-            pieces = gather_start(feed_mine, i)
+            pieces = begins(*gather_start(feed_mine, i))
             yield
             pieces = after(pieces)
+            for name, array in dict(second=second, hidden=hidden, first=first, mixed=mixed).items():
+                results[name, b, i] = array
             feed_rows, pre_grad, *parts = run(
                 functools.partial(feed_back_kernel, len(pieces)),
                 [low_rows, shape(row_count, hidden_cols, bf16), *terms],
@@ -668,11 +772,12 @@
                 wup[b],
                 wdown[b],
                 slope,
-                name="feed_back", vmem=12,
-                flops=4 * row_count * width * hidden_cols,
+                name="feed_back", vmem=7,
             )
             ends(pre_grad)
-            pieces = scatter_start(parts, i)
+            results["feed_rows", b, i] = feed_rows
+            results["pre_grad", b, i] = pre_grad
+            pieces = begins(*scatter_start(parts, i))
             yield
             pieces = after(pieces)
             middle_grad, attn_mine, sums_two = run(
@@ -689,7 +794,7 @@
                 name="after_feed_back", vmem=8,
             )
             ends(attn_mine)
-            pieces = gather_start(attn_mine, i)
+            pieces = begins(*gather_start(attn_mine, i))
             yield
             pieces = after(pieces)
             attn_rows, query_grad, own_grad, other_grad = run(
@@ -708,22 +813,25 @@
                 key_labels[i][None, :],
                 head_gate[i],
                 lse,
-                name="attend_back", vmem=32,
-                flops=20 * row_count * row_count * hc + 2 * row_count * hc * width,
-                exps=2 * row_count * row_count * heads,
+                name="attend_back", vmem=14,
             )
+            ends(query_grad)
+            arrived = begins(swap_cores(other_grad), ())
+            yield
+            arrived = after(arrived)
             qkv_grad, *parts = run(
                 qkv_back_kernel,
                 [shape(row_count, 3 * hc, bf16), *terms],
                 query_grad,
                 own_grad,
-                swap_cores(other_grad),
+                arrived,
                 wqkv[b],
-                name="qkv_back", vmem=8,
-                flops=6 * row_count * width * hc,
+                name="qkv_back", vmem=5,
             )
             ends(qkv_grad)
-            pieces = scatter_start(parts, i)
+            results["attn_rows", b, i] = attn_rows
+            results["qkv_grad", b, i] = qkv_grad
+            pieces = begins(*scatter_start(parts, i))
             yield
             pieces = after(pieces)
             if b == 1:
@@ -754,56 +862,80 @@
             ends(g)
             results["grad", b, i] = g
             results["mod", b, i] = jnp.concatenate([sums_one, sums_two], axis=1)
-            results["pairs", b, i] = (
-                second, pre_grad, feed_rows, hidden, first, qkv_grad, attn_rows, mixed
-            )
-
-    def weight_sums(b):
-        second, pre_grad, feed_rows, hidden, first, qkv_grad, attn_rows, mixed = zip(
-            *(results["pairs", b, i] for i in range(micro))
+
+    flag = section.astype(jnp.int32)[None]
+
+    def summed(kernel, name, b, lefts, rights, cols):
+        lefts = [array for group in lefts for array in collected(group, b)]
+        rights = [array for group in rights for array in collected(group, b)]
+        lefts, rights = after((lefts, rights))
+        keep, send = weight_sums(
+            functools.partial(kernel, micro), flag, lefts, rights, cols, name
         )
-        up = outer(second, pre_grad)
-        down = outer(feed_rows, hidden)
-        proj = outer(attn_rows, mixed)
-        qkv = outer(first, qkv_grad)
-
-        def reduced(zero, one):
-            total = choose(zero, one).astype(f32) + swap_cores(choose(one, zero)).astype(f32)
-            return lax.psum_scatter(total.astype(bf16), "dp", scatter_dimension=0, tiled=True)
-
-        wide = reduced(up, down)
-        fill = ((0, 0), (0, padded - 2 * hc))
-        narrow = reduced(
-            jnp.pad(qkv[:, : 2 * hc], fill),
-            jnp.pad(jnp.concatenate([qkv[:, 2 * hc :], proj], axis=1), fill),
+        ends(keep)
+        results[name, b] = (keep, swap_cores(send))
+
+    def reduced(name, b):
+        if (name, b) == ("narrow", 0):
+            total = add(*results[name, b], vmem=12)
+        else:
+            total = add(*after(results[name, b]), vmem=12)
+            ends(total)
+        results[name, b] = lax.psum_scatter(total, "dp", scatter_dimension=0, tiled=True)
+
+    def wide(b):
+        summed(
+            wide_kernel, "wide", b, ("second", "feed_rows"), ("pre_grad", "hidden"), hidden_cols
         )
-        return (wide, narrow)
+
+    def narrow(b):
+        summed(
+            narrow_kernel, "narrow", b, ("first", "attn_rows"), ("qkv_grad", "mixed"), padded
+        )
 
     def my_rows(array):
         block = lax.dynamic_slice_in_dim(array, section * mine, mine, 1)
-        return [block[i].astype(f32) for i in range(micro)]
+        return [block[i] for i in range(micro)]
 
     results = {}
+
+    def collected(name, b):
+        return [results[name, b, i] for i in range(micro)]
+
     xs = my_rows(x_in)
     gs = my_rows(cotangent)
     running = [stream(i, xs[i], gs[i], results) for i in range(micro)]
-    while running:
-        running = [s for s in running if next(s, "ended") != "ended"]
-
-    def collected(name, b):
-        return [results[name, b, i] for i in range(micro)]
-
+    extra = {12: (wide, 1), 15: (narrow, 1), 17: (wide, 0)}
+    ready = {13: ("wide", 1), 16: ("narrow", 1), 18: ("wide", 0)}
+    settled = {16: ("wide", 1), 19: ("narrow", 1)}
+    for step in range(21):
+        for i, one in enumerate(running):
+            if step == 20 and i == 0:
+                narrow(0)
+            if step < 21:
+                next(one, None)
+            behind = step
+            if i == 0 and behind in ready:
+                reduced(*ready[behind])
+            if i == micro - 1 and behind in extra:
+                work, b = extra[behind]
+                work(b)
+            if i == 0 and behind in settled:
+                ends((latest[0], results[settled[behind]]))
+
+    reduced("narrow", 0)
     out_zero, out_one = collected("out", 0), collected("out", 1)
     back_zero, back_one = collected("grad", 0), collected("grad", 1)
     rms_zero, rms_one = (
-        jnp.concatenate([column for pair in collected("rms", b) for column in pair], axis=1)
-        .T.reshape(micro, 2, mine)
-        .transpose(1, 0, 2)
+        jnp.stack(
+            [jnp.concatenate([pair[k] for pair in collected("rms", b)]) for k in range(2)]
+        )
         for b in range(2)
     )
     mods_zero, mods_one = (jnp.concatenate(collected("mod", b), axis=0) for b in range(2))
-    weights_one = weight_sums(1)
-    weights_zero = weight_sums(0)
+    weights_zero, weights_one = (
+        (results["wide", b], results["narrow", b]) for b in range(2)
+    )
 
     residual = jnp.concatenate(to_owner(jnp.stack(out_zero), jnp.stack(out_one)), axis=1)
     input_grad = jnp.concatenate(
@@ -812,12 +944,14 @@
     sublayer_rms = jnp.concatenate(to_owner(rms_zero, rms_one), axis=2)
 
     mod_sum = choose(mods_zero, mods_one) + swap_cores(choose(mods_one, mods_zero))
-    mod_all = gather_dp(scatter_columns(mod_sum))
+    mod_here = scatter_columns(mod_sum.astype(bf16))
+    mod_here = lax.optimization_barrier((mod_here, results["wide", 0]))[0]
+    mod_all = gather_dp(mod_here)
     condition_all = gather_dp(flat_condition)
     rows_here = width // lax.axis_size("dp")
     condition_here = lax.dynamic_slice_in_dim(condition_all, dp_index * rows_here, rows_here, 2)
     ada_grad = jnp.einsum(
-        "psd,pse->de", condition_here.astype(f32), mod_all, precision=highest
+        "psd,pse->de", condition_here, mod_all, preferred_element_type=f32
     )
 
     wide, narrow = (

time: 974 us -> 829 us (0.85)
  waiting for transfers between devices: 438 us -> 178 us
  starting transfers between devices: 120 us -> 219 us
  Pallas kernels: 207 us -> 284 us
  matrix products: 47.9 us -> 7 us
  other arithmetic: 57.6 us -> 32.7 us
    ppermute x50 -> x98, waiting for transfers between devices: 212 us -> 86.6 us  [along_y(): return lax.ppermute(block, 'tensor', [(0, 2), (2, 0), (1, 3), (3, 1)])]
    ppermute x51 -> x99, waiting for transfers between devices: 181 us -> 62.4 us  [along_x(): return lax.ppermute(block, 'tensor', [(0, 1), (1, 0), (2, 3), (3, 2)])]
    ppermute x51 -> x99, starting transfers between devices: 51.8 us -> 105 us  [along_x(): return lax.ppermute(block, 'tensor', [(0, 1), (1, 0), (2, 3), (3, 2)])]
    ppermute x50 -> x98, starting transfers between devices: 56 us -> 101 us  [along_y(): return lax.ppermute(block, 'tensor', [(0, 2), (2, 0), (1, 3), (3, 1)])]
    dot_general x9 -> x1, matrix products: 44.3 us -> 2.63 us  [on_device(): jnp.einsum('psd,pse->de', condition_here, mod_all, preferred_element_type...]
    pallas_call x0 -> x4, Pallas kernels: none -> 40.4 us  [weight_sums(): pl.pallas_call(kernel, grid=(depth // step,), in_specs=[pl.BlockSpec(memo...]
    pallas_call x90 -> x115, Pallas kernels: 207 us -> 244 us  [run(): pl.pallas_call(kernel, out_shape=tuple(shapes), compiler_params=pltpu.Com...]
    ppermute x6, waiting for transfers between devices: 32.5 us -> 1.62 us  [gather_dp(): lax.ppermute(block, 'dp', [(i, (i + step) % size) for i in range(size)])]
  transfers between devices with their start and end apart: 138 -> 234, of which waited for: 63 -> 62; matrix products, arithmetic and copies ran while one was open for 12% -> 5% of each run, Pallas kernels for 20% -> 33%
where the time goes in v3:
time: 829 us; the launch traced here: 819 us
  Pallas kernels  284 us (34%)
  starting transfers between devices  219 us (26%)
  waiting for transfers between devices  178 us (21%)
  local copies, waits for them, and re-layouts  78.6 us (9%)
  other arithmetic  32.7 us (4%)
  between operations  18.8 us (2%)
    pallas_call x115, Pallas kernels, run(): pl.pallas_call(kernel, out_shape=tuple(shapes), compiler_params=pltpu.Com...  244 us
    ppermute x99, starting transfers between devices, along_x(): return lax.ppermute(block, 'tensor', [(0, 1), (1, 0), (2, 3), (3, 2)])  105 us
    ppermute x98, starting transfers between devices, along_y(): return lax.ppermute(block, 'tensor', [(0, 2), (2, 0), (1, 3), (3, 1)])  101 us
    ppermute x98, waiting for transfers between devices, along_y(): return lax.ppermute(block, 'tensor', [(0, 2), (2, 0), (1, 3), (3, 1)])  86.6 us
    unnamed x756, local copies, waits for them, and re-layouts  72.5 us
    ppermute x99, waiting for transfers between devices, along_x(): return lax.ppermute(block, 'tensor', [(0, 1), (1, 0), (2, 3), (3, 2)])  62.4 us
    pallas_call x4, Pallas kernels, weight_sums(): pl.pallas_call(kernel, grid=(depth // step,), in_specs=[pl.BlockSpec(memo...  40.4 us
    reduce_scatter x4, waiting for transfers between devices, reduced(): lax.psum_scatter(total, 'dp', scatter_dimension=0, tiled=True)  27.2 us
  transfers between devices with their start and end apart: 234, of which 62 were waited for; matrix products, arithmetic and copies ran while one was open for 5% of the time, Pallas kernels for 33%

profile of v3, /device:TPU:0, one launch (start us, length us, event | category | flops | bytes accessed | tf_op | source)
XLA Modules:
  0.0 818.6 jit_solution(8402292107551542190)
XLA Ops:
  7.2 4.2 fusion
  11.4 3.0 collective-permute-start.5
  56.9 3.7 qkv.6
  63.1 2.7 qkv.7
  67.4 4.0 qkv.8
  71.5 8.5 %attend.6 = (bf16[512,288]{1,0:T(8,128)(2,1)S(1)}, f32[4,512]{1,0:T(4,128)S(1)}, bf16[128,1152]{1,0:T(8,128)(2,1)S(1)}, bf16[128,1152]{1,0:T(8,128)(2,1)S(1)}, b...) custom-call(bf16[512,288]{1,0:T(8,128)(2,1)S(1)} %get-tuple-element.680.query_ref.refs_6_, ...), custom_call_target="tpu_custom_call" | custom-call | flops 12000000000 | bytes 1 | tf_op jit(solution)/shard_map/attend/pallas_call | solution.py:217
  82.0 8.7 %attend.7 = (bf16[512,288]{1,0:T(8,128)(2,1)S(1)}, f32[4,512]{1,0:T(4,128)S(1)}, bf16[128,1152]{1,0:T(8,128)(2,1)S(1)}, bf16[128,1152]{1,0:T(8,128)(2,1)S(1)}, b...) custom-call(bf16[512,288]{1,0:T(8,128)(2,1)S(1)} %get-tuple-element.691.query_ref.refs_6_, ...), custom_call_target="tpu_custom_call" | custom-call | flops 12000000000 | bytes 1 | tf_op jit(solution)/shard_map/attend/pallas_call | solution.py:217
  93.8 8.5 %attend.8 = (bf16[512,288]{1,0:T(8,128)(2,1)S(1)}, f32[4,512]{1,0:T(4,128)S(1)}, bf16[128,1152]{1,0:T(8,128)(2,1)S(1)}, bf16[128,1152]{1,0:T(8,128)(2,1)S(1)}, b...) custom-call(bf16[512,288]{1,0:T(8,128)(2,1)S(1)} %get-tuple-element.697.query_ref.refs_6_, ...), custom_call_target="tpu_custom_call" | custom-call | flops 12000000000 | bytes 1 | tf_op jit(solution)/shard_map/attend/pallas_call | solution.py:217
  106.0 3.2 collective-permute-done.22.refs_4_
  117.4 4.9 collective-permute-done.32.second.refs_2_
  132.6 5.4 collective-permute-done.33.refs_3_
  145.1 5.0 feed.6
  154.6 5.0 feed.7
  165.0 5.4 feed.8
  176.5 4.6 collective-permute-done.55.first.refs_1_
  181.4 3.0 collective-permute-done.53.refs_3_
  193.0 5.7 collective-permute-done.57.refs_3_
  220.1 8.7 %attend.9 = (bf16[512,288]{1,0:T(8,128)(2,1)S(1)}, f32[4,512]{1,0:T(4,128)S(1)}, bf16[128,1152]{1,0:T(8,128)(2,1)S(1)}, bf16[128,1152]{1,0:T(8,128)(2,1)S(1)}, b...) custom-call(bf16[512,288]{1,0:T(8,128)(2,1)S(1)} %get-tuple-element.816.query_ref.refs_6_, ...), custom_call_target="tpu_custom_call" | custom-call | flops 12000000000 | bytes 1 | tf_op jit(solution)/shard_map/attend/pallas_call | solution.py:217
  230.7 8.8 %attend.10 = (bf16[512,288]{1,0:T(8,128)(2,1)S(1)}, f32[4,512]{1,0:T(4,128)S(1)}, bf16[128,1152]{1,0:T(8,128)(2,1)S(1)}, bf16[128,1152]{1,0:T(8,128)(2,1)S(1)}, ...) custom-call(bf16[512,288]{1,0:T(8,128)(2,1)S(1)} %get-tuple-element.826.query_ref.refs_6_, ...), custom_call_target="tpu_custom_call" | custom-call | flops 12000000000 | bytes 1 | tf_op jit(solution)/shard_map/attend/pallas_call | solution.py:217
  245.7 3.8 collective-permute-done.78.first.refs_1_
  251.8 8.6 %attend.11 = (bf16[512,288]{1,0:T(8,128)(2,1)S(1)}, f32[4,512]{1,0:T(4,128)S(1)}, bf16[128,1152]{1,0:T(8,128)(2,1)S(1)}, bf16[128,1152]{1,0:T(8,128)(2,1)S(1)}, ...) custom-call(bf16[512,288]{1,0:T(8,128)(2,1)S(1)} %get-tuple-element.832.query_ref.refs_6_, ...), custom_call_target="tpu_custom_call" | custom-call | flops 12000000000 | bytes 1 | tf_op jit(solution)/shard_map/attend/pallas_call | solution.py:217
  267.5 5.0 collective-permute-done.88.refs_3_
  274.0 6.0 collective-permute-done.89.refs_4_
  286.3 6.8 collective-permute-done.113.refs_3_
  297.6 2.9 collective-permute-done.86.refs_3_
  301.9 3.2 collective-permute-done.87.refs_4_
  313.0 5.0 feed.9
  319.5 4.1 feed_back.6
  328.4 5.0 feed.10
  333.4 2.8 collective-permute-done.92.first.refs_1_
  337.5 4.1 feed_back.7
  349.2 5.0 feed.11
  359.6 4.1 feed_back.8
  363.7 3.6 collective-permute-done.94.refs_3_
  374.3 12.8 %collective-permute-done.138.refs_4_ = bf16[64,1152]{1,0:T(8,128)(2,1)S(1)} collective-permute-done((bf16[64,1152]{1,0:T(8,128)(2,1)S(1)}, bf16[64,1152]{1,0:T(8,128)(2,1)S(1)}, u32[]{:S(2)}, u32[]{:S(2)}) %collective-permute-start.138) | collective-permute-done | bytes 147488 | tf_op jit(solution)/shard_map/ppermute | solution.py:43
  409.3 12.8 %wide.2 = (bf16[1152,1152]{1,0:T(8,128)(2,1)S(1)}, bf16[1152,1152]{1,0:T(8,128)(2,1)S(1)}) custom-call(s32[1]{0:T(128)} %bitcast.62.flag, bf16[512,1152]{1,0:T(8,128)(2,1)S(1)} %get-tuple-element.1019.refs_0_, bf16[512,1152]{1,0:T(8,128)(2,1)S(1)} %get-tuple-element.1020.refs_1_, bf16[512,1152]{1,0:T(8,128)(2,1)S(1)} %get-tuple-element.1021.refs_2_, ...), custom_call_target="tpu_custom_call" | custom-call | flops 12000000000 | bytes 1 | tf_op jit(solution)/shard_map/wide/pallas_call | solution.py:520
  431.2 8.6 %attend_back.6 = (bf16[512,1152]{1,0:T(8,128)(2,1)S(1)}, bf16[512,288]{1,0:T(8,128)(2,1)S(1)}, f32[512,576]{1,0:T(8,128)S(1)}, bf16[512,640]{1,0:T(8,128)(2,1)}) custom-call(bf16[128,1152]{1,0:T(8,128)(2,1)S(1)} %get-tuple-element.1032.refs_0_, bf16[128,1152]{1,0:T(8,128)(2,1)S(1)} %collective-permute-done.129.far.refs_1_, ...), custom_call_target="tpu_custom_call" | custom-call | flops 12000000000 | bytes 1 | tf_op jit(solution)/shard_map/attend_back/pallas_call | solution.py:217
  447.8 10.0 %attend_back.7 = (bf16[512,1152]{1,0:T(8,128)(2,1)S(1)}, bf16[512,288]{1,0:T(8,128)(2,1)S(1)}, f32[512,576]{1,0:T(8,128)S(1)}, bf16[512,640]{1,0:T(8,128)(2,1)}) custom-call(bf16[128,1152]{1,0:T(8,128)(2,1)S(1)} %copy-done.199, bf16[128,1152]{1,0:T(8,128)(2,1)S(1)} %copy-done.213, bf16[128,1152]{1,0:T(8,128)(2,1)S(1)} %collective-permute-done.139.near.refs_2_, ...), custom_call_target="tpu_custom_call" | custom-call | flops 12000000000 | bytes 1 | tf_op jit(solution)/shard_map/attend_back/pallas_call | solution.py:217
  460.8 9.5 %attend_back.8 = (bf16[512,1152]{1,0:T(8,128)(2,1)S(1)}, bf16[512,288]{1,0:T(8,128)(2,1)S(1)}, f32[512,576]{1,0:T(8,128)S(1)}, bf16[512,640]{1,0:T(8,128)(2,1)S(1)}) custom-call(bf16[128,1152]{1,0:T(8,128)(2,1)S(1)} %copy-done.215, bf16[128,1152]{1,0:T(8,128)(2,1)S(1)} %copy-done.219, bf16[128,1152]{1,0:T(8,128)(2,1)S(1)} %copy-done.223, ...), custom_call_target="tpu_custom_call" | custom-call | flops 12000000000 | bytes 1 | tf_op jit(solution)/shard_map/attend_back/pallas_call | solution.py:217
  470.5 4.3 qkv_back.6
  480.9 5.3 collective-permute-done.149.first.refs_1_
  491.5 3.0 qkv_back.7
  502.7 2.8 collective-permute-done.156.second.refs_2_
  527.2 3.3 collective-permute-done.167.near.refs_2_
  532.5 7.3 narrow.2
  540.0 4.1 feed_back.9
  553.2 3.4 collective-permute-done.169.first.refs_1_
  569.5 5.2 feed_back.10
  576.8 5.2 feed_back.11
  598.5 3.4 collective-permute-done.182.far.refs_1_
  608.3 2.7 collective-permute-done.192.near.refs_2_
  612.6 13.3 %wide.3 = (bf16[1152,1152]{1,0:T(8,128)(2,1)S(1)}, bf16[1152,1152]{1,0:T(8,128)(2,1)}) custom-call(s32[1]{0:T(128)} %bitcast.62.flag, bf16[512,1152]{1,0:T(8,128)(2,1)S(1)} %copy-done.240, bf16[512,1152]{1,0:T(8,128)(2,1)S(1)} %copy-done.244, bf16[512,1152]{1,0:T(8,128)(2,1)S(1)} %copy-done.248, bf16[512,1152]{1,0:T(8,128)(2,1)S(1)} %copy-done.252, ...), custom_call_target="tpu_custom_call" | custom-call | flops 12000000000 | bytes 1 | tf_op jit(solution)/shard_map/wide/pallas_call | solution.py:520
  632.8 3.0 collective-permute-done.184.refs_3_
  646.0 9.7 %attend_back.9 = (bf16[512,1152]{1,0:T(8,128)(2,1)S(1)}, bf16[512,288]{1,0:T(8,128)(2,1)S(1)}, f32[512,576]{1,0:T(8,128)S(1)}, bf16[512,640]{1,0:T(8,128)(2,1)}) custom-call(bf16[128,1152]{1,0:T(8,128)(2,1)S(1)} %copy-done.181, bf16[128,1152]{1,0:T(8,128)(2,1)S(1)} %copy-done.191, bf16[128,1152]{1,0:T(8,128)(2,1)S(1)} %copy-done.203, ...), custom_call_target="tpu_custom_call" | custom-call | flops 12000000000 | bytes 1 | tf_op jit(solution)/shard_map/attend_back/pallas_call | solution.py:217
  659.3 3.9 add.422
  672.4 10.0 %attend_back.10 = (bf16[512,1152]{1,0:T(8,128)(2,1)S(1)}, bf16[512,288]{1,0:T(8,128)(2,1)S(1)}, f32[512,576]{1,0:T(8,128)S(1)}, bf16[512,640]{1,0:T(8,128)(2,1)}) custom-call(bf16[128,1152]{1,0:T(8,128)(2,1)S(1)} %copy-done.183, bf16[128,1152]{1,0:T(8,128)(2,1)S(1)} %copy-done.195, bf16[128,1152]{1,0:T(8,128)(2,1)S(1)} %copy-done.189, ...), custom_call_target="tpu_custom_call" | custom-call | flops 12000000000 | bytes 1 | tf_op jit(solution)/shard_map/attend_back/pallas_call | solution.py:217
  685.4 9.2 %attend_back.11 = (bf16[512,1152]{1,0:T(8,128)(2,1)S(1)}, bf16[512,288]{1,0:T(8,128)(2,1)S(1)}, f32[512,576]{1,0:T(8,128)S(1)}, bf16[512,640]{1,0:T(8,128)(2,1)S(1)}) custom-call(bf16[128,1152]{1,0:T(8,128)(2,1)S(1)} %copy-done.197, bf16[128,1152]{1,0:T(8,128)(2,1)S(1)} %copy-done.217, bf16[128,1152]{1,0:T(8,128)(2,1)S(1)} %copy-done.221, ...), custom_call_target="tpu_custom_call" | custom-call | flops 12000000000 | bytes 1 | tf_op jit(solution)/shard_map/attend_back/pallas_call | solution.py:217
  694.8 4.3 qkv_back.9
  704.5 6.6 collective-permute-done.202.first.refs_1_
  722.9 3.0 qkv_back.11
  732.4 7.1 narrow.3
  745.9 2.7 collective-permute-start.219
  760.1 3.6 maximum_bitcast_fusion
  771.9 27.2 %reduce-scatter.11.cloned.1.call-done = bf16[288,640]{1,0:T(8,128)(2,1)} async-done(((bf16[1152,640]{1,0:T(8,128)(2,1)}), bf16[288,640]{1,0:T(8,128)(2,1)}) %reduce-scatter.11.cloned.1.call-update) | async-done | bytes 368656 | tf_op jit(solution)/shard_map/reduce_scatter | solution.py:884
  (1370 shorter events, 419.4 us)
Async XLA Ops:
  7.2 556.4 %reduce-scatter.5.cloned.1.call-start = ((), (), s32[]{:S(2)}) async-start(), calls=%async_computation.4 | async-start | bytes 3317760 | tf_op jit(solution)/shard_map/reduce_scatter | solution.py:884
  11.4 16.4 %collective-permute-start.5 = (f32[24,1728]{1,0:T(8,128)}, f32[24,1728]{1,0:T(8,128)}, u32[]{:S(2)}, u32[]{:S(2)}) collective-permute-start(f32[24,1728]{1,0:T(8,128)} %fusion), channel_id=1, source_target_pairs={{0,8},{8,0},{4,12},{12,4},{1,9},{9,1},{5,13},{13,5},{2,10},{10,2},... | collective-permute-start | bytes 497672 | tf_op jit(solution)/shard_map/ppermute | solution.py:43
  14.4 19.9 %collective-permute-start.4 = (f32[24,1728]{1,0:T(8,128)}, f32[24,1728]{1,0:T(8,128)}, u32[]{:S(2)}, u32[]{:S(2)}) collective-permute-start(f32[24,1728]{1,0:T(8,128)} %fusion), channel_id=1, source_target_pairs={{0,4},{4,0},{8,12},{12,8},{1,5},{5,1},{9,13},{13,9},{2,6},{6,2},{1... | collective-permute-start | bytes 497672 | tf_op jit(solution)/shard_map/ppermute | solution.py:39
  17.7 21.9 %collective-permute-start.10 = (bf16[128,1152]{1,0:T(8,128)(2,1)S(1)}, bf16[128,1152]{1,0:T(8,128)(2,1)S(1)}, u32[]{:S(2)}, u32[]{:S(2)}) collective-permute-start(bf16[128,1152]{1,0:T(8,128)(2,1)S(1)} %get-tuple-element.692.refs_0_), channel_id=1, source_target_pairs={{0,8},{8,0},{4,12},{12,4},{1,9},{9,1},{5,13},{13,5},{2,10},{10,2},... | collective-permute-start | bytes 884744 | tf_op jit(solution)/shard_map/ppermute | solution.py:43
  45.5 67.2 %collective-permute-start.40 = (bf16[1152,1152]{1,0:T(8,128)(2,1)S(1)}, bf16[1152,1152]{1,0:T(8,128)(2,1)S(1)}, u32[]{:S(2)}, u32[]{:S(2)}) collective-permute-start(bf16[1152,1152]{1,0:T(8,128)(2,1)S(1)} %bitcast.209), channel_id=1, source_target_pairs={{0,16},{16,0},{1,17},{17,1},{2,18},{18,2},{3,19},{19,3},{4,20},{20... | collective-permute-start | bytes 7962632 | tf_op jit(solution)/shard_map/ppermute | solution.py:35
  45.5 82.5 %collective-permute-start.39 = (bf16[1152,1152]{1,0:T(8,128)(2,1)}, bf16[1152,1152]{1,0:T(8,128)(2,1)S(1)}, u32[]{:S(2)}, u32[]{:S(2)}) collective-permute-start(bf16[1152,1152]{1,0:T(8,128)(2,1)} %bitcast.210), channel_id=1, source_target_pairs={{0,16},{16,0},{1,17},{17,1},{2,18},{18,2},{3,19},{19,3},{4,20},{20... | collective-permute-start | bytes 7962632 | tf_op jit(solution)/shard_map/ppermute | solution.py:35
  71.4 21.8 %collective-permute-start.23 = (bf16[512,640]{1,0:T(8,128)(2,1)S(1)}, bf16[512,640]{1,0:T(8,128)(2,1)S(1)}, u32[]{:S(2)}, u32[]{:S(2)}) collective-permute-start(bf16[512,640]{1,0:T(8,128)(2,1)S(1)} %get-tuple-element.705.own_ref.refs_7_), channel_id=1, source_target_pairs={{0,16},{16,0},{1,17},{17,1},{2,18},{18,2},{3,19},{19,3},{4,20},{20... | collective-permute-start | bytes 1966088 | tf_op jit(solution)/shard_map/ppermute | solution.py:35
  104.6 19.0 %collective-permute-start.35 = (bf16[64,1152]{1,0:T(8,128)(2,1)S(1)}, bf16[64,1152]{1,0:T(8,128)(2,1)S(1)}, u32[]{:S(2)}, u32[]{:S(2)}) collective-permute-start(bf16[64,1152]{1,0:T(8,128)(2,1)S(1)} %get-tuple-element.715), channel_id=1, source_target_pairs={{0,4},{4,0},{8,12},{12,8},{1,5},{5,1},{9,13},{13,9},{2,6},{6,2},{1... | collective-permute-start | bytes 442376 | tf_op jit(solution)/shard_map/ppermute | solution.py:39
  185.8 15.9 %collective-permute-start.63 = (bf16[128,1152]{1,0:T(8,128)(2,1)S(1)}, bf16[128,1152]{1,0:T(8,128)(2,1)S(1)}, u32[]{:S(2)}, u32[]{:S(2)}) collective-permute-start(bf16[128,1152]{1,0:T(8,128)(2,1)S(1)} %get-tuple-element.821.refs_0_), channel_id=1, source_target_pairs={{0,8},{8,0},{4,12},{12,4},{1,9},{9,1},{5,13},{13,5},{2,10},{10,2},... | collective-permute-start | bytes 884744 | tf_op jit(solution)/shard_map/ppermute | solution.py:43
  191.9 52.7 %collective-permute-start.110 = (bf16[128,1152]{1,0:T(8,128)(2,1)S(1)}, bf16[128,1152]{1,0:T(8,128)(2,1)S(1)}, u32[]{:S(2)}, u32[]{:S(2)}) collective-permute-start(bf16[128,1152]{1,0:T(8,128)(2,1)S(1)} %upstream.3.refs_0_), channel_id=1, source_target_pairs={{0,4},{4,0},{8,12},{12,8},{1,5},{5,1},{9,13},{13,9},{2,6},{6,2},{1... | collective-permute-start | bytes 884744 | tf_op jit(solution)/shard_map/ppermute | solution.py:39
  220.0 23.4 %collective-permute-start.76 = (bf16[512,640]{1,0:T(8,128)(2,1)S(1)}, bf16[512,640]{1,0:T(8,128)(2,1)S(1)}, u32[]{:S(2)}, u32[]{:S(2)}) collective-permute-start(bf16[512,640]{1,0:T(8,128)(2,1)S(1)} %get-tuple-element.840.own_ref.refs_7_), channel_id=1, source_target_pairs={{0,16},{16,0},{1,17},{17,1},{2,18},{18,2},{3,19},{19,3},{4,20},{20... | collective-permute-start | bytes 1966088 | tf_op jit(solution)/shard_map/ppermute | solution.py:35
  242.4 18.7 %collective-permute-start.111 = (bf16[128,1152]{1,0:T(8,128)(2,1)S(1)}, bf16[128,1152]{1,0:T(8,128)(2,1)S(1)}, u32[]{:S(2)}, u32[]{:S(2)}) collective-permute-start(bf16[128,1152]{1,0:T(8,128)(2,1)S(1)} %upstream.3.refs_0_), channel_id=1, source_target_pairs={{0,8},{8,0},{4,12},{12,4},{1,9},{9,1},{5,13},{13,5},{2,10},{10,2},... | collective-permute-start | bytes 884744 | tf_op jit(solution)/shard_map/ppermute | solution.py:43
  243.3 18.8 %collective-permute-start.115 = (bf16[128,1152]{1,0:T(8,128)(2,1)S(1)}, bf16[128,1152]{1,0:T(8,128)(2,1)S(1)}, u32[]{:S(2)}, u32[]{:S(2)}) collective-permute-start(bf16[128,1152]{1,0:T(8,128)(2,1)S(1)} %upstream.4.refs_0_), channel_id=1, source_target_pairs={{0,8},{8,0},{4,12},{12,4},{1,9},{9,1},{5,13},{13,5},{2,10},{10,2},... | collective-permute-start | bytes 884744 | tf_op jit(solution)/shard_map/ppermute | solution.py:43
  244.6 18.5 %collective-permute-start.116 = (bf16[128,1152]{1,0:T(8,128)(2,1)S(1)}, bf16[128,1152]{1,0:T(8,128)(2,1)S(1)}, u32[]{:S(2)}, u32[]{:S(2)}) collective-permute-start(bf16[128,1152]{1,0:T(8,128)(2,1)S(1)} %upstream.4.refs_0_), channel_id=1, source_target_pairs={{0,4},{4,0},{8,12},{12,8},{1,5},{5,1},{9,13},{13,9},{2,6},{6,2},{1... | collective-permute-start | bytes 884744 | tf_op jit(solution)/shard_map/ppermute | solution.py:39
  261.1 22.2 %collective-permute-start.121 = (bf16[128,1152]{1,0:T(8,128)(2,1)S(1)}, bf16[128,1152]{1,0:T(8,128)(2,1)S(1)}, u32[]{:S(2)}, u32[]{:S(2)}) collective-permute-start(bf16[128,1152]{1,0:T(8,128)(2,1)S(1)} %upstream.5.refs_0_), channel_id=1, source_target_pairs={{0,8},{8,0},{4,12},{12,4},{1,9},{9,1},{5,13},{13,5},{2,10},{10,2},... | collective-permute-start | bytes 884744 | tf_op jit(solution)/shard_map/ppermute | solution.py:43
  262.1 19.2 %collective-permute-start.84 = (bf16[128,1152]{1,0:T(8,128)(2,1)S(1)}, bf16[128,1152]{1,0:T(8,128)(2,1)S(1)}, u32[]{:S(2)}, u32[]{:S(2)}) collective-permute-start(bf16[128,1152]{1,0:T(8,128)(2,1)S(1)} %get-tuple-element.861), channel_id=1, source_target_pairs={{0,4},{4,0},{8,12},{12,8},{1,5},{5,1},{9,13},{13,9},{2,6},{6,2},{1... | collective-permute-start | bytes 884744 | tf_op jit(solution)/shard_map/ppermute | solution.py:39
  263.1 19.0 %collective-permute-start.85 = (bf16[128,1152]{1,0:T(8,128)(2,1)S(1)}, bf16[128,1152]{1,0:T(8,128)(2,1)S(1)}, u32[]{:S(2)}, u32[]{:S(2)}) collective-permute-start(bf16[128,1152]{1,0:T(8,128)(2,1)S(1)} %get-tuple-element.862), channel_id=1, source_target_pairs={{0,8},{8,0},{4,12},{12,4},{1,9},{9,1},{5,13},{13,5},{2,10},{10,2},... | collective-permute-start | bytes 884744 | tf_op jit(solution)/shard_map/ppermute | solution.py:43
  284.9 22.3 %collective-permute-start.90 = (bf16[128,1152]{1,0:T(8,128)(2,1)S(1)}, bf16[128,1152]{1,0:T(8,128)(2,1)S(1)}, u32[]{:S(2)}, u32[]{:S(2)}) collective-permute-start(bf16[128,1152]{1,0:T(8,128)(2,1)S(1)} %get-tuple-element.895.refs_0_), channel_id=1, source_target_pairs={{0,8},{8,0},{4,12},{12,4},{1,9},{9,1},{5,13},{13,5},{2,10},{10,2},... | collective-permute-start | bytes 884744 | tf_op jit(solution)/shard_map/ppermute | solution.py:43
  296.6 21.4 %collective-permute-start.125 = (bf16[64,1152]{1,0:T(8,128)(2,1)S(1)}, bf16[64,1152]{1,0:T(8,128)(2,1)S(1)}, u32[]{:S(2)}, u32[]{:S(2)}) collective-permute-start(bf16[64,1152]{1,0:T(8,128)(2,1)S(1)} %get-tuple-element.942), channel_id=1, source_target_pairs={{0,4},{4,0},{8,12},{12,8},{1,5},{5,1},{9,13},{13,9},{2,6},{6,2},{1... | collective-permute-start | bytes 442376 | tf_op jit(solution)/shard_map/ppermute | solution.py:39
  307.2 16.4 %collective-permute-start.126 = (bf16[64,1152]{1,0:T(8,128)(2,1)S(1)}, bf16[64,1152]{1,0:T(8,128)(2,1)S(1)}, u32[]{:S(2)}, u32[]{:S(2)}) collective-permute-start(bf16[64,1152]{1,0:T(8,128)(2,1)S(1)} %get-tuple-element.943), channel_id=1, source_target_pairs={{0,8},{8,0},{4,12},{12,4},{1,9},{9,1},{5,13},{13,5},{2,10},{10,2},... | collective-permute-start | bytes 442376 | tf_op jit(solution)/shard_map/ppermute | solution.py:43
  308.7 16.0 %collective-permute-start.96 = (bf16[128,1152]{1,0:T(8,128)(2,1)S(1)}, bf16[128,1152]{1,0:T(8,128)(2,1)S(1)}, u32[]{:S(2)}, u32[]{:S(2)}) collective-permute-start(bf16[128,1152]{1,0:T(8,128)(2,1)S(1)} %get-tuple-element.901.refs_0_), channel_id=1, source_target_pairs={{0,8},{8,0},{4,12},{12,4},{1,9},{9,1},{5,13},{13,5},{2,10},{10,2},... | collective-permute-start | bytes 884744 | tf_op jit(solution)/shard_map/ppermute | solution.py:43
  309.3 15.8 %collective-permute-start.97 = (bf16[128,1152]{1,0:T(8,128)(2,1)S(1)}, bf16[128,1152]{1,0:T(8,128)(2,1)S(1)}, u32[]{:S(2)}, u32[]{:S(2)}) collective-permute-start(bf16[128,1152]{1,0:T(8,128)(2,1)S(1)} %get-tuple-element.901.refs_0_), channel_id=1, source_target_pairs={{0,4},{4,0},{8,12},{12,8},{1,5},{5,1},{9,13},{13,9},{2,6},{6,2},{1... | collective-permute-start | bytes 884744 | tf_op jit(solution)/shard_map/ppermute | solution.py:39
  323.6 21.2 %collective-permute-start.117 = (bf16[128,1152]{1,0:T(8,128)(2,1)S(1)}, bf16[128,1152]{1,0:T(8,128)(2,1)S(1)}, u32[]{:S(2)}, u32[]{:S(2)}) collective-permute-start(bf16[128,1152]{1,0:T(8,128)(2,1)S(1)} %get-tuple-element.951), channel_id=1, source_target_pairs={{0,4},{4,0},{8,12},{12,8},{1,5},{5,1},{9,13},{13,9},{2,6},{6,2},{1... | collective-permute-start | bytes 884744 | tf_op jit(solution)/shard_map/ppermute | solution.py:39
  324.7 21.2 %collective-permute-start.118 = (bf16[128,1152]{1,0:T(8,128)(2,1)S(1)}, bf16[128,1152]{1,0:T(8,128)(2,1)S(1)}, u32[]{:S(2)}, u32[]{:S(2)}) collective-permute-start(bf16[128,1152]{1,0:T(8,128)(2,1)S(1)} %get-tuple-element.952), channel_id=1, source_target_pairs={{0,8},{8,0},{4,12},{12,4},{1,9},{9,1},{5,13},{13,5},{2,10},{10,2},... | collective-permute-start | bytes 884744 | tf_op jit(solution)/shard_map/ppermute | solution.py:43
  367.3 19.9 %collective-permute-start.133 = (bf16[128,1152]{1,0:T(8,128)(2,1)S(1)}, bf16[128,1152]{1,0:T(8,128)(2,1)S(1)}, u32[]{:S(2)}, u32[]{:S(2)}) collective-permute-start(bf16[128,1152]{1,0:T(8,128)(2,1)S(1)} %get-tuple-element.995), channel_id=1, source_target_pairs={{0,4},{4,0},{8,12},{12,8},{1,5},{5,1},{9,13},{13,9},{2,6},{6,2},{1... | collective-permute-start | bytes 884744 | tf_op jit(solution)/shard_map/ppermute | solution.py:39
  368.4 19.6 %collective-permute-start.134 = (bf16[128,1152]{1,0:T(8,128)(2,1)S(1)}, bf16[128,1152]{1,0:T(8,128)(2,1)S(1)}, u32[]{:S(2)}, u32[]{:S(2)}) collective-permute-start(bf16[128,1152]{1,0:T(8,128)(2,1)S(1)} %get-tuple-element.996), channel_id=1, source_target_pairs={{0,8},{8,0},{4,12},{12,4},{1,9},{9,1},{5,13},{13,5},{2,10},{10,2},... | collective-permute-start | bytes 884744 | tf_op jit(solution)/shard_map/ppermute | solution.py:43
  368.4 21.6 %collective-permute-start.106 = (bf16[128,1152]{1,0:T(8,128)(2,1)S(1)}, bf16[128,1152]{1,0:T(8,128)(2,1)S(1)}, u32[]{:S(2)}, u32[]{:S(2)}) collective-permute-start(bf16[128,1152]{1,0:T(8,128)(2,1)S(1)} %get-tuple-element.921), channel_id=1, source_target_pairs={{0,4},{4,0},{8,12},{12,8},{1,5},{5,1},{9,13},{13,9},{2,6},{6,2},{1... | collective-permute-start | bytes 884744 | tf_op jit(solution)/shard_map/ppermute | solution.py:39
  369.5 21.8 %collective-permute-start.107 = (bf16[128,1152]{1,0:T(8,128)(2,1)S(1)}, bf16[128,1152]{1,0:T(8,128)(2,1)S(1)}, u32[]{:S(2)}, u32[]{:S(2)}) collective-permute-start(bf16[128,1152]{1,0:T(8,128)(2,1)S(1)} %get-tuple-element.922), channel_id=1, source_target_pairs={{0,8},{8,0},{4,12},{12,4},{1,9},{9,1},{5,13},{13,5},{2,10},{10,2},... | collective-permute-start | bytes 884744 | tf_op jit(solution)/shard_map/ppermute | solution.py:43
  422.0 20.7 %collective-permute-start.148 = (bf16[1152,1152]{1,0:T(8,128)(2,1)S(1)}, bf16[1152,1152]{1,0:T(8,128)(2,1)S(1)}, u32[]{:S(2)}, u32[]{:S(2)}) collective-permute-start(bf16[1152,1152]{1,0:T(8,128)(2,1)S(1)} %get-tuple-element.1043), channel_id=1, source_target_pairs={{0,16},{16,0},{1,17},{17,1},{2,18},{18,2},{3,19},{19,3},{4,20},{20... | collective-permute-start | bytes 7962632 | tf_op jit(solution)/shard_map/ppermute | solution.py:35
  428.8 17.0 %collective-permute-start.146 = (bf16[64,1152]{1,0:T(8,128)(2,1)}, bf16[64,1152]{1,0:T(8,128)(2,1)}, u32[]{:S(2)}, u32[]{:S(2)}) collective-permute-start(bf16[64,1152]{1,0:T(8,128)(2,1)} %get-tuple-element.1017), channel_id=1, source_target_pairs={{0,4},{4,0},{8,12},{12,8},{1,5},{5,1},{9,13},{13,9},{2,6},{6,2},{1... | collective-permute-start | bytes 442376 | tf_op jit(solution)/shard_map/ppermute | solution.py:39
  439.8 30.6 %collective-permute-start.141 = (bf16[512,640]{1,0:T(8,128)(2,1)}, bf16[512,640]{1,0:T(8,128)(2,1)}, u32[]{:S(2)}, u32[]{:S(2)}) collective-permute-start(bf16[512,640]{1,0:T(8,128)(2,1)} %get-tuple-element.1040), channel_id=1, source_target_pairs={{0,16},{16,0},{1,17},{17,1},{2,18},{18,2},{3,19},{19,3},{4,20},{20... | collective-permute-start | bytes 1966088 | tf_op jit(solution)/shard_map/ppermute | solution.py:35
  441.6 19.1 %collective-permute-start.144 = (bf16[64,1152]{1,0:T(8,128)(2,1)}, bf16[64,1152]{1,0:T(8,128)(2,1)}, u32[]{:S(2)}, u32[]{:S(2)}) collective-permute-start(bf16[64,1152]{1,0:T(8,128)(2,1)} %get-tuple-element.1041), channel_id=1, source_target_pairs={{0,8},{8,0},{4,12},{12,4},{1,9},{9,1},{5,13},{13,5},{2,10},{10,2},... | collective-permute-start | bytes 442376 | tf_op jit(solution)/shard_map/ppermute | solution.py:43
  442.7 18.0 %collective-permute-start.145 = (bf16[64,1152]{1,0:T(8,128)(2,1)}, bf16[64,1152]{1,0:T(8,128)(2,1)}, u32[]{:S(2)}, u32[]{:S(2)}) collective-permute-start(bf16[64,1152]{1,0:T(8,128)(2,1)} %get-tuple-element.1042), channel_id=1, source_target_pairs={{0,4},{4,0},{8,12},{12,8},{1,5},{5,1},{9,13},{13,9},{2,6},{6,2},{1... | collective-permute-start | bytes 442376 | tf_op jit(solution)/shard_map/ppermute | solution.py:39
  470.3 21.1 %collective-permute-start.154 = (bf16[512,640]{1,0:T(8,128)(2,1)}, bf16[512,640]{1,0:T(8,128)(2,1)}, u32[]{:S(2)}, u32[]{:S(2)}) collective-permute-start(bf16[512,640]{1,0:T(8,128)(2,1)} %get-tuple-element.1070), channel_id=1, source_target_pairs={{0,16},{16,0},{1,17},{17,1},{2,18},{18,2},{3,19},{19,3},{4,20},{20... | collective-permute-start | bytes 1966088 | tf_op jit(solution)/shard_map/ppermute | solution.py:35
  479.9 236.8 %reduce-scatter.7.cloned.1.call-start = ((), (), s32[]{:S(2)}) async-start(), calls=%async_computation.5 | async-start | bytes 1843200 | tf_op jit(solution)/shard_map/reduce_scatter | solution.py:884
  489.3 17.4 %collective-permute-start.151 = (bf16[64,1152]{1,0:T(8,128)(2,1)S(1)}, bf16[64,1152]{1,0:T(8,128)(2,1)S(1)}, u32[]{:S(2)}, u32[]{:S(2)}) collective-permute-start(bf16[64,1152]{1,0:T(8,128)(2,1)S(1)} %get-tuple-element.1065), channel_id=1, source_target_pairs={{0,8},{8,0},{4,12},{12,4},{1,9},{9,1},{5,13},{13,5},{2,10},{10,2},... | collective-permute-start | bytes 442376 | tf_op jit(solution)/shard_map/ppermute | solution.py:43
  490.3 17.3 %collective-permute-start.152 = (bf16[64,1152]{1,0:T(8,128)(2,1)S(1)}, bf16[64,1152]{1,0:T(8,128)(2,1)S(1)}, u32[]{:S(2)}, u32[]{:S(2)}) collective-permute-start(bf16[64,1152]{1,0:T(8,128)(2,1)S(1)} %get-tuple-element.1066), channel_id=1, source_target_pairs={{0,4},{4,0},{8,12},{12,8},{1,5},{5,1},{9,13},{13,9},{2,6},{6,2},{1... | collective-permute-start | bytes 442376 | tf_op jit(solution)/shard_map/ppermute | solution.py:39
  522.2 17.6 %collective-permute-start.159 = (bf16[64,1152]{1,0:T(8,128)(2,1)S(1)}, bf16[64,1152]{1,0:T(8,128)(2,1)S(1)}, u32[]{:S(2)}, u32[]{:S(2)}) collective-permute-start(bf16[64,1152]{1,0:T(8,128)(2,1)S(1)} %get-tuple-element.1088), channel_id=1, source_target_pairs={{0,8},{8,0},{4,12},{12,4},{1,9},{9,1},{5,13},{13,5},{2,10},{10,2},... | collective-permute-start | bytes 442376 | tf_op jit(solution)/shard_map/ppermute | solution.py:43
  526.1 24.3 %collective-permute-start.173 = (bf16[128,1152]{1,0:T(8,128)(2,1)S(1)}, bf16[128,1152]{1,0:T(8,128)(2,1)S(1)}, u32[]{:S(2)}, u32[]{:S(2)}) collective-permute-start(bf16[128,1152]{1,0:T(8,128)(2,1)S(1)} %get-tuple-element.1160.refs_0_), channel_id=1, source_target_pairs={{0,8},{8,0},{4,12},{12,4},{1,9},{9,1},{5,13},{13,5},{2,10},{10,2},... | collective-permute-start | bytes 884744 | tf_op jit(solution)/shard_map/ppermute | solution.py:43
  530.6 20.9 %collective-permute-start.174 = (bf16[128,1152]{1,0:T(8,128)(2,1)S(1)}, bf16[128,1152]{1,0:T(8,128)(2,1)S(1)}, u32[]{:S(2)}, u32[]{:S(2)}) collective-permute-start(bf16[128,1152]{1,0:T(8,128)(2,1)S(1)} %get-tuple-element.1160.refs_0_), channel_id=1, source_target_pairs={{0,4},{4,0},{8,12},{12,8},{1,5},{5,1},{9,13},{13,9},{2,6},{6,2},{1... | collective-permute-start | bytes 884744 | tf_op jit(solution)/shard_map/ppermute | solution.py:39
  539.8 19.5 %collective-permute-start.179 = (bf16[1152,640]{1,0:T(8,128)(2,1)S(1)}, bf16[1152,640]{1,0:T(8,128)(2,1)S(1)}, u32[]{:S(2)}, u32[]{:S(2)}) collective-permute-start(bf16[1152,640]{1,0:T(8,128)(2,1)S(1)} %get-tuple-element.1149), channel_id=1, source_target_pairs={{0,16},{16,0},{1,17},{17,1},{2,18},{18,2},{3,19},{19,3},{4,20},{20... | collective-permute-start | bytes 4423688 | tf_op jit(solution)/shard_map/ppermute | solution.py:35
  556.6 19.1 %collective-permute-start.175 = (bf16[64,1152]{1,0:T(8,128)(2,1)}, bf16[64,1152]{1,0:T(8,128)(2,1)}, u32[]{:S(2)}, u32[]{:S(2)}) collective-permute-start(bf16[64,1152]{1,0:T(8,128)(2,1)} %get-tuple-element.1147), channel_id=1, source_target_pairs={{0,8},{8,0},{4,12},{12,4},{1,9},{9,1},{5,13},{13,5},{2,10},{10,2},... | collective-permute-start | bytes 442376 | tf_op jit(solution)/shard_map/ppermute | solution.py:43
  557.7 19.1 %collective-permute-start.176 = (bf16[64,1152]{1,0:T(8,128)(2,1)}, bf16[64,1152]{1,0:T(8,128)(2,1)}, u32[]{:S(2)}, u32[]{:S(2)}) collective-permute-start(bf16[64,1152]{1,0:T(8,128)(2,1)} %get-tuple-element.1148), channel_id=1, source_target_pairs={{0,4},{4,0},{8,12},{12,8},{1,5},{5,1},{9,13},{13,9},{2,6},{6,2},{1... | collective-permute-start | bytes 442376 | tf_op jit(solution)/shard_map/ppermute | solution.py:39
  560.0 24.3 %collective-permute-start.171 = (bf16[64,1152]{1,0:T(8,128)(2,1)}, bf16[64,1152]{1,0:T(8,128)(2,1)}, u32[]{:S(2)}, u32[]{:S(2)}) collective-permute-start(bf16[64,1152]{1,0:T(8,128)(2,1)} %get-tuple-element.1144), channel_id=1, source_target_pairs={{0,8},{8,0},{4,12},{12,4},{1,9},{9,1},{5,13},{13,5},{2,10},{10,2},... | collective-permute-start | bytes 442376 | tf_op jit(solution)/shard_map/ppermute | solution.py:43
  562.5 22.4 %collective-permute-start.172 = (bf16[64,1152]{1,0:T(8,128)(2,1)}, bf16[64,1152]{1,0:T(8,128)(2,1)}, u32[]{:S(2)}, u32[]{:S(2)}) collective-permute-start(bf16[64,1152]{1,0:T(8,128)(2,1)} %copy-done.229), channel_id=1, source_target_pairs={{0,4},{4,0},{8,12},{12,8},{1,5},{5,1},{9,13},{13,9},{2,6},{6,2},{1... | collective-permute-start | bytes 442376 | tf_op jit(solution)/shard_map/ppermute | solution.py:39
  584.3 41.6 %collective-permute-start.112 = (f32[3,128,1152]{2,1,0:T(8,128)S(1)}, f32[3,128,1152]{2,1,0:T(8,128)S(1)}, u32[]{:S(2)}, u32[]{:S(2)}) collective-permute-start(f32[3,128,1152]{2,1,0:T(8,128)S(1)} %copy-done.363), channel_id=1, source_target_pairs={{0,16},{16,0},{1,17},{17,1},{2,18},{18,2},{3,19},{19,3},{4,20},{20... | collective-permute-start | bytes 5308424 | tf_op jit(solution)/shard_map/ppermute | solution.py:35
  605.3 193.8 %collective-permute-start.218 = (bf16[24,1152]{1,0:T(8,128)(2,1)}, bf16[24,1152]{1,0:T(8,128)(2,1)}, u32[]{:S(2)}, u32[]{:S(2)}) collective-permute-start(bf16[24,1152]{1,0:T(8,128)(2,1)} %get-tuple-element.1434), channel_id=1, source_target_pairs={{0,1},{1,2},{2,3},{3,0},{4,5},{5,6},{6,7},{7,4},{8,9},{9,10},{10,1... | collective-permute-start | bytes 165896 | tf_op jit(solution)/shard_map/ppermute | solution.py:190
  625.9 31.7 %collective-permute-start.201 = (bf16[1152,1152]{1,0:T(8,128)(2,1)}, bf16[1152,1152]{1,0:T(8,128)(2,1)}, u32[]{:S(2)}, u32[]{:S(2)}) collective-permute-start(bf16[1152,1152]{1,0:T(8,128)(2,1)} %get-tuple-element.1237), channel_id=1, source_target_pairs={{0,16},{16,0},{1,17},{17,1},{2,18},{18,2},{3,19},{19,3},{4,20},{20... | collective-permute-start | bytes 7962632 | tf_op jit(solution)/shard_map/ppermute | solution.py:35
  631.7 138.5 %reduce-scatter.9.cloned.1.call-start = ((), (), s32[]{:S(2)}) async-start(), calls=%async_computation.6 | async-start | bytes 3317760 | tf_op jit(solution)/shard_map/reduce_scatter | solution.py:884
  631.7 24.0 %collective-permute-start.195 = (bf16[128,1152]{1,0:T(8,128)(2,1)}, bf16[128,1152]{1,0:T(8,128)(2,1)S(1)}, u32[]{:S(2)}, u32[]{:S(2)}) collective-permute-start(bf16[128,1152]{1,0:T(8,128)(2,1)} %copy-done.196), channel_id=1, source_target_pairs={{0,8},{8,0},{4,12},{12,4},{1,9},{9,1},{5,13},{13,5},{2,10},{10,2},... | collective-permute-start | bytes 884744 | tf_op jit(solution)/shard_map/ppermute | solution.py:43
  635.9 21.0 %collective-permute-start.196 = (bf16[128,1152]{1,0:T(8,128)(2,1)}, bf16[128,1152]{1,0:T(8,128)(2,1)S(1)}, u32[]{:S(2)}, u32[]{:S(2)}) collective-permute-start(bf16[128,1152]{1,0:T(8,128)(2,1)} %copy-done.196), channel_id=1, source_target_pairs={{0,4},{4,0},{8,12},{12,8},{1,5},{5,1},{9,13},{13,9},{2,6},{6,2},{1... | collective-permute-start | bytes 884744 | tf_op jit(solution)/shard_map/ppermute | solution.py:39
  636.9 26.4 %collective-permute-start.199 = (bf16[64,1152]{1,0:T(8,128)(2,1)}, bf16[64,1152]{1,0:T(8,128)(2,1)}, u32[]{:S(2)}, u32[]{:S(2)}) collective-permute-start(bf16[64,1152]{1,0:T(8,128)(2,1)} %copy-done.228), channel_id=1, source_target_pairs={{0,4},{4,0},{8,12},{12,8},{1,5},{5,1},{9,13},{13,9},{2,6},{6,2},{1... | collective-permute-start | bytes 442376 | tf_op jit(solution)/shard_map/ppermute | solution.py:39
  656.9 37.8 %collective-permute-start.194 = (bf16[512,640]{1,0:T(8,128)(2,1)}, bf16[512,640]{1,0:T(8,128)(2,1)}, u32[]{:S(2)}, u32[]{:S(2)}) collective-permute-start(bf16[512,640]{1,0:T(8,128)(2,1)} %get-tuple-element.1234), channel_id=1, source_target_pairs={{0,16},{16,0},{1,17},{17,1},{2,18},{18,2},{3,19},{19,3},{4,20},{20... | collective-permute-start | bytes 1966088 | tf_op jit(solution)/shard_map/ppermute | solution.py:35
  658.3 27.0 %collective-permute-start.197 = (bf16[64,1152]{1,0:T(8,128)(2,1)}, bf16[64,1152]{1,0:T(8,128)(2,1)}, u32[]{:S(2)}, u32[]{:S(2)}) collective-permute-start(bf16[64,1152]{1,0:T(8,128)(2,1)} %get-tuple-element.1235), channel_id=1, source_target_pairs={{0,8},{8,0},{4,12},{12,4},{1,9},{9,1},{5,13},{13,5},{2,10},{10,2},... | collective-permute-start | bytes 442376 | tf_op jit(solution)/shard_map/ppermute | solution.py:43
  663.3 22.1 %collective-permute-start.198 = (bf16[64,1152]{1,0:T(8,128)(2,1)}, bf16[64,1152]{1,0:T(8,128)(2,1)S(1)}, u32[]{:S(2)}, u32[]{:S(2)}) collective-permute-start(bf16[64,1152]{1,0:T(8,128)(2,1)} %copy-done.230), channel_id=1, source_target_pairs={{0,4},{4,0},{8,12},{12,8},{1,5},{5,1},{9,13},{13,9},{2,6},{6,2},{1... | collective-permute-start | bytes 442376 | tf_op jit(solution)/shard_map/ppermute | solution.py:39
  694.7 22.0 %collective-permute-start.206 = (bf16[512,640]{1,0:T(8,128)(2,1)}, bf16[512,640]{1,0:T(8,128)(2,1)S(1)}, u32[]{:S(2)}, u32[]{:S(2)}) collective-permute-start(bf16[512,640]{1,0:T(8,128)(2,1)} %get-tuple-element.1269), channel_id=1, source_target_pairs={{0,16},{16,0},{1,17},{17,1},{2,18},{18,2},{3,19},{19,3},{4,20},{20... | collective-permute-start | bytes 1966088 | tf_op jit(solution)/shard_map/ppermute | solution.py:35
  704.4 94.7 %reduce-scatter.11.cloned.1.call-start = ((), (), s32[]{:S(2)}) async-start(), calls=%async_computation.7 | async-start | bytes 1843200 | tf_op jit(solution)/shard_map/reduce_scatter | solution.py:884
  704.4 17.5 %collective-permute-start.207 = (bf16[512,640]{1,0:T(8,128)(2,1)S(1)}, bf16[512,640]{1,0:T(8,128)(2,1)}, u32[]{:S(2)}, u32[]{:S(2)}) collective-permute-start(bf16[512,640]{1,0:T(8,128)(2,1)S(1)} %copy-done.163), channel_id=1, source_target_pairs={{0,16},{16,0},{1,17},{17,1},{2,18},{18,2},{3,19},{19,3},{4,20},{20... | collective-permute-start | bytes 1966088 | tf_op jit(solution)/shard_map/ppermute | solution.py:35
  714.6 24.9 %collective-permute-start.204 = (bf16[64,1152]{1,0:T(8,128)(2,1)}, bf16[64,1152]{1,0:T(8,128)(2,1)}, u32[]{:S(2)}, u32[]{:S(2)}) collective-permute-start(bf16[64,1152]{1,0:T(8,128)(2,1)} %get-tuple-element.1259), channel_id=1, source_target_pairs={{0,8},{8,0},{4,12},{12,4},{1,9},{9,1},{5,13},{13,5},{2,10},{10,2},... | collective-permute-start | bytes 442376 | tf_op jit(solution)/shard_map/ppermute | solution.py:43
  715.6 25.1 %collective-permute-start.205 = (bf16[64,1152]{1,0:T(8,128)(2,1)}, bf16[64,1152]{1,0:T(8,128)(2,1)}, u32[]{:S(2)}, u32[]{:S(2)}) collective-permute-start(bf16[64,1152]{1,0:T(8,128)(2,1)} %get-tuple-element.1260), channel_id=1, source_target_pairs={{0,4},{4,0},{8,12},{12,8},{1,5},{5,1},{9,13},{13,9},{2,6},{6,2},{1... | collective-permute-start | bytes 442376 | tf_op jit(solution)/shard_map/ppermute | solution.py:39
  745.9 54.6 %collective-permute-start.219 = (bf16[24,1152]{1,0:T(8,128)(2,1)}, bf16[24,1152]{1,0:T(8,128)(2,1)S(1)}, u32[]{:S(2)}, u32[]{:S(2)}) collective-permute-start(bf16[24,1152]{1,0:T(8,128)(2,1)} %get-tuple-element.1434), channel_id=1, source_target_pairs={{0,2},{1,3},{2,0},{3,1},{4,6},{5,7},{6,4},{7,5},{8,10},{9,11},{10,... | collective-permute-start | bytes 165896 | tf_op jit(solution)/shard_map/ppermute | solution.py:190
  748.7 53.2 %collective-permute-start.220 = (bf16[24,1152]{1,0:T(8,128)(2,1)}, bf16[24,1152]{1,0:T(8,128)(2,1)}, u32[]{:S(2)}, u32[]{:S(2)}) collective-permute-start(bf16[24,1152]{1,0:T(8,128)(2,1)} %get-tuple-element.1434), channel_id=1, source_target_pairs={{0,3},{1,0},{2,1},{3,2},{4,7},{5,4},{6,5},{7,6},{8,11},{9,8},{10,9... | collective-permute-start | bytes 165896 | tf_op jit(solution)/shard_map/ppermute | solution.py:190
  770.2 32.8 %collective-permute-start.224 = (bf16[24,1728]{1,0:T(8,128)(2,1)S(1)}, bf16[24,1728]{1,0:T(8,128)(2,1)S(1)}, u32[]{:S(2)}, u32[]{:S(2)}) collective-permute-start(bf16[24,1728]{1,0:T(8,128)(2,1)S(1)} %fusion.24), channel_id=1, source_target_pairs={{0,1},{1,2},{2,3},{3,0},{4,5},{5,6},{6,7},{7,4},{8,9},{9,10},{10,1... | collective-permute-start | bytes 248840 | tf_op jit(solution)/shard_map/ppermute | solution.py:190
  770.9 32.1 %collective-permute-start.225 = (bf16[24,1728]{1,0:T(8,128)(2,1)S(1)}, bf16[24,1728]{1,0:T(8,128)(2,1)S(1)}, u32[]{:S(2)}, u32[]{:S(2)}) collective-permute-start(bf16[24,1728]{1,0:T(8,128)(2,1)S(1)} %fusion.24), channel_id=1, source_target_pairs={{0,2},{1,3},{2,0},{3,1},{4,6},{5,7},{6,4},{7,5},{8,10},{9,11},{10,... | collective-permute-start | bytes 248840 | tf_op jit(solution)/shard_map/ppermute | solution.py:190
  (547 other events, 6131.8 us)
Sparse Core Ops, SparseCore 0:
  480.0 52.8 reduce-scatter.4
  631.8 33.9 reduce-scatter.6
  704.5 55.1 reduce-scatter.8
  762.0 37.0 reduce-scatter.10

commit v4 on v3

--- a/solution.py
+++ b/solution.py
@@ -14,7 +14,7 @@
 bf16 = jnp.bfloat16
 log2e = math.log2(math.e)
 brief = pl.CostEstimate(flops=1000000000, bytes_accessed=1, transcendentals=0)
-lengthy = pl.CostEstimate(flops=12000000000, bytes_accessed=1, transcendentals=0)
+lengthy = pl.CostEstimate(flops=9000000000, bytes_accessed=1, transcendentals=0)
 
 
 def normalize_keep(value):
@@ -876,11 +876,8 @@
         results[name, b] = (keep, swap_cores(send))
 
     def reduced(name, b):
-        if (name, b) == ("narrow", 0):
-            total = add(*results[name, b], vmem=12)
-        else:
-            total = add(*after(results[name, b]), vmem=12)
-            ends(total)
+        total = add(*after(results[name, b]), vmem=12)
+        ends(total)
         results[name, b] = lax.psum_scatter(total, "dp", scatter_dimension=0, tiled=True)
 
     def wide(b):
@@ -912,18 +909,19 @@
         for i, one in enumerate(running):
             if step == 20 and i == 0:
                 narrow(0)
+            if step == 20 and i == micro - 1:
+                reduced("narrow", 0)
             if step < 21:
                 next(one, None)
             behind = step
             if i == 0 and behind in ready:
                 reduced(*ready[behind])
-            if i == micro - 1 and behind in extra:
+            if i == 1 and behind in extra:
                 work, b = extra[behind]
                 work(b)
             if i == 0 and behind in settled:
                 ends((latest[0], results[settled[behind]]))
 
-    reduced("narrow", 0)
     out_zero, out_one = collected("out", 0), collected("out", 1)
     back_zero, back_one = collected("grad", 0), collected("grad", 1)
     rms_zero, rms_one = (

time: 829 us -> 813 us (0.981)
  waiting for transfers between devices: 178 us -> 165 us
    reduce_scatter x4, waiting for transfers between devices: 27.2 us -> 16.8 us  [reduced(): lax.psum_scatter(total, 'dp', scatter_dimension=0, tiled=True)]
    ppermute x98, waiting for transfers between devices: 86.6 us -> 76.3 us  [along_y(): return lax.ppermute(block, 'tensor', [(0, 2), (2, 0), (1, 3), (3, 1)])]
    unnamed x756 -> x820, local copies, waits for them, and re-layouts: 72.5 us -> 77.3 us
  transfers between devices with their start and end apart: 234 -> 234, of which waited for: 62 -> 63; matrix products, arithmetic and copies ran while one was open for 5% -> 5% of each run, Pallas kernels for 33% -> 33%
where the time goes in v4:
time: 813 us; the launch traced here: 803 us
  Pallas kernels  279 us (34%)
  starting transfers between devices  220 us (27%)
  waiting for transfers between devices  165 us (20%)
  local copies, waits for them, and re-layouts  82.6 us (10%)
  other arithmetic  30.1 us (4%)
  between operations  19.1 us (2%)
    pallas_call x115, Pallas kernels, run(): pl.pallas_call(kernel, out_shape=tuple(shapes), compiler_params=pltpu.Com...  239 us
    ppermute x98, starting transfers between devices, along_y(): return lax.ppermute(block, 'tensor', [(0, 2), (2, 0), (1, 3), (3, 1)])  105 us
    ppermute x99, starting transfers between devices, along_x(): return lax.ppermute(block, 'tensor', [(0, 1), (1, 0), (2, 3), (3, 2)])  102 us
    unnamed x820, local copies, waits for them, and re-layouts  77.3 us
    ppermute x98, waiting for transfers between devices, along_y(): return lax.ppermute(block, 'tensor', [(0, 2), (2, 0), (1, 3), (3, 1)])  76.3 us
    ppermute x99, waiting for transfers between devices, along_x(): return lax.ppermute(block, 'tensor', [(0, 1), (1, 0), (2, 3), (3, 2)])  69.6 us
    pallas_call x4, Pallas kernels, weight_sums(): pl.pallas_call(kernel, grid=(depth // step,), in_specs=[pl.BlockSpec(memo...  40.3 us
    reduce_scatter x4, waiting for transfers between devices, reduced(): lax.psum_scatter(total, 'dp', scatter_dimension=0, tiled=True)  16.8 us
  transfers between devices with their start and end apart: 234, of which 63 were waited for; matrix products, arithmetic and copies ran while one was open for 5% of the time, Pallas kernels for 33%

profile of v4, /device:TPU:0, one launch (start us, length us, event | category | flops | bytes accessed | tf_op | source)
XLA Modules:
  0.0 803.3 jit_solution(16770300022853674502)
XLA Ops:
  7.2 4.2 fusion
  11.4 3.0 collective-permute-start.5
  40.1 3.0 collective-permute-done.14.far.refs_1_
  55.0 3.8 qkv.6
  61.4 3.6 qkv.7
  66.7 4.0 qkv.8
  71.9 8.5 %attend.6 = (bf16[512,288]{1,0:T(8,128)(2,1)S(1)}, f32[4,512]{1,0:T(4,128)S(1)}, bf16[128,1152]{1,0:T(8,128)(2,1)S(1)}, bf16[128,1152]{1,0:T(8,128)(2,1)S(1)}, b...) custom-call(bf16[512,288]{1,0:T(8,128)(2,1)S(1)} %get-tuple-element.682.query_ref.refs_6_, ...), custom_call_target="tpu_custom_call" | custom-call | flops 8999999488 | bytes 1 | tf_op jit(solution)/shard_map/attend/pallas_call | solution.py:217
  82.6 8.7 %attend.7 = (bf16[512,288]{1,0:T(8,128)(2,1)S(1)}, f32[4,512]{1,0:T(4,128)S(1)}, bf16[128,1152]{1,0:T(8,128)(2,1)S(1)}, bf16[128,1152]{1,0:T(8,128)(2,1)S(1)}, b...) custom-call(bf16[512,288]{1,0:T(8,128)(2,1)S(1)} %get-tuple-element.693.query_ref.refs_6_, ...), custom_call_target="tpu_custom_call" | custom-call | flops 8999999488 | bytes 1 | tf_op jit(solution)/shard_map/attend/pallas_call | solution.py:217
  95.4 8.5 %attend.8 = (bf16[512,288]{1,0:T(8,128)(2,1)S(1)}, f32[4,512]{1,0:T(4,128)S(1)}, bf16[128,1152]{1,0:T(8,128)(2,1)S(1)}, bf16[128,1152]{1,0:T(8,128)(2,1)S(1)}, b...) custom-call(bf16[512,288]{1,0:T(8,128)(2,1)S(1)} %get-tuple-element.699.query_ref.refs_6_, ...), custom_call_target="tpu_custom_call" | custom-call | flops 8999999488 | bytes 1 | tf_op jit(solution)/shard_map/attend/pallas_call | solution.py:217
  107.1 4.2 collective-permute-done.22.refs_4_
  119.4 5.0 collective-permute-done.32.second.refs_2_
  132.5 7.6 collective-permute-done.33.refs_3_
  145.2 5.0 feed.6
  156.3 5.0 feed.7
  165.7 5.4 feed.8
  179.2 3.4 collective-permute-done.55.first.refs_1_
  194.8 6.9 collective-permute-done.57.refs_3_
  222.4 8.7 %attend.9 = (bf16[512,288]{1,0:T(8,128)(2,1)S(1)}, f32[4,512]{1,0:T(4,128)S(1)}, bf16[128,1152]{1,0:T(8,128)(2,1)S(1)}, bf16[128,1152]{1,0:T(8,128)(2,1)S(1)}, b...) custom-call(bf16[512,288]{1,0:T(8,128)(2,1)S(1)} %get-tuple-element.818.query_ref.refs_6_, ...), custom_call_target="tpu_custom_call" | custom-call | flops 8999999488 | bytes 1 | tf_op jit(solution)/shard_map/attend/pallas_call | solution.py:217
  233.6 8.8 %attend.10 = (bf16[512,288]{1,0:T(8,128)(2,1)S(1)}, f32[4,512]{1,0:T(4,128)S(1)}, bf16[128,1152]{1,0:T(8,128)(2,1)S(1)}, bf16[128,1152]{1,0:T(8,128)(2,1)S(1)}, ...) custom-call(bf16[512,288]{1,0:T(8,128)(2,1)S(1)} %get-tuple-element.828.query_ref.refs_6_, ...), custom_call_target="tpu_custom_call" | custom-call | flops 8999999488 | bytes 1 | tf_op jit(solution)/shard_map/attend/pallas_call | solution.py:217
  248.2 4.2 collective-permute-done.78.first.refs_1_
  254.8 8.6 %attend.11 = (bf16[512,288]{1,0:T(8,128)(2,1)S(1)}, f32[4,512]{1,0:T(4,128)S(1)}, bf16[128,1152]{1,0:T(8,128)(2,1)S(1)}, bf16[128,1152]{1,0:T(8,128)(2,1)S(1)}, ...) custom-call(bf16[512,288]{1,0:T(8,128)(2,1)S(1)} %get-tuple-element.834.query_ref.refs_6_, ...), custom_call_target="tpu_custom_call" | custom-call | flops 8999999488 | bytes 1 | tf_op jit(solution)/shard_map/attend/pallas_call | solution.py:217
  270.6 4.8 collective-permute-done.88.refs_3_
  277.6 5.3 collective-permute-done.89.refs_4_
  288.8 7.3 collective-permute-done.113.refs_3_
  300.7 3.0 collective-permute-done.86.refs_3_
  304.4 4.0 collective-permute-done.87.refs_4_
  316.9 5.0 feed.9
  322.1 4.1 feed_back.6
  332.3 5.0 feed.10
  339.9 4.1 feed_back.7
  348.9 5.0 feed.11
  360.9 4.1 feed_back.8
  375.2 8.0 collective-permute-done.137.refs_3_
  399.6 12.4 %wide.2 = (bf16[1152,1152]{1,0:T(8,128)(2,1)S(1)}, bf16[1152,1152]{1,0:T(8,128)(2,1)S(1)}) custom-call(s32[1]{0:T(128)} %bitcast.62.flag, bf16[512,1152]{1,0:T(8,128)(2,1)S(1)} %get-tuple-element.1011.refs_0_, bf16[512,1152]{1,0:T(8,128)(2,1)S(1)} %copy-done.281, bf16[512,1152]{1,0:T(8,128)(2,1)S(1)} %copy-done.289, ...), custom_call_target="tpu_custom_call" | custom-call | flops 8999999488 | bytes 1 | tf_op jit(solution)/shard_map/wide/pallas_call | solution.py:520
  416.2 2.6 collective-permute-done.135.refs_3_
  425.9 2.8 collective-permute-done.139.near.refs_2_
  434.0 8.7 %attend_back.6 = (bf16[512,1152]{1,0:T(8,128)(2,1)S(1)}, bf16[512,288]{1,0:T(8,128)(2,1)S(1)}, f32[512,576]{1,0:T(8,128)S(1)}, bf16[512,640]{1,0:T(8,128)(2,1)}) custom-call(bf16[128,1152]{1,0:T(8,128)(2,1)S(1)} %get-tuple-element.1034.refs_0_, bf16[128,1152]{1,0:T(8,128)(2,1)S(1)} %collective-permute-done.129.far.refs_1_, ...), custom_call_target="tpu_custom_call" | custom-call | flops 8999999488 | bytes 1 | tf_op jit(solution)/shard_map/attend_back/pallas_call | solution.py:217
  452.9 9.0 %attend_back.7 = (bf16[512,1152]{1,0:T(8,128)(2,1)S(1)}, bf16[512,288]{1,0:T(8,128)(2,1)S(1)}, f32[512,576]{1,0:T(8,128)S(1)}, bf16[512,640]{1,0:T(8,128)(2,1)S(1)}) custom-call(bf16[128,1152]{1,0:T(8,128)(2,1)S(1)} %copy-done.202, bf16[128,1152]{1,0:T(8,128)(2,1)S(1)} %copy-done.216, bf16[128,1152]{1,0:T(8,128)(2,1)S(1)} %copy-done.214, ...), custom_call_target="tpu_custom_call" | custom-call | flops 8999999488 | bytes 1 | tf_op jit(solution)/shard_map/attend_back/pallas_call | solution.py:217
  462.0 9.4 %attend_back.8 = (bf16[512,1152]{1,0:T(8,128)(2,1)S(1)}, bf16[512,288]{1,0:T(8,128)(2,1)S(1)}, f32[512,576]{1,0:T(8,128)S(1)}, bf16[512,640]{1,0:T(8,128)(2,1)S(1)}) custom-call(bf16[128,1152]{1,0:T(8,128)(2,1)S(1)} %copy-done.232, bf16[128,1152]{1,0:T(8,128)(2,1)S(1)} %copy-done.238, bf16[128,1152]{1,0:T(8,128)(2,1)S(1)} %copy-done.244, ...), custom_call_target="tpu_custom_call" | custom-call | flops 8999999488 | bytes 1 | tf_op jit(solution)/shard_map/attend_back/pallas_call | solution.py:217
  471.6 2.9 qkv_back.6
  476.7 7.2 collective-permute-done.149.first.refs_1_
  493.6 3.4 collective-permute-done.155.first.refs_1_
  512.1 4.3 collective-permute-done.157.far.refs_1_
  518.7 7.3 narrow.2
  531.3 4.1 feed_back.9
  544.4 3.6 collective-permute-done.169.first.refs_1_
  560.9 5.2 feed_back.10
  570.9 5.8 feed_back.11
  605.6 13.3 %wide.3 = (bf16[1152,1152]{1,0:T(8,128)(2,1)S(1)}, bf16[1152,1152]{1,0:T(8,128)(2,1)}) custom-call(s32[1]{0:T(128)} %bitcast.62.flag, bf16[512,1152]{1,0:T(8,128)(2,1)S(1)} %copy-done.269, bf16[512,1152]{1,0:T(8,128)(2,1)S(1)} %copy-done.273, bf16[512,1152]{1,0:T(8,128)(2,1)S(1)} %copy-done.277, bf16[512,1152]{1,0:T(8,128)(2,1)S(1)} %copy-done.285, ...), custom_call_target="tpu_custom_call" | custom-call | flops 8999999488 | bytes 1 | tf_op jit(solution)/shard_map/wide/pallas_call | solution.py:520
  621.0 4.6 broadcast_select_fusion.11
  635.7 2.9 collective-permute-done.192.near.refs_2_
  644.0 8.6 %attend_back.9 = (bf16[512,1152]{1,0:T(8,128)(2,1)S(1)}, bf16[512,288]{1,0:T(8,128)(2,1)S(1)}, f32[512,576]{1,0:T(8,128)S(1)}, bf16[512,640]{1,0:T(8,128)(2,1)}) custom-call(bf16[128,1152]{1,0:T(8,128)(2,1)S(1)} %copy-done.196, bf16[128,1152]{1,0:T(8,128)(2,1)S(1)} %copy-done.198, bf16[128,1152]{1,0:T(8,128)(2,1)S(1)} %copy-done.200, ...), custom_call_target="tpu_custom_call" | custom-call | flops 8999999488 | bytes 1 | tf_op jit(solution)/shard_map/attend_back/pallas_call | solution.py:217
  656.4 3.9 add.422
  664.0 9.8 %attend_back.10 = (bf16[512,1152]{1,0:T(8,128)(2,1)S(1)}, bf16[512,288]{1,0:T(8,128)(2,1)S(1)}, f32[512,576]{1,0:T(8,128)S(1)}, bf16[512,640]{1,0:T(8,128)(2,1)}) custom-call(bf16[128,1152]{1,0:T(8,128)(2,1)S(1)} %copy-done.194, bf16[128,1152]{1,0:T(8,128)(2,1)S(1)} %copy-done.224, bf16[128,1152]{1,0:T(8,128)(2,1)S(1)} %copy-done.220, ...), custom_call_target="tpu_custom_call" | custom-call | flops 8999999488 | bytes 1 | tf_op jit(solution)/shard_map/attend_back/pallas_call | solution.py:217
  676.6 10.0 %attend_back.11 = (bf16[512,1152]{1,0:T(8,128)(2,1)S(1)}, bf16[512,288]{1,0:T(8,128)(2,1)S(1)}, f32[512,576]{1,0:T(8,128)S(1)}, bf16[512,640]{1,0:T(8,128)(2,1)}) custom-call(bf16[128,1152]{1,0:T(8,128)(2,1)S(1)} %copy-done.222, bf16[128,1152]{1,0:T(8,128)(2,1)S(1)} %copy-done.234, bf16[128,1152]{1,0:T(8,128)(2,1)S(1)} %copy-done.240, ...), custom_call_target="tpu_custom_call" | custom-call | flops 8999999488 | bytes 1 | tf_op jit(solution)/shard_map/attend_back/pallas_call | solution.py:217
  686.7 3.4 qkv_back.9
  694.7 6.1 collective-permute-done.202.first.refs_1_
  711.0 3.0 qkv_back.11
  718.6 7.3 narrow.3
  733.4 3.2 collective-permute-done.212.first.refs_1_
  738.1 2.7 collective-permute-start.220
  757.7 3.1 collective-permute-done.223
  767.1 16.7 %reduce-scatter.11.cloned.1.call-done = bf16[288,640]{1,0:T(8,128)(2,1)} async-done(((bf16[1152,640]{1,0:T(8,128)(2,1)}), bf16[288,640]{1,0:T(8,128)(2,1)}) %reduce-scatter.11.cloned.1.call-update) | async-done | bytes 368656 | tf_op jit(solution)/shard_map/reduce_scatter | solution.py:881
  789.4 2.7 convolution_bitcast_fusion
  (1434 shorter events, 414.6 us)
Async XLA Ops:
  7.2 547.8 %reduce-scatter.5.cloned.1.call-start = ((), (), s32[]{:S(2)}) async-start(), calls=%async_computation.4 | async-start | bytes 3317760 | tf_op jit(solution)/shard_map/reduce_scatter | solution.py:881
  14.4 16.6 %collective-permute-start.4 = (f32[24,1728]{1,0:T(8,128)}, f32[24,1728]{1,0:T(8,128)}, u32[]{:S(2)}, u32[]{:S(2)}) collective-permute-start(f32[24,1728]{1,0:T(8,128)} %fusion), channel_id=1, source_target_pairs={{0,4},{4,0},{8,12},{12,8},{1,5},{5,1},{9,13},{13,9},{2,6},{6,2},{1... | collective-permute-start | bytes 497672 | tf_op jit(solution)/shard_map/ppermute | solution.py:39
  17.7 19.1 %collective-permute-start.10 = (bf16[128,1152]{1,0:T(8,128)(2,1)S(1)}, bf16[128,1152]{1,0:T(8,128)(2,1)}, u32[]{:S(2)}, u32[]{:S(2)}) collective-permute-start(bf16[128,1152]{1,0:T(8,128)(2,1)S(1)} %get-tuple-element.694.refs_0_), channel_id=1, source_target_pairs={{0,8},{8,0},{4,12},{12,4},{1,9},{9,1},{5,13},{13,5},{2,10},{10,2},... | collective-permute-start | bytes 884744 | tf_op jit(solution)/shard_map/ppermute | solution.py:43
  43.1 71.1 %collective-permute-start.40 = (bf16[1152,1152]{1,0:T(8,128)(2,1)S(1)}, bf16[1152,1152]{1,0:T(8,128)(2,1)S(1)}, u32[]{:S(2)}, u32[]{:S(2)}) collective-permute-start(bf16[1152,1152]{1,0:T(8,128)(2,1)S(1)} %bitcast.209), channel_id=1, source_target_pairs={{0,16},{16,0},{1,17},{17,1},{2,18},{18,2},{3,19},{19,3},{4,20},{20... | collective-permute-start | bytes 7962632 | tf_op jit(solution)/shard_map/ppermute | solution.py:35
  43.1 86.1 %collective-permute-start.39 = (bf16[1152,1152]{1,0:T(8,128)(2,1)}, bf16[1152,1152]{1,0:T(8,128)(2,1)S(1)}, u32[]{:S(2)}, u32[]{:S(2)}) collective-permute-start(bf16[1152,1152]{1,0:T(8,128)(2,1)} %bitcast.210), channel_id=1, source_target_pairs={{0,16},{16,0},{1,17},{17,1},{2,18},{18,2},{3,19},{19,3},{4,20},{20... | collective-permute-start | bytes 7962632 | tf_op jit(solution)/shard_map/ppermute | solution.py:35
  71.8 23.0 %collective-permute-start.23 = (bf16[512,640]{1,0:T(8,128)(2,1)S(1)}, bf16[512,640]{1,0:T(8,128)(2,1)S(1)}, u32[]{:S(2)}, u32[]{:S(2)}) collective-permute-start(bf16[512,640]{1,0:T(8,128)(2,1)S(1)} %get-tuple-element.707.own_ref.refs_7_), channel_id=1, source_target_pairs={{0,16},{16,0},{1,17},{17,1},{2,18},{18,2},{3,19},{19,3},{4,20},{20... | collective-permute-start | bytes 1966088 | tf_op jit(solution)/shard_map/ppermute | solution.py:35
  106.7 18.0 %collective-permute-start.35 = (bf16[64,1152]{1,0:T(8,128)(2,1)S(1)}, bf16[64,1152]{1,0:T(8,128)(2,1)S(1)}, u32[]{:S(2)}, u32[]{:S(2)}) collective-permute-start(bf16[64,1152]{1,0:T(8,128)(2,1)S(1)} %get-tuple-element.717), channel_id=1, source_target_pairs={{0,4},{4,0},{8,12},{12,8},{1,5},{5,1},{9,13},{13,9},{2,6},{6,2},{1... | collective-permute-start | bytes 442376 | tf_op jit(solution)/shard_map/ppermute | solution.py:39
  188.7 16.1 %collective-permute-start.63 = (bf16[128,1152]{1,0:T(8,128)(2,1)S(1)}, bf16[128,1152]{1,0:T(8,128)(2,1)S(1)}, u32[]{:S(2)}, u32[]{:S(2)}) collective-permute-start(bf16[128,1152]{1,0:T(8,128)(2,1)S(1)} %get-tuple-element.823.refs_0_), channel_id=1, source_target_pairs={{0,8},{8,0},{4,12},{12,4},{1,9},{9,1},{5,13},{13,5},{2,10},{10,2},... | collective-permute-start | bytes 884744 | tf_op jit(solution)/shard_map/ppermute | solution.py:43
  189.8 16.3 %collective-permute-start.64 = (bf16[128,1152]{1,0:T(8,128)(2,1)S(1)}, bf16[128,1152]{1,0:T(8,128)(2,1)S(1)}, u32[]{:S(2)}, u32[]{:S(2)}) collective-permute-start(bf16[128,1152]{1,0:T(8,128)(2,1)S(1)} %get-tuple-element.823.refs_0_), channel_id=1, source_target_pairs={{0,4},{4,0},{8,12},{12,8},{1,5},{5,1},{9,13},{13,9},{2,6},{6,2},{1... | collective-permute-start | bytes 884744 | tf_op jit(solution)/shard_map/ppermute | solution.py:39
  193.2 54.3 %collective-permute-start.110 = (bf16[128,1152]{1,0:T(8,128)(2,1)S(1)}, bf16[128,1152]{1,0:T(8,128)(2,1)S(1)}, u32[]{:S(2)}, u32[]{:S(2)}) collective-permute-start(bf16[128,1152]{1,0:T(8,128)(2,1)S(1)} %upstream.3.refs_0_), channel_id=1, source_target_pairs={{0,4},{4,0},{8,12},{12,8},{1,5},{5,1},{9,13},{13,9},{2,6},{6,2},{1... | collective-permute-start | bytes 884744 | tf_op jit(solution)/shard_map/ppermute | solution.py:39
  216.8 16.8 %collective-permute-start.77 = (bf16[512,640]{1,0:T(8,128)(2,1)S(1)}, bf16[512,640]{1,0:T(8,128)(2,1)S(1)}, u32[]{:S(2)}, u32[]{:S(2)}) collective-permute-start(bf16[512,640]{1,0:T(8,128)(2,1)S(1)} %get-tuple-element.843.own_ref.refs_7_), channel_id=1, source_target_pairs={{0,16},{16,0},{1,17},{17,1},{2,18},{18,2},{3,19},{19,3},{4,20},{20... | collective-permute-start | bytes 1966088 | tf_op jit(solution)/shard_map/ppermute | solution.py:35
  222.3 24.5 %collective-permute-start.76 = (bf16[512,640]{1,0:T(8,128)(2,1)S(1)}, bf16[512,640]{1,0:T(8,128)(2,1)S(1)}, u32[]{:S(2)}, u32[]{:S(2)}) collective-permute-start(bf16[512,640]{1,0:T(8,128)(2,1)S(1)} %get-tuple-element.842.own_ref.refs_7_), channel_id=1, source_target_pairs={{0,16},{16,0},{1,17},{17,1},{2,18},{18,2},{3,19},{19,3},{4,20},{20... | collective-permute-start | bytes 1966088 | tf_op jit(solution)/shard_map/ppermute | solution.py:35
  245.3 18.8 %collective-permute-start.111 = (bf16[128,1152]{1,0:T(8,128)(2,1)S(1)}, bf16[128,1152]{1,0:T(8,128)(2,1)S(1)}, u32[]{:S(2)}, u32[]{:S(2)}) collective-permute-start(bf16[128,1152]{1,0:T(8,128)(2,1)S(1)} %upstream.3.refs_0_), channel_id=1, source_target_pairs={{0,8},{8,0},{4,12},{12,4},{1,9},{9,1},{5,13},{13,5},{2,10},{10,2},... | collective-permute-start | bytes 884744 | tf_op jit(solution)/shard_map/ppermute | solution.py:43
  246.9 18.7 %collective-permute-start.115 = (bf16[128,1152]{1,0:T(8,128)(2,1)S(1)}, bf16[128,1152]{1,0:T(8,128)(2,1)S(1)}, u32[]{:S(2)}, u32[]{:S(2)}) collective-permute-start(bf16[128,1152]{1,0:T(8,128)(2,1)S(1)} %upstream.4.refs_0_), channel_id=1, source_target_pairs={{0,8},{8,0},{4,12},{12,4},{1,9},{9,1},{5,13},{13,5},{2,10},{10,2},... | collective-permute-start | bytes 884744 | tf_op jit(solution)/shard_map/ppermute | solution.py:43
  247.6 19.2 %collective-permute-start.116 = (bf16[128,1152]{1,0:T(8,128)(2,1)S(1)}, bf16[128,1152]{1,0:T(8,128)(2,1)S(1)}, u32[]{:S(2)}, u32[]{:S(2)}) collective-permute-start(bf16[128,1152]{1,0:T(8,128)(2,1)S(1)} %upstream.4.refs_0_), channel_id=1, source_target_pairs={{0,4},{4,0},{8,12},{12,8},{1,5},{5,1},{9,13},{13,9},{2,6},{6,2},{1... | collective-permute-start | bytes 884744 | tf_op jit(solution)/shard_map/ppermute | solution.py:39
  253.3 16.6 %collective-permute-start.75 = (bf16[64,1152]{1,0:T(8,128)(2,1)S(1)}, bf16[64,1152]{1,0:T(8,128)(2,1)S(1)}, u32[]{:S(2)}, u32[]{:S(2)}) collective-permute-start(bf16[64,1152]{1,0:T(8,128)(2,1)S(1)} %get-tuple-element.841), channel_id=1, source_target_pairs={{0,4},{4,0},{8,12},{12,8},{1,5},{5,1},{9,13},{13,9},{2,6},{6,2},{1... | collective-permute-start | bytes 442376 | tf_op jit(solution)/shard_map/ppermute | solution.py:39
  264.1 22.8 %collective-permute-start.121 = (bf16[128,1152]{1,0:T(8,128)(2,1)S(1)}, bf16[128,1152]{1,0:T(8,128)(2,1)S(1)}, u32[]{:S(2)}, u32[]{:S(2)}) collective-permute-start(bf16[128,1152]{1,0:T(8,128)(2,1)S(1)} %upstream.5.refs_0_), channel_id=1, source_target_pairs={{0,8},{8,0},{4,12},{12,4},{1,9},{9,1},{5,13},{13,5},{2,10},{10,2},... | collective-permute-start | bytes 884744 | tf_op jit(solution)/shard_map/ppermute | solution.py:43
  265.6 18.3 %collective-permute-start.84 = (bf16[128,1152]{1,0:T(8,128)(2,1)S(1)}, bf16[128,1152]{1,0:T(8,128)(2,1)S(1)}, u32[]{:S(2)}, u32[]{:S(2)}) collective-permute-start(bf16[128,1152]{1,0:T(8,128)(2,1)S(1)} %get-tuple-element.863), channel_id=1, source_target_pairs={{0,4},{4,0},{8,12},{12,8},{1,5},{5,1},{9,13},{13,9},{2,6},{6,2},{1... | collective-permute-start | bytes 884744 | tf_op jit(solution)/shard_map/ppermute | solution.py:39
  266.8 18.3 %collective-permute-start.85 = (bf16[128,1152]{1,0:T(8,128)(2,1)S(1)}, bf16[128,1152]{1,0:T(8,128)(2,1)S(1)}, u32[]{:S(2)}, u32[]{:S(2)}) collective-permute-start(bf16[128,1152]{1,0:T(8,128)(2,1)S(1)} %get-tuple-element.864), channel_id=1, source_target_pairs={{0,8},{8,0},{4,12},{12,4},{1,9},{9,1},{5,13},{13,5},{2,10},{10,2},... | collective-permute-start | bytes 884744 | tf_op jit(solution)/shard_map/ppermute | solution.py:43
  287.8 23.2 %collective-permute-start.90 = (bf16[128,1152]{1,0:T(8,128)(2,1)S(1)}, bf16[128,1152]{1,0:T(8,128)(2,1)S(1)}, u32[]{:S(2)}, u32[]{:S(2)}) collective-permute-start(bf16[128,1152]{1,0:T(8,128)(2,1)S(1)} %get-tuple-element.897.refs_0_), channel_id=1, source_target_pairs={{0,8},{8,0},{4,12},{12,4},{1,9},{9,1},{5,13},{13,5},{2,10},{10,2},... | collective-permute-start | bytes 884744 | tf_op jit(solution)/shard_map/ppermute | solution.py:43
  299.1 22.8 %collective-permute-start.125 = (bf16[64,1152]{1,0:T(8,128)(2,1)S(1)}, bf16[64,1152]{1,0:T(8,128)(2,1)S(1)}, u32[]{:S(2)}, u32[]{:S(2)}) collective-permute-start(bf16[64,1152]{1,0:T(8,128)(2,1)S(1)} %get-tuple-element.944), channel_id=1, source_target_pairs={{0,4},{4,0},{8,12},{12,8},{1,5},{5,1},{9,13},{13,9},{2,6},{6,2},{1... | collective-permute-start | bytes 442376 | tf_op jit(solution)/shard_map/ppermute | solution.py:39
  326.2 21.8 %collective-permute-start.117 = (bf16[128,1152]{1,0:T(8,128)(2,1)S(1)}, bf16[128,1152]{1,0:T(8,128)(2,1)S(1)}, u32[]{:S(2)}, u32[]{:S(2)}) collective-permute-start(bf16[128,1152]{1,0:T(8,128)(2,1)S(1)} %get-tuple-element.953), channel_id=1, source_target_pairs={{0,4},{4,0},{8,12},{12,8},{1,5},{5,1},{9,13},{13,9},{2,6},{6,2},{1... | collective-permute-start | bytes 884744 | tf_op jit(solution)/shard_map/ppermute | solution.py:39
  326.9 21.4 %collective-permute-start.118 = (bf16[128,1152]{1,0:T(8,128)(2,1)S(1)}, bf16[128,1152]{1,0:T(8,128)(2,1)S(1)}, u32[]{:S(2)}, u32[]{:S(2)}) collective-permute-start(bf16[128,1152]{1,0:T(8,128)(2,1)S(1)} %get-tuple-element.954), channel_id=1, source_target_pairs={{0,8},{8,0},{4,12},{12,4},{1,9},{9,1},{5,13},{13,5},{2,10},{10,2},... | collective-permute-start | bytes 884744 | tf_op jit(solution)/shard_map/ppermute | solution.py:43
  348.0 17.0 %collective-permute-start.128 = (bf16[128,1152]{1,0:T(8,128)(2,1)S(1)}, bf16[128,1152]{1,0:T(8,128)(2,1)S(1)}, u32[]{:S(2)}, u32[]{:S(2)}) collective-permute-start(bf16[128,1152]{1,0:T(8,128)(2,1)S(1)} %get-tuple-element.977), channel_id=1, source_target_pairs={{0,4},{4,0},{8,12},{12,8},{1,5},{5,1},{9,13},{13,9},{2,6},{6,2},{1... | collective-permute-start | bytes 884744 | tf_op jit(solution)/shard_map/ppermute | solution.py:39
  356.0 16.1 %collective-permute-start.102 = (bf16[128,1152]{1,0:T(8,128)(2,1)S(1)}, bf16[128,1152]{1,0:T(8,128)(2,1)S(1)}, u32[]{:S(2)}, u32[]{:S(2)}) collective-permute-start(bf16[128,1152]{1,0:T(8,128)(2,1)S(1)} %get-tuple-element.910), channel_id=1, source_target_pairs={{0,8},{8,0},{4,12},{12,4},{1,9},{9,1},{5,13},{13,5},{2,10},{10,2},... | collective-permute-start | bytes 884744 | tf_op jit(solution)/shard_map/ppermute | solution.py:43
  366.1 23.7 %collective-permute-start.133 = (bf16[128,1152]{1,0:T(8,128)(2,1)S(1)}, bf16[128,1152]{1,0:T(8,128)(2,1)S(1)}, u32[]{:S(2)}, u32[]{:S(2)}) collective-permute-start(bf16[128,1152]{1,0:T(8,128)(2,1)S(1)} %get-tuple-element.991), channel_id=1, source_target_pairs={{0,4},{4,0},{8,12},{12,8},{1,5},{5,1},{9,13},{13,9},{2,6},{6,2},{1... | collective-permute-start | bytes 884744 | tf_op jit(solution)/shard_map/ppermute | solution.py:39
  368.1 23.2 %collective-permute-start.134 = (bf16[128,1152]{1,0:T(8,128)(2,1)S(1)}, bf16[128,1152]{1,0:T(8,128)(2,1)S(1)}, u32[]{:S(2)}, u32[]{:S(2)}) collective-permute-start(bf16[128,1152]{1,0:T(8,128)(2,1)S(1)} %get-tuple-element.992), channel_id=1, source_target_pairs={{0,8},{8,0},{4,12},{12,4},{1,9},{9,1},{5,13},{13,5},{2,10},{10,2},... | collective-permute-start | bytes 884744 | tf_op jit(solution)/shard_map/ppermute | solution.py:43
  370.6 21.2 %collective-permute-start.106 = (bf16[128,1152]{1,0:T(8,128)(2,1)S(1)}, bf16[128,1152]{1,0:T(8,128)(2,1)S(1)}, u32[]{:S(2)}, u32[]{:S(2)}) collective-permute-start(bf16[128,1152]{1,0:T(8,128)(2,1)S(1)} %get-tuple-element.923), channel_id=1, source_target_pairs={{0,4},{4,0},{8,12},{12,8},{1,5},{5,1},{9,13},{13,9},{2,6},{6,2},{1... | collective-permute-start | bytes 884744 | tf_op jit(solution)/shard_map/ppermute | solution.py:39
  373.6 18.8 %collective-permute-start.107 = (bf16[128,1152]{1,0:T(8,128)(2,1)S(1)}, bf16[128,1152]{1,0:T(8,128)(2,1)S(1)}, u32[]{:S(2)}, u32[]{:S(2)}) collective-permute-start(bf16[128,1152]{1,0:T(8,128)(2,1)S(1)} %get-tuple-element.924), channel_id=1, source_target_pairs={{0,8},{8,0},{4,12},{12,4},{1,9},{9,1},{5,13},{13,5},{2,10},{10,2},... | collective-permute-start | bytes 884744 | tf_op jit(solution)/shard_map/ppermute | solution.py:43
  412.0 34.1 %collective-permute-start.148 = (bf16[1152,1152]{1,0:T(8,128)(2,1)S(1)}, bf16[1152,1152]{1,0:T(8,128)(2,1)S(1)}, u32[]{:S(2)}, u32[]{:S(2)}) collective-permute-start(bf16[1152,1152]{1,0:T(8,128)(2,1)S(1)} %get-tuple-element.1045), channel_id=1, source_target_pairs={{0,16},{16,0},{1,17},{17,1},{2,18},{18,2},{3,19},{19,3},{4,20},{20... | collective-permute-start | bytes 7962632 | tf_op jit(solution)/shard_map/ppermute | solution.py:35
  431.9 17.0 %collective-permute-start.146 = (bf16[64,1152]{1,0:T(8,128)(2,1)}, bf16[64,1152]{1,0:T(8,128)(2,1)S(1)}, u32[]{:S(2)}, u32[]{:S(2)}) collective-permute-start(bf16[64,1152]{1,0:T(8,128)(2,1)} %get-tuple-element.1032), channel_id=1, source_target_pairs={{0,4},{4,0},{8,12},{12,8},{1,5},{5,1},{9,13},{13,9},{2,6},{6,2},{1... | collective-permute-start | bytes 442376 | tf_op jit(solution)/shard_map/ppermute | solution.py:39
  442.7 28.8 %collective-permute-start.141 = (bf16[512,640]{1,0:T(8,128)(2,1)}, bf16[512,640]{1,0:T(8,128)(2,1)}, u32[]{:S(2)}, u32[]{:S(2)}) collective-permute-start(bf16[512,640]{1,0:T(8,128)(2,1)} %get-tuple-element.1042), channel_id=1, source_target_pairs={{0,16},{16,0},{1,17},{17,1},{2,18},{18,2},{3,19},{19,3},{4,20},{20... | collective-permute-start | bytes 1966088 | tf_op jit(solution)/shard_map/ppermute | solution.py:35
  444.5 17.4 %collective-permute-start.144 = (bf16[64,1152]{1,0:T(8,128)(2,1)}, bf16[64,1152]{1,0:T(8,128)(2,1)}, u32[]{:S(2)}, u32[]{:S(2)}) collective-permute-start(bf16[64,1152]{1,0:T(8,128)(2,1)} %get-tuple-element.1043), channel_id=1, source_target_pairs={{0,8},{8,0},{4,12},{12,4},{1,9},{9,1},{5,13},{13,5},{2,10},{10,2},... | collective-permute-start | bytes 442376 | tf_op jit(solution)/shard_map/ppermute | solution.py:43
  448.6 256.1 %reduce-scatter.7.cloned.1.call-start = ((), (), s32[]{:S(2)}) async-start(), calls=%async_computation.5 | async-start | bytes 1843200 | tf_op jit(solution)/shard_map/reduce_scatter | solution.py:881
  485.3 16.1 %collective-permute-start.151 = (bf16[64,1152]{1,0:T(8,128)(2,1)S(1)}, bf16[64,1152]{1,0:T(8,128)(2,1)S(1)}, u32[]{:S(2)}, u32[]{:S(2)}) collective-permute-start(bf16[64,1152]{1,0:T(8,128)(2,1)S(1)} %get-tuple-element.1067), channel_id=1, source_target_pairs={{0,8},{8,0},{4,12},{12,4},{1,9},{9,1},{5,13},{13,5},{2,10},{10,2},... | collective-permute-start | bytes 442376 | tf_op jit(solution)/shard_map/ppermute | solution.py:43
  485.8 16.0 %collective-permute-start.152 = (bf16[64,1152]{1,0:T(8,128)(2,1)S(1)}, bf16[64,1152]{1,0:T(8,128)(2,1)S(1)}, u32[]{:S(2)}, u32[]{:S(2)}) collective-permute-start(bf16[64,1152]{1,0:T(8,128)(2,1)S(1)} %get-tuple-element.1068), channel_id=1, source_target_pairs={{0,4},{4,0},{8,12},{12,8},{1,5},{5,1},{9,13},{13,9},{2,6},{6,2},{1... | collective-permute-start | bytes 442376 | tf_op jit(solution)/shard_map/ppermute | solution.py:39
  507.7 18.3 %collective-permute-start.163 = (bf16[64,1152]{1,0:T(8,128)(2,1)S(1)}, bf16[64,1152]{1,0:T(8,128)(2,1)S(1)}, u32[]{:S(2)}, u32[]{:S(2)}) collective-permute-start(bf16[64,1152]{1,0:T(8,128)(2,1)S(1)} %get-tuple-element.1096), channel_id=1, source_target_pairs={{0,8},{8,0},{4,12},{12,4},{1,9},{9,1},{5,13},{13,5},{2,10},{10,2},... | collective-permute-start | bytes 442376 | tf_op jit(solution)/shard_map/ppermute | solution.py:43
  509.1 17.6 %collective-permute-start.164 = (bf16[64,1152]{1,0:T(8,128)(2,1)S(1)}, bf16[64,1152]{1,0:T(8,128)(2,1)S(1)}, u32[]{:S(2)}, u32[]{:S(2)}) collective-permute-start(bf16[64,1152]{1,0:T(8,128)(2,1)S(1)} %get-tuple-element.1097), channel_id=1, source_target_pairs={{0,4},{4,0},{8,12},{12,8},{1,5},{5,1},{9,13},{13,9},{2,6},{6,2},{1... | collective-permute-start | bytes 442376 | tf_op jit(solution)/shard_map/ppermute | solution.py:39
  511.6 15.9 %collective-permute-start.167 = (bf16[128,1152]{1,0:T(8,128)(2,1)S(1)}, bf16[128,1152]{1,0:T(8,128)(2,1)S(1)}, u32[]{:S(2)}, u32[]{:S(2)}) collective-permute-start(bf16[128,1152]{1,0:T(8,128)(2,1)S(1)} %get-tuple-element.1155.refs_0_), channel_id=1, source_target_pairs={{0,8},{8,0},{4,12},{12,4},{1,9},{9,1},{5,13},{13,5},{2,10},{10,2},... | collective-permute-start | bytes 884744 | tf_op jit(solution)/shard_map/ppermute | solution.py:43
  526.7 24.7 %collective-permute-start.179 = (bf16[1152,640]{1,0:T(8,128)(2,1)S(1)}, bf16[1152,640]{1,0:T(8,128)(2,1)S(1)}, u32[]{:S(2)}, u32[]{:S(2)}) collective-permute-start(bf16[1152,640]{1,0:T(8,128)(2,1)S(1)} %get-tuple-element.1151), channel_id=1, source_target_pairs={{0,16},{16,0},{1,17},{17,1},{2,18},{18,2},{3,19},{19,3},{4,20},{20... | collective-permute-start | bytes 4423688 | tf_op jit(solution)/shard_map/ppermute | solution.py:35
  548.0 21.4 %collective-permute-start.175 = (bf16[64,1152]{1,0:T(8,128)(2,1)}, bf16[64,1152]{1,0:T(8,128)(2,1)}, u32[]{:S(2)}, u32[]{:S(2)}) collective-permute-start(bf16[64,1152]{1,0:T(8,128)(2,1)} %get-tuple-element.1149), channel_id=1, source_target_pairs={{0,8},{8,0},{4,12},{12,4},{1,9},{9,1},{5,13},{13,5},{2,10},{10,2},... | collective-permute-start | bytes 442376 | tf_op jit(solution)/shard_map/ppermute | solution.py:43
  548.6 22.3 %collective-permute-start.176 = (bf16[64,1152]{1,0:T(8,128)(2,1)}, bf16[64,1152]{1,0:T(8,128)(2,1)}, u32[]{:S(2)}, u32[]{:S(2)}) collective-permute-start(bf16[64,1152]{1,0:T(8,128)(2,1)} %get-tuple-element.1150), channel_id=1, source_target_pairs={{0,4},{4,0},{8,12},{12,8},{1,5},{5,1},{9,13},{13,9},{2,6},{6,2},{1... | collective-permute-start | bytes 442376 | tf_op jit(solution)/shard_map/ppermute | solution.py:39
  551.4 30.7 %collective-permute-start.171 = (bf16[64,1152]{1,0:T(8,128)(2,1)}, bf16[64,1152]{1,0:T(8,128)(2,1)S(1)}, u32[]{:S(2)}, u32[]{:S(2)}) collective-permute-start(bf16[64,1152]{1,0:T(8,128)(2,1)} %get-tuple-element.1146), channel_id=1, source_target_pairs={{0,8},{8,0},{4,12},{12,4},{1,9},{9,1},{5,13},{13,5},{2,10},{10,2},... | collective-permute-start | bytes 442376 | tf_op jit(solution)/shard_map/ppermute | solution.py:43
  553.5 30.8 %collective-permute-start.172 = (bf16[64,1152]{1,0:T(8,128)(2,1)}, bf16[64,1152]{1,0:T(8,128)(2,1)}, u32[]{:S(2)}, u32[]{:S(2)}) collective-permute-start(bf16[64,1152]{1,0:T(8,128)(2,1)} %copy-done.257), channel_id=1, source_target_pairs={{0,4},{4,0},{8,12},{12,8},{1,5},{5,1},{9,13},{13,9},{2,6},{6,2},{1... | collective-permute-start | bytes 442376 | tf_op jit(solution)/shard_map/ppermute | solution.py:39
  591.2 174.4 %reduce-scatter.9.cloned.1.call-start = ((), (), s32[]{:S(2)}) async-start(), calls=%async_computation.6 | async-start | bytes 3317760 | tf_op jit(solution)/shard_map/reduce_scatter | solution.py:881
  591.3 28.3 %collective-permute-start.218 = (f32[2,3,128]{2,1,0:T(4,128)}, f32[2,3,128]{2,1,0:T(4,128)}, u32[]{:S(2)}, u32[]{:S(2)}) collective-permute-start(f32[2,3,128]{2,1,0:T(4,128)} %fusion.35), channel_id=1, source_target_pairs={{0,16},{16,0},{1,17},{17,1},{2,18},{18,2},{3,19},{19,3},{4,20},{20... | collective-permute-start | bytes 9224 | tf_op jit(solution)/shard_map/ppermute | solution.py:35
  593.3 27.7 %collective-permute-start.112 = (f32[3,128,1152]{2,1,0:T(8,128)}, f32[3,128,1152]{2,1,0:T(8,128)}, u32[]{:S(2)}, u32[]{:S(2)}) collective-permute-start(f32[3,128,1152]{2,1,0:T(8,128)} %fusion.2), channel_id=1, source_target_pairs={{0,16},{16,0},{1,17},{17,1},{2,18},{18,2},{3,19},{19,3},{4,20},{20... | collective-permute-start | bytes 5308424 | tf_op jit(solution)/shard_map/ppermute | solution.py:35
  618.9 36.9 %collective-permute-start.201 = (bf16[1152,1152]{1,0:T(8,128)(2,1)}, bf16[1152,1152]{1,0:T(8,128)(2,1)}, u32[]{:S(2)}, u32[]{:S(2)}) collective-permute-start(bf16[1152,1152]{1,0:T(8,128)(2,1)} %get-tuple-element.1239), channel_id=1, source_target_pairs={{0,16},{16,0},{1,17},{17,1},{2,18},{18,2},{3,19},{19,3},{4,20},{20... | collective-permute-start | bytes 7962632 | tf_op jit(solution)/shard_map/ppermute | solution.py:35
  641.7 18.9 %collective-permute-start.199 = (bf16[64,1152]{1,0:T(8,128)(2,1)}, bf16[64,1152]{1,0:T(8,128)(2,1)}, u32[]{:S(2)}, u32[]{:S(2)}) collective-permute-start(bf16[64,1152]{1,0:T(8,128)(2,1)} %get-tuple-element.1226), channel_id=1, source_target_pairs={{0,4},{4,0},{8,12},{12,8},{1,5},{5,1},{9,13},{13,9},{2,6},{6,2},{1... | collective-permute-start | bytes 442376 | tf_op jit(solution)/shard_map/ppermute | solution.py:39
  643.2 17.4 %collective-permute-start.200 = (bf16[64,1152]{1,0:T(8,128)(2,1)}, bf16[64,1152]{1,0:T(8,128)(2,1)}, u32[]{:S(2)}, u32[]{:S(2)}) collective-permute-start(bf16[64,1152]{1,0:T(8,128)(2,1)} %get-tuple-element.1227), channel_id=1, source_target_pairs={{0,8},{8,0},{4,12},{12,4},{1,9},{9,1},{5,13},{13,5},{2,10},{10,2},... | collective-permute-start | bytes 442376 | tf_op jit(solution)/shard_map/ppermute | solution.py:43
  652.6 34.0 %collective-permute-start.194 = (bf16[512,640]{1,0:T(8,128)(2,1)}, bf16[512,640]{1,0:T(8,128)(2,1)}, u32[]{:S(2)}, u32[]{:S(2)}) collective-permute-start(bf16[512,640]{1,0:T(8,128)(2,1)} %get-tuple-element.1236), channel_id=1, source_target_pairs={{0,16},{16,0},{1,17},{17,1},{2,18},{18,2},{3,19},{19,3},{4,20},{20... | collective-permute-start | bytes 1966088 | tf_op jit(solution)/shard_map/ppermute | solution.py:35
  654.4 22.1 %collective-permute-start.197 = (bf16[64,1152]{1,0:T(8,128)(2,1)}, bf16[64,1152]{1,0:T(8,128)(2,1)}, u32[]{:S(2)}, u32[]{:S(2)}) collective-permute-start(bf16[64,1152]{1,0:T(8,128)(2,1)} %get-tuple-element.1237), channel_id=1, source_target_pairs={{0,8},{8,0},{4,12},{12,4},{1,9},{9,1},{5,13},{13,5},{2,10},{10,2},... | collective-permute-start | bytes 442376 | tf_op jit(solution)/shard_map/ppermute | solution.py:43
  655.7 20.8 %collective-permute-start.198 = (bf16[64,1152]{1,0:T(8,128)(2,1)}, bf16[64,1152]{1,0:T(8,128)(2,1)}, u32[]{:S(2)}, u32[]{:S(2)}) collective-permute-start(bf16[64,1152]{1,0:T(8,128)(2,1)} %get-tuple-element.1238), channel_id=1, source_target_pairs={{0,4},{4,0},{8,12},{12,8},{1,5},{5,1},{9,13},{13,9},{2,6},{6,2},{1... | collective-permute-start | bytes 442376 | tf_op jit(solution)/shard_map/ppermute | solution.py:39
  660.4 123.5 %reduce-scatter.11.cloned.1.call-start = ((), (), s32[]{:S(2)}) async-start(), calls=%async_computation.7 | async-start | bytes 1843200 | tf_op jit(solution)/shard_map/reduce_scatter | solution.py:881
  686.6 18.1 %collective-permute-start.206 = (bf16[512,640]{1,0:T(8,128)(2,1)}, bf16[512,640]{1,0:T(8,128)(2,1)S(1)}, u32[]{:S(2)}, u32[]{:S(2)}) collective-permute-start(bf16[512,640]{1,0:T(8,128)(2,1)} %get-tuple-element.1271), channel_id=1, source_target_pairs={{0,16},{16,0},{1,17},{17,1},{2,18},{18,2},{3,19},{19,3},{4,20},{20... | collective-permute-start | bytes 1966088 | tf_op jit(solution)/shard_map/ppermute | solution.py:35
  694.7 16.2 %collective-permute-start.207 = (bf16[512,640]{1,0:T(8,128)(2,1)}, bf16[512,640]{1,0:T(8,128)(2,1)}, u32[]{:S(2)}, u32[]{:S(2)}) collective-permute-start(bf16[512,640]{1,0:T(8,128)(2,1)} %get-tuple-element.1275), channel_id=1, source_target_pairs={{0,16},{16,0},{1,17},{17,1},{2,18},{18,2},{3,19},{19,3},{4,20},{20... | collective-permute-start | bytes 1966088 | tf_op jit(solution)/shard_map/ppermute | solution.py:35
  702.7 26.2 %collective-permute-start.204 = (bf16[64,1152]{1,0:T(8,128)(2,1)}, bf16[64,1152]{1,0:T(8,128)(2,1)}, u32[]{:S(2)}, u32[]{:S(2)}) collective-permute-start(bf16[64,1152]{1,0:T(8,128)(2,1)} %get-tuple-element.1261), channel_id=1, source_target_pairs={{0,8},{8,0},{4,12},{12,4},{1,9},{9,1},{5,13},{13,5},{2,10},{10,2},... | collective-permute-start | bytes 442376 | tf_op jit(solution)/shard_map/ppermute | solution.py:43
  703.4 26.8 %collective-permute-start.205 = (bf16[64,1152]{1,0:T(8,128)(2,1)}, bf16[64,1152]{1,0:T(8,128)(2,1)}, u32[]{:S(2)}, u32[]{:S(2)}) collective-permute-start(bf16[64,1152]{1,0:T(8,128)(2,1)} %get-tuple-element.1262), channel_id=1, source_target_pairs={{0,4},{4,0},{8,12},{12,8},{1,5},{5,1},{9,13},{13,9},{2,6},{6,2},{1... | collective-permute-start | bytes 442376 | tf_op jit(solution)/shard_map/ppermute | solution.py:39
  726.0 19.3 %collective-permute-start.216 = (bf16[1152,640]{1,0:T(8,128)(2,1)S(1)}, bf16[1152,640]{1,0:T(8,128)(2,1)S(1)}, u32[]{:S(2)}, u32[]{:S(2)}) collective-permute-start(bf16[1152,640]{1,0:T(8,128)(2,1)S(1)} %get-tuple-element.1317), channel_id=1, source_target_pairs={{0,16},{16,0},{1,17},{17,1},{2,18},{18,2},{3,19},{19,3},{4,20},{20... | collective-permute-start | bytes 4423688 | tf_op jit(solution)/shard_map/ppermute | solution.py:35
  736.6 47.3 %collective-permute-start.219 = (bf16[24,1152]{1,0:T(8,128)(2,1)}, bf16[24,1152]{1,0:T(8,128)(2,1)}, u32[]{:S(2)}, u32[]{:S(2)}) collective-permute-start(bf16[24,1152]{1,0:T(8,128)(2,1)} %get-tuple-element.1438), channel_id=1, source_target_pairs={{0,1},{1,2},{2,3},{3,0},{4,5},{5,6},{6,7},{7,4},{8,9},{9,10},{10,1... | collective-permute-start | bytes 165896 | tf_op jit(solution)/shard_map/ppermute | solution.py:190
  738.1 47.0 %collective-permute-start.220 = (bf16[24,1152]{1,0:T(8,128)(2,1)}, bf16[24,1152]{1,0:T(8,128)(2,1)}, u32[]{:S(2)}, u32[]{:S(2)}) collective-permute-start(bf16[24,1152]{1,0:T(8,128)(2,1)} %get-tuple-element.1438), channel_id=1, source_target_pairs={{0,2},{1,3},{2,0},{3,1},{4,6},{5,7},{6,4},{7,5},{8,10},{9,11},{10,... | collective-permute-start | bytes 165896 | tf_op jit(solution)/shard_map/ppermute | solution.py:190
  745.3 41.4 %collective-permute-start.221 = (bf16[24,1152]{1,0:T(8,128)(2,1)}, bf16[24,1152]{1,0:T(8,128)(2,1)}, u32[]{:S(2)}, u32[]{:S(2)}) collective-permute-start(bf16[24,1152]{1,0:T(8,128)(2,1)} %get-tuple-element.1438), channel_id=1, source_target_pairs={{0,3},{1,0},{2,1},{3,2},{4,7},{5,4},{6,5},{7,6},{8,11},{9,8},{10,9... | collective-permute-start | bytes 165896 | tf_op jit(solution)/shard_map/ppermute | solution.py:190
  765.6 22.2 %collective-permute-start.225 = (bf16[24,1728]{1,0:T(8,128)(2,1)S(1)}, bf16[24,1728]{1,0:T(8,128)(2,1)S(1)}, u32[]{:S(2)}, u32[]{:S(2)}) collective-permute-start(bf16[24,1728]{1,0:T(8,128)(2,1)S(1)} %fusion.24), channel_id=1, source_target_pairs={{0,1},{1,2},{2,3},{3,0},{4,5},{5,6},{6,7},{7,4},{8,9},{9,10},{10,1... | collective-permute-start | bytes 248840 | tf_op jit(solution)/shard_map/ppermute | solution.py:190
  766.3 21.5 %collective-permute-start.226 = (bf16[24,1728]{1,0:T(8,128)(2,1)S(1)}, bf16[24,1728]{1,0:T(8,128)(2,1)S(1)}, u32[]{:S(2)}, u32[]{:S(2)}) collective-permute-start(bf16[24,1728]{1,0:T(8,128)(2,1)S(1)} %fusion.24), channel_id=1, source_target_pairs={{0,2},{1,3},{2,0},{3,1},{4,6},{5,7},{6,4},{7,5},{8,10},{9,11},{10,... | collective-permute-start | bytes 248840 | tf_op jit(solution)/shard_map/ppermute | solution.py:190
  (579 other events, 7813.0 us)
Sparse Core Ops, SparseCore 0:
  448.7 53.0 reduce-scatter.4
  591.3 34.0 reduce-scatter.6
  660.5 53.0 reduce-scatter.8
  748.4 35.4 reduce-scatter.10

commit v5 on v4

--- a/solution.py
+++ b/solution.py
@@ -916,7 +916,7 @@
             behind = step
             if i == 0 and behind in ready:
                 reduced(*ready[behind])
-            if i == 1 and behind in extra:
+            if i == (1 if extra.get(behind, (wide,))[0] is wide else 0) and behind in extra:
                 work, b = extra[behind]
                 work(b)
             if i == 0 and behind in settled:

time: 813 us -> 812 us (level)
  transfers between devices with their start and end apart: 234 -> 234, of which waited for: 63 -> 64; matrix products, arithmetic and copies ran while one was open for 5% -> 5% of each run, Pallas kernels for 33% -> 33%
where the time goes in v5:
time: 812 us; the launch traced here: 802 us
  Pallas kernels  279 us (34%)
  starting transfers between devices  220 us (27%)
  waiting for transfers between devices  164 us (20%)
  local copies, waits for them, and re-layouts  82 us (10%)
  other arithmetic  30 us (4%)
  between operations  19.1 us (2%)
    pallas_call x115, Pallas kernels, run(): pl.pallas_call(kernel, out_shape=tuple(shapes), compiler_params=pltpu.Com...  239 us
    ppermute x98, starting transfers between devices, along_y(): return lax.ppermute(block, 'tensor', [(0, 2), (2, 0), (1, 3), (3, 1)])  106 us
    ppermute x99, starting transfers between devices, along_x(): return lax.ppermute(block, 'tensor', [(0, 1), (1, 0), (2, 3), (3, 2)])  101 us
    unnamed x820, local copies, waits for them, and re-layouts  76.8 us
    ppermute x98, waiting for transfers between devices, along_y(): return lax.ppermute(block, 'tensor', [(0, 2), (2, 0), (1, 3), (3, 1)])  74.3 us
    ppermute x99, waiting for transfers between devices, along_x(): return lax.ppermute(block, 'tensor', [(0, 1), (1, 0), (2, 3), (3, 2)])  70.6 us
    pallas_call x4, Pallas kernels, weight_sums(): pl.pallas_call(kernel, grid=(depth // step,), in_specs=[pl.BlockSpec(memo...  40.6 us
    reduce_scatter x4, waiting for transfers between devices, reduced(): lax.psum_scatter(total, 'dp', scatter_dimension=0, tiled=True)  16.7 us
  transfers between devices with their start and end apart: 234, of which 64 were waited for; matrix products, arithmetic and copies ran while one was open for 5% of the time, Pallas kernels for 33%

profile of v5, /device:TPU:0, one launch (start us, length us, event | category | flops | bytes accessed | tf_op | source)
XLA Modules:
  0.0 801.8 jit_solution(2831255331151833014)
XLA Ops:
  7.2 4.2 fusion
  11.4 3.0 collective-permute-start.5
  40.1 3.0 collective-permute-done.14.far.refs_1_
  55.0 3.8 qkv.6
  61.4 3.6 qkv.7
  66.7 4.0 qkv.8
  71.9 8.5 %attend.6 = (bf16[512,288]{1,0:T(8,128)(2,1)S(1)}, f32[4,512]{1,0:T(4,128)S(1)}, bf16[128,1152]{1,0:T(8,128)(2,1)S(1)}, bf16[128,1152]{1,0:T(8,128)(2,1)S(1)}, b...) custom-call(bf16[512,288]{1,0:T(8,128)(2,1)S(1)} %get-tuple-element.682.query_ref.refs_6_, ...), custom_call_target="tpu_custom_call" | custom-call | flops 8999999488 | bytes 1 | tf_op jit(solution)/shard_map/attend/pallas_call | solution.py:217
  82.6 8.7 %attend.7 = (bf16[512,288]{1,0:T(8,128)(2,1)S(1)}, f32[4,512]{1,0:T(4,128)S(1)}, bf16[128,1152]{1,0:T(8,128)(2,1)S(1)}, bf16[128,1152]{1,0:T(8,128)(2,1)S(1)}, b...) custom-call(bf16[512,288]{1,0:T(8,128)(2,1)S(1)} %get-tuple-element.693.query_ref.refs_6_, ...), custom_call_target="tpu_custom_call" | custom-call | flops 8999999488 | bytes 1 | tf_op jit(solution)/shard_map/attend/pallas_call | solution.py:217
  95.4 8.5 %attend.8 = (bf16[512,288]{1,0:T(8,128)(2,1)S(1)}, f32[4,512]{1,0:T(4,128)S(1)}, bf16[128,1152]{1,0:T(8,128)(2,1)S(1)}, bf16[128,1152]{1,0:T(8,128)(2,1)S(1)}, b...) custom-call(bf16[512,288]{1,0:T(8,128)(2,1)S(1)} %get-tuple-element.699.query_ref.refs_6_, ...), custom_call_target="tpu_custom_call" | custom-call | flops 8999999488 | bytes 1 | tf_op jit(solution)/shard_map/attend/pallas_call | solution.py:217
  107.1 4.2 collective-permute-done.22.refs_4_
  114.7 2.5 collective-permute-done.31.first.refs_1_
  119.4 5.0 collective-permute-done.32.second.refs_2_
  132.5 7.6 collective-permute-done.33.refs_3_
  145.2 5.0 feed.6
  156.3 5.0 feed.7
  165.7 5.4 feed.8
  179.2 3.4 collective-permute-done.55.first.refs_1_
  194.8 6.9 collective-permute-done.57.refs_3_
  222.4 8.7 %attend.9 = (bf16[512,288]{1,0:T(8,128)(2,1)S(1)}, f32[4,512]{1,0:T(4,128)S(1)}, bf16[128,1152]{1,0:T(8,128)(2,1)S(1)}, bf16[128,1152]{1,0:T(8,128)(2,1)S(1)}, b...) custom-call(bf16[512,288]{1,0:T(8,128)(2,1)S(1)} %get-tuple-element.818.query_ref.refs_6_, ...), custom_call_target="tpu_custom_call" | custom-call | flops 8999999488 | bytes 1 | tf_op jit(solution)/shard_map/attend/pallas_call | solution.py:217
  233.6 8.8 %attend.10 = (bf16[512,288]{1,0:T(8,128)(2,1)S(1)}, f32[4,512]{1,0:T(4,128)S(1)}, bf16[128,1152]{1,0:T(8,128)(2,1)S(1)}, bf16[128,1152]{1,0:T(8,128)(2,1)S(1)}, ...) custom-call(bf16[512,288]{1,0:T(8,128)(2,1)S(1)} %get-tuple-element.828.query_ref.refs_6_, ...), custom_call_target="tpu_custom_call" | custom-call | flops 8999999488 | bytes 1 | tf_op jit(solution)/shard_map/attend/pallas_call | solution.py:217
  248.2 4.2 collective-permute-done.78.first.refs_1_
  254.8 8.6 %attend.11 = (bf16[512,288]{1,0:T(8,128)(2,1)S(1)}, f32[4,512]{1,0:T(4,128)S(1)}, bf16[128,1152]{1,0:T(8,128)(2,1)S(1)}, bf16[128,1152]{1,0:T(8,128)(2,1)S(1)}, ...) custom-call(bf16[512,288]{1,0:T(8,128)(2,1)S(1)} %get-tuple-element.834.query_ref.refs_6_, ...), custom_call_target="tpu_custom_call" | custom-call | flops 8999999488 | bytes 1 | tf_op jit(solution)/shard_map/attend/pallas_call | solution.py:217
  270.6 4.8 collective-permute-done.88.refs_3_
  277.6 5.3 collective-permute-done.89.refs_4_
  288.8 7.3 collective-permute-done.113.refs_3_
  300.7 3.0 collective-permute-done.86.refs_3_
  304.4 4.0 collective-permute-done.87.refs_4_
  316.9 5.0 feed.9
  322.1 4.1 feed_back.6
  332.3 5.0 feed.10
  339.9 4.1 feed_back.7
  348.9 5.0 feed.11
  360.9 4.1 feed_back.8
  375.2 8.0 collective-permute-done.137.refs_3_
  399.6 12.4 %wide.2 = (bf16[1152,1152]{1,0:T(8,128)(2,1)S(1)}, bf16[1152,1152]{1,0:T(8,128)(2,1)S(1)}) custom-call(s32[1]{0:T(128)} %bitcast.62.flag, bf16[512,1152]{1,0:T(8,128)(2,1)S(1)} %get-tuple-element.1011.refs_0_, bf16[512,1152]{1,0:T(8,128)(2,1)S(1)} %copy-done.281, bf16[512,1152]{1,0:T(8,128)(2,1)S(1)} %copy-done.289, ...), custom_call_target="tpu_custom_call" | custom-call | flops 8999999488 | bytes 1 | tf_op jit(solution)/shard_map/wide/pallas_call | solution.py:520
  416.2 2.6 collective-permute-done.135.refs_3_
  425.9 2.8 collective-permute-done.139.near.refs_2_
  434.0 8.7 %attend_back.6 = (bf16[512,1152]{1,0:T(8,128)(2,1)S(1)}, bf16[512,288]{1,0:T(8,128)(2,1)S(1)}, f32[512,576]{1,0:T(8,128)S(1)}, bf16[512,640]{1,0:T(8,128)(2,1)}) custom-call(bf16[128,1152]{1,0:T(8,128)(2,1)S(1)} %get-tuple-element.1034.refs_0_, bf16[128,1152]{1,0:T(8,128)(2,1)S(1)} %collective-permute-done.129.far.refs_1_, ...), custom_call_target="tpu_custom_call" | custom-call | flops 8999999488 | bytes 1 | tf_op jit(solution)/shard_map/attend_back/pallas_call | solution.py:217
  452.9 9.0 %attend_back.7 = (bf16[512,1152]{1,0:T(8,128)(2,1)S(1)}, bf16[512,288]{1,0:T(8,128)(2,1)S(1)}, f32[512,576]{1,0:T(8,128)S(1)}, bf16[512,640]{1,0:T(8,128)(2,1)S(1)}) custom-call(bf16[128,1152]{1,0:T(8,128)(2,1)S(1)} %copy-done.202, bf16[128,1152]{1,0:T(8,128)(2,1)S(1)} %copy-done.216, bf16[128,1152]{1,0:T(8,128)(2,1)S(1)} %copy-done.214, ...), custom_call_target="tpu_custom_call" | custom-call | flops 8999999488 | bytes 1 | tf_op jit(solution)/shard_map/attend_back/pallas_call | solution.py:217
  462.0 9.4 %attend_back.8 = (bf16[512,1152]{1,0:T(8,128)(2,1)S(1)}, bf16[512,288]{1,0:T(8,128)(2,1)S(1)}, f32[512,576]{1,0:T(8,128)S(1)}, bf16[512,640]{1,0:T(8,128)(2,1)S(1)}) custom-call(bf16[128,1152]{1,0:T(8,128)(2,1)S(1)} %copy-done.232, bf16[128,1152]{1,0:T(8,128)(2,1)S(1)} %copy-done.238, bf16[128,1152]{1,0:T(8,128)(2,1)S(1)} %copy-done.244, ...), custom_call_target="tpu_custom_call" | custom-call | flops 8999999488 | bytes 1 | tf_op jit(solution)/shard_map/attend_back/pallas_call | solution.py:217
  471.6 2.9 qkv_back.6
  476.7 7.2 collective-permute-done.149.first.refs_1_
  493.6 3.4 collective-permute-done.155.first.refs_1_
  509.6 7.2 narrow.2
  532.0 4.1 feed_back.9
  542.6 3.6 collective-permute-done.169.first.refs_1_
  559.1 5.2 feed_back.10
  569.1 6.0 feed_back.11
  603.4 13.7 %wide.3 = (bf16[1152,1152]{1,0:T(8,128)(2,1)S(1)}, bf16[1152,1152]{1,0:T(8,128)(2,1)}) custom-call(s32[1]{0:T(128)} %bitcast.62.flag, bf16[512,1152]{1,0:T(8,128)(2,1)S(1)} %copy-done.269, bf16[512,1152]{1,0:T(8,128)(2,1)S(1)} %copy-done.273, bf16[512,1152]{1,0:T(8,128)(2,1)S(1)} %copy-done.277, bf16[512,1152]{1,0:T(8,128)(2,1)S(1)} %copy-done.285, ...), custom_call_target="tpu_custom_call" | custom-call | flops 8999999488 | bytes 1 | tf_op jit(solution)/shard_map/wide/pallas_call | solution.py:520
  619.4 4.6 broadcast_select_fusion.11
  634.0 2.9 collective-permute-done.192.near.refs_2_
  642.3 8.6 %attend_back.9 = (bf16[512,1152]{1,0:T(8,128)(2,1)S(1)}, bf16[512,288]{1,0:T(8,128)(2,1)S(1)}, f32[512,576]{1,0:T(8,128)S(1)}, bf16[512,640]{1,0:T(8,128)(2,1)}) custom-call(bf16[128,1152]{1,0:T(8,128)(2,1)S(1)} %copy-done.196, bf16[128,1152]{1,0:T(8,128)(2,1)S(1)} %copy-done.198, bf16[128,1152]{1,0:T(8,128)(2,1)S(1)} %copy-done.200, ...), custom_call_target="tpu_custom_call" | custom-call | flops 8999999488 | bytes 1 | tf_op jit(solution)/shard_map/attend_back/pallas_call | solution.py:217
  654.7 3.9 add.422
  662.3 9.8 %attend_back.10 = (bf16[512,1152]{1,0:T(8,128)(2,1)S(1)}, bf16[512,288]{1,0:T(8,128)(2,1)S(1)}, f32[512,576]{1,0:T(8,128)S(1)}, bf16[512,640]{1,0:T(8,128)(2,1)}) custom-call(bf16[128,1152]{1,0:T(8,128)(2,1)S(1)} %copy-done.194, bf16[128,1152]{1,0:T(8,128)(2,1)S(1)} %copy-done.224, bf16[128,1152]{1,0:T(8,128)(2,1)S(1)} %copy-done.220, ...), custom_call_target="tpu_custom_call" | custom-call | flops 8999999488 | bytes 1 | tf_op jit(solution)/shard_map/attend_back/pallas_call | solution.py:217
  675.0 10.0 %attend_back.11 = (bf16[512,1152]{1,0:T(8,128)(2,1)S(1)}, bf16[512,288]{1,0:T(8,128)(2,1)S(1)}, f32[512,576]{1,0:T(8,128)S(1)}, bf16[512,640]{1,0:T(8,128)(2,1)}) custom-call(bf16[128,1152]{1,0:T(8,128)(2,1)S(1)} %copy-done.222, bf16[128,1152]{1,0:T(8,128)(2,1)S(1)} %copy-done.234, bf16[128,1152]{1,0:T(8,128)(2,1)S(1)} %copy-done.240, ...), custom_call_target="tpu_custom_call" | custom-call | flops 8999999488 | bytes 1 | tf_op jit(solution)/shard_map/attend_back/pallas_call | solution.py:217
  685.1 3.4 qkv_back.9
  693.1 6.0 collective-permute-done.202.first.refs_1_
  709.5 3.0 qkv_back.11
  717.1 7.3 narrow.3
  731.9 3.2 collective-permute-done.212.first.refs_1_
  736.6 2.7 collective-permute-start.220
  756.2 3.1 collective-permute-done.223
  765.6 16.7 %reduce-scatter.11.cloned.1.call-done = bf16[288,640]{1,0:T(8,128)(2,1)} async-done(((bf16[1152,640]{1,0:T(8,128)(2,1)}), bf16[288,640]{1,0:T(8,128)(2,1)}) %reduce-scatter.11.cloned.1.call-update) | async-done | bytes 368656 | tf_op jit(solution)/shard_map/reduce_scatter | solution.py:881
  787.9 2.7 convolution_bitcast_fusion
  (1434 shorter events, 414.4 us)
Async XLA Ops:
  7.2 546.0 %reduce-scatter.5.cloned.1.call-start = ((), (), s32[]{:S(2)}) async-start(), calls=%async_computation.4 | async-start | bytes 3317760 | tf_op jit(solution)/shard_map/reduce_scatter | solution.py:881
  14.4 16.6 %collective-permute-start.4 = (f32[24,1728]{1,0:T(8,128)}, f32[24,1728]{1,0:T(8,128)}, u32[]{:S(2)}, u32[]{:S(2)}) collective-permute-start(f32[24,1728]{1,0:T(8,128)} %fusion), channel_id=1, source_target_pairs={{0,4},{4,0},{8,12},{12,8},{1,5},{5,1},{9,13},{13,9},{2,6},{6,2},{1... | collective-permute-start | bytes 497672 | tf_op jit(solution)/shard_map/ppermute | solution.py:39
  17.7 19.1 %collective-permute-start.10 = (bf16[128,1152]{1,0:T(8,128)(2,1)S(1)}, bf16[128,1152]{1,0:T(8,128)(2,1)}, u32[]{:S(2)}, u32[]{:S(2)}) collective-permute-start(bf16[128,1152]{1,0:T(8,128)(2,1)S(1)} %get-tuple-element.694.refs_0_), channel_id=1, source_target_pairs={{0,8},{8,0},{4,12},{12,4},{1,9},{9,1},{5,13},{13,5},{2,10},{10,2},... | collective-permute-start | bytes 884744 | tf_op jit(solution)/shard_map/ppermute | solution.py:43
  43.1 71.1 %collective-permute-start.40 = (bf16[1152,1152]{1,0:T(8,128)(2,1)S(1)}, bf16[1152,1152]{1,0:T(8,128)(2,1)S(1)}, u32[]{:S(2)}, u32[]{:S(2)}) collective-permute-start(bf16[1152,1152]{1,0:T(8,128)(2,1)S(1)} %bitcast.209), channel_id=1, source_target_pairs={{0,16},{16,0},{1,17},{17,1},{2,18},{18,2},{3,19},{19,3},{4,20},{20... | collective-permute-start | bytes 7962632 | tf_op jit(solution)/shard_map/ppermute | solution.py:35
  43.1 86.1 %collective-permute-start.39 = (bf16[1152,1152]{1,0:T(8,128)(2,1)}, bf16[1152,1152]{1,0:T(8,128)(2,1)S(1)}, u32[]{:S(2)}, u32[]{:S(2)}) collective-permute-start(bf16[1152,1152]{1,0:T(8,128)(2,1)} %bitcast.210), channel_id=1, source_target_pairs={{0,16},{16,0},{1,17},{17,1},{2,18},{18,2},{3,19},{19,3},{4,20},{20... | collective-permute-start | bytes 7962632 | tf_op jit(solution)/shard_map/ppermute | solution.py:35
  71.8 23.0 %collective-permute-start.23 = (bf16[512,640]{1,0:T(8,128)(2,1)S(1)}, bf16[512,640]{1,0:T(8,128)(2,1)S(1)}, u32[]{:S(2)}, u32[]{:S(2)}) collective-permute-start(bf16[512,640]{1,0:T(8,128)(2,1)S(1)} %get-tuple-element.707.own_ref.refs_7_), channel_id=1, source_target_pairs={{0,16},{16,0},{1,17},{17,1},{2,18},{18,2},{3,19},{19,3},{4,20},{20... | collective-permute-start | bytes 1966088 | tf_op jit(solution)/shard_map/ppermute | solution.py:35
  106.7 18.0 %collective-permute-start.35 = (bf16[64,1152]{1,0:T(8,128)(2,1)S(1)}, bf16[64,1152]{1,0:T(8,128)(2,1)S(1)}, u32[]{:S(2)}, u32[]{:S(2)}) collective-permute-start(bf16[64,1152]{1,0:T(8,128)(2,1)S(1)} %get-tuple-element.717), channel_id=1, source_target_pairs={{0,4},{4,0},{8,12},{12,8},{1,5},{5,1},{9,13},{13,9},{2,6},{6,2},{1... | collective-permute-start | bytes 442376 | tf_op jit(solution)/shard_map/ppermute | solution.py:39
  188.7 16.1 %collective-permute-start.63 = (bf16[128,1152]{1,0:T(8,128)(2,1)S(1)}, bf16[128,1152]{1,0:T(8,128)(2,1)S(1)}, u32[]{:S(2)}, u32[]{:S(2)}) collective-permute-start(bf16[128,1152]{1,0:T(8,128)(2,1)S(1)} %get-tuple-element.823.refs_0_), channel_id=1, source_target_pairs={{0,8},{8,0},{4,12},{12,4},{1,9},{9,1},{5,13},{13,5},{2,10},{10,2},... | collective-permute-start | bytes 884744 | tf_op jit(solution)/shard_map/ppermute | solution.py:43
  189.8 16.3 %collective-permute-start.64 = (bf16[128,1152]{1,0:T(8,128)(2,1)S(1)}, bf16[128,1152]{1,0:T(8,128)(2,1)S(1)}, u32[]{:S(2)}, u32[]{:S(2)}) collective-permute-start(bf16[128,1152]{1,0:T(8,128)(2,1)S(1)} %get-tuple-element.823.refs_0_), channel_id=1, source_target_pairs={{0,4},{4,0},{8,12},{12,8},{1,5},{5,1},{9,13},{13,9},{2,6},{6,2},{1... | collective-permute-start | bytes 884744 | tf_op jit(solution)/shard_map/ppermute | solution.py:39
  193.2 54.3 %collective-permute-start.110 = (bf16[128,1152]{1,0:T(8,128)(2,1)S(1)}, bf16[128,1152]{1,0:T(8,128)(2,1)S(1)}, u32[]{:S(2)}, u32[]{:S(2)}) collective-permute-start(bf16[128,1152]{1,0:T(8,128)(2,1)S(1)} %upstream.3.refs_0_), channel_id=1, source_target_pairs={{0,4},{4,0},{8,12},{12,8},{1,5},{5,1},{9,13},{13,9},{2,6},{6,2},{1... | collective-permute-start | bytes 884744 | tf_op jit(solution)/shard_map/ppermute | solution.py:39
  216.8 16.8 %collective-permute-start.77 = (bf16[512,640]{1,0:T(8,128)(2,1)S(1)}, bf16[512,640]{1,0:T(8,128)(2,1)S(1)}, u32[]{:S(2)}, u32[]{:S(2)}) collective-permute-start(bf16[512,640]{1,0:T(8,128)(2,1)S(1)} %get-tuple-element.843.own_ref.refs_7_), channel_id=1, source_target_pairs={{0,16},{16,0},{1,17},{17,1},{2,18},{18,2},{3,19},{19,3},{4,20},{20... | collective-permute-start | bytes 1966088 | tf_op jit(solution)/shard_map/ppermute | solution.py:35
  222.3 24.5 %collective-permute-start.76 = (bf16[512,640]{1,0:T(8,128)(2,1)S(1)}, bf16[512,640]{1,0:T(8,128)(2,1)S(1)}, u32[]{:S(2)}, u32[]{:S(2)}) collective-permute-start(bf16[512,640]{1,0:T(8,128)(2,1)S(1)} %get-tuple-element.842.own_ref.refs_7_), channel_id=1, source_target_pairs={{0,16},{16,0},{1,17},{17,1},{2,18},{18,2},{3,19},{19,3},{4,20},{20... | collective-permute-start | bytes 1966088 | tf_op jit(solution)/shard_map/ppermute | solution.py:35
  245.3 18.8 %collective-permute-start.111 = (bf16[128,1152]{1,0:T(8,128)(2,1)S(1)}, bf16[128,1152]{1,0:T(8,128)(2,1)S(1)}, u32[]{:S(2)}, u32[]{:S(2)}) collective-permute-start(bf16[128,1152]{1,0:T(8,128)(2,1)S(1)} %upstream.3.refs_0_), channel_id=1, source_target_pairs={{0,8},{8,0},{4,12},{12,4},{1,9},{9,1},{5,13},{13,5},{2,10},{10,2},... | collective-permute-start | bytes 884744 | tf_op jit(solution)/shard_map/ppermute | solution.py:43
  246.9 18.7 %collective-permute-start.115 = (bf16[128,1152]{1,0:T(8,128)(2,1)S(1)}, bf16[128,1152]{1,0:T(8,128)(2,1)S(1)}, u32[]{:S(2)}, u32[]{:S(2)}) collective-permute-start(bf16[128,1152]{1,0:T(8,128)(2,1)S(1)} %upstream.4.refs_0_), channel_id=1, source_target_pairs={{0,8},{8,0},{4,12},{12,4},{1,9},{9,1},{5,13},{13,5},{2,10},{10,2},... | collective-permute-start | bytes 884744 | tf_op jit(solution)/shard_map/ppermute | solution.py:43
  247.6 19.2 %collective-permute-start.116 = (bf16[128,1152]{1,0:T(8,128)(2,1)S(1)}, bf16[128,1152]{1,0:T(8,128)(2,1)S(1)}, u32[]{:S(2)}, u32[]{:S(2)}) collective-permute-start(bf16[128,1152]{1,0:T(8,128)(2,1)S(1)} %upstream.4.refs_0_), channel_id=1, source_target_pairs={{0,4},{4,0},{8,12},{12,8},{1,5},{5,1},{9,13},{13,9},{2,6},{6,2},{1... | collective-permute-start | bytes 884744 | tf_op jit(solution)/shard_map/ppermute | solution.py:39
  253.3 16.6 %collective-permute-start.75 = (bf16[64,1152]{1,0:T(8,128)(2,1)S(1)}, bf16[64,1152]{1,0:T(8,128)(2,1)S(1)}, u32[]{:S(2)}, u32[]{:S(2)}) collective-permute-start(bf16[64,1152]{1,0:T(8,128)(2,1)S(1)} %get-tuple-element.841), channel_id=1, source_target_pairs={{0,4},{4,0},{8,12},{12,8},{1,5},{5,1},{9,13},{13,9},{2,6},{6,2},{1... | collective-permute-start | bytes 442376 | tf_op jit(solution)/shard_map/ppermute | solution.py:39
  264.1 22.8 %collective-permute-start.121 = (bf16[128,1152]{1,0:T(8,128)(2,1)S(1)}, bf16[128,1152]{1,0:T(8,128)(2,1)S(1)}, u32[]{:S(2)}, u32[]{:S(2)}) collective-permute-start(bf16[128,1152]{1,0:T(8,128)(2,1)S(1)} %upstream.5.refs_0_), channel_id=1, source_target_pairs={{0,8},{8,0},{4,12},{12,4},{1,9},{9,1},{5,13},{13,5},{2,10},{10,2},... | collective-permute-start | bytes 884744 | tf_op jit(solution)/shard_map/ppermute | solution.py:43
  265.6 18.3 %collective-permute-start.84 = (bf16[128,1152]{1,0:T(8,128)(2,1)S(1)}, bf16[128,1152]{1,0:T(8,128)(2,1)S(1)}, u32[]{:S(2)}, u32[]{:S(2)}) collective-permute-start(bf16[128,1152]{1,0:T(8,128)(2,1)S(1)} %get-tuple-element.863), channel_id=1, source_target_pairs={{0,4},{4,0},{8,12},{12,8},{1,5},{5,1},{9,13},{13,9},{2,6},{6,2},{1... | collective-permute-start | bytes 884744 | tf_op jit(solution)/shard_map/ppermute | solution.py:39
  266.8 18.3 %collective-permute-start.85 = (bf16[128,1152]{1,0:T(8,128)(2,1)S(1)}, bf16[128,1152]{1,0:T(8,128)(2,1)S(1)}, u32[]{:S(2)}, u32[]{:S(2)}) collective-permute-start(bf16[128,1152]{1,0:T(8,128)(2,1)S(1)} %get-tuple-element.864), channel_id=1, source_target_pairs={{0,8},{8,0},{4,12},{12,4},{1,9},{9,1},{5,13},{13,5},{2,10},{10,2},... | collective-permute-start | bytes 884744 | tf_op jit(solution)/shard_map/ppermute | solution.py:43
  287.8 23.2 %collective-permute-start.90 = (bf16[128,1152]{1,0:T(8,128)(2,1)S(1)}, bf16[128,1152]{1,0:T(8,128)(2,1)S(1)}, u32[]{:S(2)}, u32[]{:S(2)}) collective-permute-start(bf16[128,1152]{1,0:T(8,128)(2,1)S(1)} %get-tuple-element.897.refs_0_), channel_id=1, source_target_pairs={{0,8},{8,0},{4,12},{12,4},{1,9},{9,1},{5,13},{13,5},{2,10},{10,2},... | collective-permute-start | bytes 884744 | tf_op jit(solution)/shard_map/ppermute | solution.py:43
  299.1 22.8 %collective-permute-start.125 = (bf16[64,1152]{1,0:T(8,128)(2,1)S(1)}, bf16[64,1152]{1,0:T(8,128)(2,1)S(1)}, u32[]{:S(2)}, u32[]{:S(2)}) collective-permute-start(bf16[64,1152]{1,0:T(8,128)(2,1)S(1)} %get-tuple-element.944), channel_id=1, source_target_pairs={{0,4},{4,0},{8,12},{12,8},{1,5},{5,1},{9,13},{13,9},{2,6},{6,2},{1... | collective-permute-start | bytes 442376 | tf_op jit(solution)/shard_map/ppermute | solution.py:39
  326.2 21.8 %collective-permute-start.117 = (bf16[128,1152]{1,0:T(8,128)(2,1)S(1)}, bf16[128,1152]{1,0:T(8,128)(2,1)S(1)}, u32[]{:S(2)}, u32[]{:S(2)}) collective-permute-start(bf16[128,1152]{1,0:T(8,128)(2,1)S(1)} %get-tuple-element.953), channel_id=1, source_target_pairs={{0,4},{4,0},{8,12},{12,8},{1,5},{5,1},{9,13},{13,9},{2,6},{6,2},{1... | collective-permute-start | bytes 884744 | tf_op jit(solution)/shard_map/ppermute | solution.py:39
  326.9 21.4 %collective-permute-start.118 = (bf16[128,1152]{1,0:T(8,128)(2,1)S(1)}, bf16[128,1152]{1,0:T(8,128)(2,1)S(1)}, u32[]{:S(2)}, u32[]{:S(2)}) collective-permute-start(bf16[128,1152]{1,0:T(8,128)(2,1)S(1)} %get-tuple-element.954), channel_id=1, source_target_pairs={{0,8},{8,0},{4,12},{12,4},{1,9},{9,1},{5,13},{13,5},{2,10},{10,2},... | collective-permute-start | bytes 884744 | tf_op jit(solution)/shard_map/ppermute | solution.py:43
  348.0 17.0 %collective-permute-start.128 = (bf16[128,1152]{1,0:T(8,128)(2,1)S(1)}, bf16[128,1152]{1,0:T(8,128)(2,1)S(1)}, u32[]{:S(2)}, u32[]{:S(2)}) collective-permute-start(bf16[128,1152]{1,0:T(8,128)(2,1)S(1)} %get-tuple-element.977), channel_id=1, source_target_pairs={{0,4},{4,0},{8,12},{12,8},{1,5},{5,1},{9,13},{13,9},{2,6},{6,2},{1... | collective-permute-start | bytes 884744 | tf_op jit(solution)/shard_map/ppermute | solution.py:39
  356.0 16.1 %collective-permute-start.102 = (bf16[128,1152]{1,0:T(8,128)(2,1)S(1)}, bf16[128,1152]{1,0:T(8,128)(2,1)S(1)}, u32[]{:S(2)}, u32[]{:S(2)}) collective-permute-start(bf16[128,1152]{1,0:T(8,128)(2,1)S(1)} %get-tuple-element.910), channel_id=1, source_target_pairs={{0,8},{8,0},{4,12},{12,4},{1,9},{9,1},{5,13},{13,5},{2,10},{10,2},... | collective-permute-start | bytes 884744 | tf_op jit(solution)/shard_map/ppermute | solution.py:43
  366.1 23.7 %collective-permute-start.133 = (bf16[128,1152]{1,0:T(8,128)(2,1)S(1)}, bf16[128,1152]{1,0:T(8,128)(2,1)S(1)}, u32[]{:S(2)}, u32[]{:S(2)}) collective-permute-start(bf16[128,1152]{1,0:T(8,128)(2,1)S(1)} %get-tuple-element.991), channel_id=1, source_target_pairs={{0,4},{4,0},{8,12},{12,8},{1,5},{5,1},{9,13},{13,9},{2,6},{6,2},{1... | collective-permute-start | bytes 884744 | tf_op jit(solution)/shard_map/ppermute | solution.py:39
  368.1 23.2 %collective-permute-start.134 = (bf16[128,1152]{1,0:T(8,128)(2,1)S(1)}, bf16[128,1152]{1,0:T(8,128)(2,1)S(1)}, u32[]{:S(2)}, u32[]{:S(2)}) collective-permute-start(bf16[128,1152]{1,0:T(8,128)(2,1)S(1)} %get-tuple-element.992), channel_id=1, source_target_pairs={{0,8},{8,0},{4,12},{12,4},{1,9},{9,1},{5,13},{13,5},{2,10},{10,2},... | collective-permute-start | bytes 884744 | tf_op jit(solution)/shard_map/ppermute | solution.py:43
  370.6 21.2 %collective-permute-start.106 = (bf16[128,1152]{1,0:T(8,128)(2,1)S(1)}, bf16[128,1152]{1,0:T(8,128)(2,1)S(1)}, u32[]{:S(2)}, u32[]{:S(2)}) collective-permute-start(bf16[128,1152]{1,0:T(8,128)(2,1)S(1)} %get-tuple-element.923), channel_id=1, source_target_pairs={{0,4},{4,0},{8,12},{12,8},{1,5},{5,1},{9,13},{13,9},{2,6},{6,2},{1... | collective-permute-start | bytes 884744 | tf_op jit(solution)/shard_map/ppermute | solution.py:39
  373.6 18.8 %collective-permute-start.107 = (bf16[128,1152]{1,0:T(8,128)(2,1)S(1)}, bf16[128,1152]{1,0:T(8,128)(2,1)S(1)}, u32[]{:S(2)}, u32[]{:S(2)}) collective-permute-start(bf16[128,1152]{1,0:T(8,128)(2,1)S(1)} %get-tuple-element.924), channel_id=1, source_target_pairs={{0,8},{8,0},{4,12},{12,4},{1,9},{9,1},{5,13},{13,5},{2,10},{10,2},... | collective-permute-start | bytes 884744 | tf_op jit(solution)/shard_map/ppermute | solution.py:43
  412.0 34.1 %collective-permute-start.148 = (bf16[1152,1152]{1,0:T(8,128)(2,1)S(1)}, bf16[1152,1152]{1,0:T(8,128)(2,1)S(1)}, u32[]{:S(2)}, u32[]{:S(2)}) collective-permute-start(bf16[1152,1152]{1,0:T(8,128)(2,1)S(1)} %get-tuple-element.1045), channel_id=1, source_target_pairs={{0,16},{16,0},{1,17},{17,1},{2,18},{18,2},{3,19},{19,3},{4,20},{20... | collective-permute-start | bytes 7962632 | tf_op jit(solution)/shard_map/ppermute | solution.py:35
  431.9 17.0 %collective-permute-start.146 = (bf16[64,1152]{1,0:T(8,128)(2,1)}, bf16[64,1152]{1,0:T(8,128)(2,1)S(1)}, u32[]{:S(2)}, u32[]{:S(2)}) collective-permute-start(bf16[64,1152]{1,0:T(8,128)(2,1)} %get-tuple-element.1032), channel_id=1, source_target_pairs={{0,4},{4,0},{8,12},{12,8},{1,5},{5,1},{9,13},{13,9},{2,6},{6,2},{1... | collective-permute-start | bytes 442376 | tf_op jit(solution)/shard_map/ppermute | solution.py:39
  442.7 28.8 %collective-permute-start.141 = (bf16[512,640]{1,0:T(8,128)(2,1)}, bf16[512,640]{1,0:T(8,128)(2,1)}, u32[]{:S(2)}, u32[]{:S(2)}) collective-permute-start(bf16[512,640]{1,0:T(8,128)(2,1)} %get-tuple-element.1042), channel_id=1, source_target_pairs={{0,16},{16,0},{1,17},{17,1},{2,18},{18,2},{3,19},{19,3},{4,20},{20... | collective-permute-start | bytes 1966088 | tf_op jit(solution)/shard_map/ppermute | solution.py:35
  444.5 17.4 %collective-permute-start.144 = (bf16[64,1152]{1,0:T(8,128)(2,1)}, bf16[64,1152]{1,0:T(8,128)(2,1)}, u32[]{:S(2)}, u32[]{:S(2)}) collective-permute-start(bf16[64,1152]{1,0:T(8,128)(2,1)} %get-tuple-element.1043), channel_id=1, source_target_pairs={{0,8},{8,0},{4,12},{12,4},{1,9},{9,1},{5,13},{13,5},{2,10},{10,2},... | collective-permute-start | bytes 442376 | tf_op jit(solution)/shard_map/ppermute | solution.py:43
  448.6 254.6 %reduce-scatter.7.cloned.1.call-start = ((), (), s32[]{:S(2)}) async-start(), calls=%async_computation.5 | async-start | bytes 1843200 | tf_op jit(solution)/shard_map/reduce_scatter | solution.py:881
  485.3 16.1 %collective-permute-start.151 = (bf16[64,1152]{1,0:T(8,128)(2,1)S(1)}, bf16[64,1152]{1,0:T(8,128)(2,1)S(1)}, u32[]{:S(2)}, u32[]{:S(2)}) collective-permute-start(bf16[64,1152]{1,0:T(8,128)(2,1)S(1)} %get-tuple-element.1067), channel_id=1, source_target_pairs={{0,8},{8,0},{4,12},{12,4},{1,9},{9,1},{5,13},{13,5},{2,10},{10,2},... | collective-permute-start | bytes 442376 | tf_op jit(solution)/shard_map/ppermute | solution.py:43
  485.8 16.0 %collective-permute-start.152 = (bf16[64,1152]{1,0:T(8,128)(2,1)S(1)}, bf16[64,1152]{1,0:T(8,128)(2,1)S(1)}, u32[]{:S(2)}, u32[]{:S(2)}) collective-permute-start(bf16[64,1152]{1,0:T(8,128)(2,1)S(1)} %get-tuple-element.1068), channel_id=1, source_target_pairs={{0,4},{4,0},{8,12},{12,8},{1,5},{5,1},{9,13},{13,9},{2,6},{6,2},{1... | collective-permute-start | bytes 442376 | tf_op jit(solution)/shard_map/ppermute | solution.py:39
  499.8 17.1 %collective-permute-start.165 = (bf16[64,1152]{1,0:T(8,128)(2,1)S(1)}, bf16[64,1152]{1,0:T(8,128)(2,1)S(1)}, u32[]{:S(2)}, u32[]{:S(2)}) collective-permute-start(bf16[64,1152]{1,0:T(8,128)(2,1)S(1)} %get-tuple-element.1081), channel_id=1, source_target_pairs={{0,4},{4,0},{8,12},{12,8},{1,5},{5,1},{9,13},{13,9},{2,6},{6,2},{1... | collective-permute-start | bytes 442376 | tf_op jit(solution)/shard_map/ppermute | solution.py:39
  501.4 15.9 %collective-permute-start.166 = (bf16[64,1152]{1,0:T(8,128)(2,1)S(1)}, bf16[64,1152]{1,0:T(8,128)(2,1)S(1)}, u32[]{:S(2)}, u32[]{:S(2)}) collective-permute-start(bf16[64,1152]{1,0:T(8,128)(2,1)S(1)} %get-tuple-element.1082), channel_id=1, source_target_pairs={{0,8},{8,0},{4,12},{12,4},{1,9},{9,1},{5,13},{13,5},{2,10},{10,2},... | collective-permute-start | bytes 442376 | tf_op jit(solution)/shard_map/ppermute | solution.py:43
  502.7 17.9 %collective-permute-start.157 = (bf16[128,1152]{1,0:T(8,128)(2,1)S(1)}, bf16[128,1152]{1,0:T(8,128)(2,1)S(1)}, u32[]{:S(2)}, u32[]{:S(2)}) collective-permute-start(bf16[128,1152]{1,0:T(8,128)(2,1)S(1)} %get-tuple-element.1136.refs_0_), channel_id=1, source_target_pairs={{0,8},{8,0},{4,12},{12,4},{1,9},{9,1},{5,13},{13,5},{2,10},{10,2},... | collective-permute-start | bytes 884744 | tf_op jit(solution)/shard_map/ppermute | solution.py:43
  521.2 28.4 %collective-permute-start.179 = (bf16[1152,640]{1,0:T(8,128)(2,1)S(1)}, bf16[1152,640]{1,0:T(8,128)(2,1)S(1)}, u32[]{:S(2)}, u32[]{:S(2)}) collective-permute-start(bf16[1152,640]{1,0:T(8,128)(2,1)S(1)} %get-tuple-element.1151), channel_id=1, source_target_pairs={{0,16},{16,0},{1,17},{17,1},{2,18},{18,2},{3,19},{19,3},{4,20},{20... | collective-permute-start | bytes 4423688 | tf_op jit(solution)/shard_map/ppermute | solution.py:35
  546.2 20.9 %collective-permute-start.175 = (bf16[64,1152]{1,0:T(8,128)(2,1)}, bf16[64,1152]{1,0:T(8,128)(2,1)}, u32[]{:S(2)}, u32[]{:S(2)}) collective-permute-start(bf16[64,1152]{1,0:T(8,128)(2,1)} %get-tuple-element.1149), channel_id=1, source_target_pairs={{0,8},{8,0},{4,12},{12,4},{1,9},{9,1},{5,13},{13,5},{2,10},{10,2},... | collective-permute-start | bytes 442376 | tf_op jit(solution)/shard_map/ppermute | solution.py:43
  546.2 22.9 %collective-permute-start.176 = (bf16[64,1152]{1,0:T(8,128)(2,1)}, bf16[64,1152]{1,0:T(8,128)(2,1)}, u32[]{:S(2)}, u32[]{:S(2)}) collective-permute-start(bf16[64,1152]{1,0:T(8,128)(2,1)} %get-tuple-element.1150), channel_id=1, source_target_pairs={{0,4},{4,0},{8,12},{12,8},{1,5},{5,1},{9,13},{13,9},{2,6},{6,2},{1... | collective-permute-start | bytes 442376 | tf_op jit(solution)/shard_map/ppermute | solution.py:39
  549.6 30.4 %collective-permute-start.171 = (bf16[64,1152]{1,0:T(8,128)(2,1)}, bf16[64,1152]{1,0:T(8,128)(2,1)S(1)}, u32[]{:S(2)}, u32[]{:S(2)}) collective-permute-start(bf16[64,1152]{1,0:T(8,128)(2,1)} %get-tuple-element.1146), channel_id=1, source_target_pairs={{0,8},{8,0},{4,12},{12,4},{1,9},{9,1},{5,13},{13,5},{2,10},{10,2},... | collective-permute-start | bytes 442376 | tf_op jit(solution)/shard_map/ppermute | solution.py:43
  551.2 31.5 %collective-permute-start.172 = (bf16[64,1152]{1,0:T(8,128)(2,1)}, bf16[64,1152]{1,0:T(8,128)(2,1)}, u32[]{:S(2)}, u32[]{:S(2)}) collective-permute-start(bf16[64,1152]{1,0:T(8,128)(2,1)} %copy-done.257), channel_id=1, source_target_pairs={{0,4},{4,0},{8,12},{12,8},{1,5},{5,1},{9,13},{13,9},{2,6},{6,2},{1... | collective-permute-start | bytes 442376 | tf_op jit(solution)/shard_map/ppermute | solution.py:39
  589.2 174.8 %reduce-scatter.9.cloned.1.call-start = ((), (), s32[]{:S(2)}) async-start(), calls=%async_computation.6 | async-start | bytes 3317760 | tf_op jit(solution)/shard_map/reduce_scatter | solution.py:881
  589.3 28.7 %collective-permute-start.218 = (f32[2,3,128]{2,1,0:T(4,128)}, f32[2,3,128]{2,1,0:T(4,128)}, u32[]{:S(2)}, u32[]{:S(2)}) collective-permute-start(f32[2,3,128]{2,1,0:T(4,128)} %fusion.35), channel_id=1, source_target_pairs={{0,16},{16,0},{1,17},{17,1},{2,18},{18,2},{3,19},{19,3},{4,20},{20... | collective-permute-start | bytes 9224 | tf_op jit(solution)/shard_map/ppermute | solution.py:35
  591.3 28.1 %collective-permute-start.112 = (f32[3,128,1152]{2,1,0:T(8,128)}, f32[3,128,1152]{2,1,0:T(8,128)}, u32[]{:S(2)}, u32[]{:S(2)}) collective-permute-start(f32[3,128,1152]{2,1,0:T(8,128)} %fusion.2), channel_id=1, source_target_pairs={{0,16},{16,0},{1,17},{17,1},{2,18},{18,2},{3,19},{19,3},{4,20},{20... | collective-permute-start | bytes 5308424 | tf_op jit(solution)/shard_map/ppermute | solution.py:35
  617.0 37.2 %collective-permute-start.201 = (bf16[1152,1152]{1,0:T(8,128)(2,1)}, bf16[1152,1152]{1,0:T(8,128)(2,1)}, u32[]{:S(2)}, u32[]{:S(2)}) collective-permute-start(bf16[1152,1152]{1,0:T(8,128)(2,1)} %get-tuple-element.1239), channel_id=1, source_target_pairs={{0,16},{16,0},{1,17},{17,1},{2,18},{18,2},{3,19},{19,3},{4,20},{20... | collective-permute-start | bytes 7962632 | tf_op jit(solution)/shard_map/ppermute | solution.py:35
  640.1 18.8 %collective-permute-start.199 = (bf16[64,1152]{1,0:T(8,128)(2,1)}, bf16[64,1152]{1,0:T(8,128)(2,1)}, u32[]{:S(2)}, u32[]{:S(2)}) collective-permute-start(bf16[64,1152]{1,0:T(8,128)(2,1)} %get-tuple-element.1226), channel_id=1, source_target_pairs={{0,4},{4,0},{8,12},{12,8},{1,5},{5,1},{9,13},{13,9},{2,6},{6,2},{1... | collective-permute-start | bytes 442376 | tf_op jit(solution)/shard_map/ppermute | solution.py:39
  641.6 17.3 %collective-permute-start.200 = (bf16[64,1152]{1,0:T(8,128)(2,1)}, bf16[64,1152]{1,0:T(8,128)(2,1)}, u32[]{:S(2)}, u32[]{:S(2)}) collective-permute-start(bf16[64,1152]{1,0:T(8,128)(2,1)} %get-tuple-element.1227), channel_id=1, source_target_pairs={{0,8},{8,0},{4,12},{12,4},{1,9},{9,1},{5,13},{13,5},{2,10},{10,2},... | collective-permute-start | bytes 442376 | tf_op jit(solution)/shard_map/ppermute | solution.py:43
  651.0 34.0 %collective-permute-start.194 = (bf16[512,640]{1,0:T(8,128)(2,1)}, bf16[512,640]{1,0:T(8,128)(2,1)}, u32[]{:S(2)}, u32[]{:S(2)}) collective-permute-start(bf16[512,640]{1,0:T(8,128)(2,1)} %get-tuple-element.1236), channel_id=1, source_target_pairs={{0,16},{16,0},{1,17},{17,1},{2,18},{18,2},{3,19},{19,3},{4,20},{20... | collective-permute-start | bytes 1966088 | tf_op jit(solution)/shard_map/ppermute | solution.py:35
  652.8 22.1 %collective-permute-start.197 = (bf16[64,1152]{1,0:T(8,128)(2,1)}, bf16[64,1152]{1,0:T(8,128)(2,1)}, u32[]{:S(2)}, u32[]{:S(2)}) collective-permute-start(bf16[64,1152]{1,0:T(8,128)(2,1)} %get-tuple-element.1237), channel_id=1, source_target_pairs={{0,8},{8,0},{4,12},{12,4},{1,9},{9,1},{5,13},{13,5},{2,10},{10,2},... | collective-permute-start | bytes 442376 | tf_op jit(solution)/shard_map/ppermute | solution.py:43
  654.2 20.6 %collective-permute-start.198 = (bf16[64,1152]{1,0:T(8,128)(2,1)}, bf16[64,1152]{1,0:T(8,128)(2,1)}, u32[]{:S(2)}, u32[]{:S(2)}) collective-permute-start(bf16[64,1152]{1,0:T(8,128)(2,1)} %get-tuple-element.1238), channel_id=1, source_target_pairs={{0,4},{4,0},{8,12},{12,8},{1,5},{5,1},{9,13},{13,9},{2,6},{6,2},{1... | collective-permute-start | bytes 442376 | tf_op jit(solution)/shard_map/ppermute | solution.py:39
  658.7 123.6 %reduce-scatter.11.cloned.1.call-start = ((), (), s32[]{:S(2)}) async-start(), calls=%async_computation.7 | async-start | bytes 1843200 | tf_op jit(solution)/shard_map/reduce_scatter | solution.py:881
  684.9 18.3 %collective-permute-start.206 = (bf16[512,640]{1,0:T(8,128)(2,1)}, bf16[512,640]{1,0:T(8,128)(2,1)S(1)}, u32[]{:S(2)}, u32[]{:S(2)}) collective-permute-start(bf16[512,640]{1,0:T(8,128)(2,1)} %get-tuple-element.1271), channel_id=1, source_target_pairs={{0,16},{16,0},{1,17},{17,1},{2,18},{18,2},{3,19},{19,3},{4,20},{20... | collective-permute-start | bytes 1966088 | tf_op jit(solution)/shard_map/ppermute | solution.py:35
  693.1 16.3 %collective-permute-start.207 = (bf16[512,640]{1,0:T(8,128)(2,1)}, bf16[512,640]{1,0:T(8,128)(2,1)}, u32[]{:S(2)}, u32[]{:S(2)}) collective-permute-start(bf16[512,640]{1,0:T(8,128)(2,1)} %get-tuple-element.1275), channel_id=1, source_target_pairs={{0,16},{16,0},{1,17},{17,1},{2,18},{18,2},{3,19},{19,3},{4,20},{20... | collective-permute-start | bytes 1966088 | tf_op jit(solution)/shard_map/ppermute | solution.py:35
  701.1 26.2 %collective-permute-start.204 = (bf16[64,1152]{1,0:T(8,128)(2,1)}, bf16[64,1152]{1,0:T(8,128)(2,1)}, u32[]{:S(2)}, u32[]{:S(2)}) collective-permute-start(bf16[64,1152]{1,0:T(8,128)(2,1)} %get-tuple-element.1261), channel_id=1, source_target_pairs={{0,8},{8,0},{4,12},{12,4},{1,9},{9,1},{5,13},{13,5},{2,10},{10,2},... | collective-permute-start | bytes 442376 | tf_op jit(solution)/shard_map/ppermute | solution.py:43
  701.7 27.0 %collective-permute-start.205 = (bf16[64,1152]{1,0:T(8,128)(2,1)}, bf16[64,1152]{1,0:T(8,128)(2,1)}, u32[]{:S(2)}, u32[]{:S(2)}) collective-permute-start(bf16[64,1152]{1,0:T(8,128)(2,1)} %get-tuple-element.1262), channel_id=1, source_target_pairs={{0,4},{4,0},{8,12},{12,8},{1,5},{5,1},{9,13},{13,9},{2,6},{6,2},{1... | collective-permute-start | bytes 442376 | tf_op jit(solution)/shard_map/ppermute | solution.py:39
  724.4 19.2 %collective-permute-start.216 = (bf16[1152,640]{1,0:T(8,128)(2,1)S(1)}, bf16[1152,640]{1,0:T(8,128)(2,1)S(1)}, u32[]{:S(2)}, u32[]{:S(2)}) collective-permute-start(bf16[1152,640]{1,0:T(8,128)(2,1)S(1)} %get-tuple-element.1317), channel_id=1, source_target_pairs={{0,16},{16,0},{1,17},{17,1},{2,18},{18,2},{3,19},{19,3},{4,20},{20... | collective-permute-start | bytes 4423688 | tf_op jit(solution)/shard_map/ppermute | solution.py:35
  735.1 47.3 %collective-permute-start.219 = (bf16[24,1152]{1,0:T(8,128)(2,1)}, bf16[24,1152]{1,0:T(8,128)(2,1)}, u32[]{:S(2)}, u32[]{:S(2)}) collective-permute-start(bf16[24,1152]{1,0:T(8,128)(2,1)} %get-tuple-element.1438), channel_id=1, source_target_pairs={{0,1},{1,2},{2,3},{3,0},{4,5},{5,6},{6,7},{7,4},{8,9},{9,10},{10,1... | collective-permute-start | bytes 165896 | tf_op jit(solution)/shard_map/ppermute | solution.py:190
  736.6 47.0 %collective-permute-start.220 = (bf16[24,1152]{1,0:T(8,128)(2,1)}, bf16[24,1152]{1,0:T(8,128)(2,1)}, u32[]{:S(2)}, u32[]{:S(2)}) collective-permute-start(bf16[24,1152]{1,0:T(8,128)(2,1)} %get-tuple-element.1438), channel_id=1, source_target_pairs={{0,2},{1,3},{2,0},{3,1},{4,6},{5,7},{6,4},{7,5},{8,10},{9,11},{10,... | collective-permute-start | bytes 165896 | tf_op jit(solution)/shard_map/ppermute | solution.py:190
  743.7 41.4 %collective-permute-start.221 = (bf16[24,1152]{1,0:T(8,128)(2,1)}, bf16[24,1152]{1,0:T(8,128)(2,1)}, u32[]{:S(2)}, u32[]{:S(2)}) collective-permute-start(bf16[24,1152]{1,0:T(8,128)(2,1)} %get-tuple-element.1438), channel_id=1, source_target_pairs={{0,3},{1,0},{2,1},{3,2},{4,7},{5,4},{6,5},{7,6},{8,11},{9,8},{10,9... | collective-permute-start | bytes 165896 | tf_op jit(solution)/shard_map/ppermute | solution.py:190
  764.0 22.2 %collective-permute-start.225 = (bf16[24,1728]{1,0:T(8,128)(2,1)S(1)}, bf16[24,1728]{1,0:T(8,128)(2,1)S(1)}, u32[]{:S(2)}, u32[]{:S(2)}) collective-permute-start(bf16[24,1728]{1,0:T(8,128)(2,1)S(1)} %fusion.24), channel_id=1, source_target_pairs={{0,1},{1,2},{2,3},{3,0},{4,5},{5,6},{6,7},{7,4},{8,9},{9,10},{10,1... | collective-permute-start | bytes 248840 | tf_op jit(solution)/shard_map/ppermute | solution.py:190
  764.7 21.5 %collective-permute-start.226 = (bf16[24,1728]{1,0:T(8,128)(2,1)S(1)}, bf16[24,1728]{1,0:T(8,128)(2,1)S(1)}, u32[]{:S(2)}, u32[]{:S(2)}) collective-permute-start(bf16[24,1728]{1,0:T(8,128)(2,1)S(1)} %fusion.24), channel_id=1, source_target_pairs={{0,2},{1,3},{2,0},{3,1},{4,6},{5,7},{6,4},{7,5},{8,10},{9,11},{10,... | collective-permute-start | bytes 248840 | tf_op jit(solution)/shard_map/ppermute | solution.py:190
  (579 other events, 7767.4 us)
Sparse Core Ops, SparseCore 0:
  448.7 53.0 reduce-scatter.4
  589.3 34.0 reduce-scatter.6
  658.8 53.1 reduce-scatter.8
  746.8 35.4 reduce-scatter.10
